TPU v7x, 32 devices: a whole 2x2x4 slice. The times are simulated.
32 devices in a mesh: grp: 2 (over x), row: 16 (over z, y, core).
Axes of the slice: x: 2, y: 2, z: 4, core: 2. Of those that a mesh axis runs over, the one named last changes fastest.
Arguments:
- features: bfloat16 [16384, 128], P(('grp', 'row')), parts along dimension 0, may hold values from -6 to 6
- patterns: int32 [4096, 128, 128], P(('grp', 'row')), parts along dimension 0, may hold values 0 or 1
- tile_dest: int32 [4096, 1], P(('grp', 'row')), parts along dimension 0, may hold values from 0 to 15; in each aligned block of 128 rows (0 to 127, 128 to 255, ...) at most 9 rows name the same one
- tile_src_block: int32 [4096], P(('grp', 'row')), parts along dimension 0, may hold values from 0 to 3
- tile_dst_block: int32 [4096], P(('grp', 'row')), parts along dimension 0, may hold values from 0 to 3
- in_degree: int32 [16384], P(('grp', 'row')), parts along dimension 0, may hold values from 32 to 96
- w_self: bfloat16 [128, 256], replicated, may hold values from -0.5 to 0.5
- w_neigh: bfloat16 [128, 256], replicated, may hold values from -0.5 to 0.5
- bias: float32 [256], replicated, may hold values from -3 to 3
- cotangent: bfloat16 [16384, 256], P(('grp', 'row')), parts along dimension 0, may hold values from -6 to 6
Outputs:
- output: bfloat16 [16384, 256], P(('grp', 'row')), parts along dimension 0
- grad_feat: bfloat16 [16384, 128], P(('grp', 'row')), parts along dimension 0
- grad_self: float32 [256, 256], P('grp'), parts along dimension 0
- grad_neigh: float32 [256, 256], P('grp'), parts along dimension 0
- grad_bias: float32 [512], P('grp'), parts along dimension 0
There are 2 independent parts, one for each index of `grp`. A program takes and returns all parts, laid end to end along the dimension named above; an argument that names none is the same for every part. Nothing has to cross between parts.
Inputs may be any that keep to these rules, and one draw needn't show every extreme that they name: `tile_dest`: among the 128 tiles of one device at most 9 have their destination on any one device, and in some devices exactly 9 share one destination device.
All inputs are finite; a program needn't handle non-finite values. No bound on the sum of `patterns` on one device may be relied on, other than what follows from the above.
Results may differ from a plain program's by a relative error of at most 0.0055.
The roundings to bfloat16 on the way count: a program that leaves them out, or rounds other values in their place, can miss the bound.
Values may be sent and summed in bfloat16 or wider, within the bound.
No kernel may reach another device: no remote copies, remote signals or barrier semaphores. Data moves between devices by JAX's collectives and lax.ppermute only.
A program may use at most 128 MiB of HBM per device.

v0:
```python
import math

import jax
import jax.numpy as jnp
from jax import lax
from jax.sharding import PartitionSpec as P


def on_device(
    features,
    patterns,
    tile_dest,
    tile_src_block,
    tile_dst_block,
    in_degree,
    w_self,
    w_neigh,
    bias,
    cotangent,
):
    devices = lax.axis_size("row")
    tile_count, tile_rows, _ = patterns.shape
    feat_width = features.shape[1]
    nblocks = features.shape[0] // tile_rows
    capacity = max(2, tile_count // devices + 1)
    slots_all = devices * capacity
    pattern = patterns.astype(jnp.bfloat16)
    blocks = features.reshape(nblocks, tile_rows, feat_width)
    source = jnp.take(blocks, tile_src_block, axis=0)
    partial_value = jnp.einsum(
        "tsd,tsf->tdf", pattern, source, preferred_element_type=jnp.float32
    ).astype(jnp.bfloat16)
    target = tile_dest[:, 0]
    onehot = (target[:, None] == jnp.arange(devices, dtype=jnp.int32)[None, :]).astype(jnp.int32)
    before = jnp.cumsum(onehot, axis=0) - onehot
    slot_rank = jnp.sum(before * onehot, axis=1)
    slot_index = target * capacity + slot_rank
    outgoing = (
        jnp.zeros((slots_all, tile_rows, feat_width), jnp.bfloat16)
        .at[slot_index]
        .set(partial_value)
    )
    outgoing = outgoing.reshape(devices, capacity, tile_rows, feat_width)
    labels = (
        jnp.full((slots_all,), -1, jnp.int32)
        .at[slot_index]
        .set(tile_dst_block)
        .reshape(devices, capacity)
    )
    incoming, in_labels = (
        lax.all_to_all(outgoing, "row", split_axis=0, concat_axis=0, tiled=True),
        lax.all_to_all(labels, "row", split_axis=0, concat_axis=0, tiled=True),
    )
    flat_labels = in_labels.reshape(slots_all)
    select = (flat_labels[:, None] == jnp.arange(nblocks, dtype=jnp.int32)[None, :]).astype(
        jnp.bfloat16
    )
    summed = jnp.einsum(
        "sb,sdf->bdf",
        select,
        incoming.reshape(slots_all, tile_rows, feat_width),
        preferred_element_type=jnp.float32,
    )
    degree = 1.0 + in_degree.astype(jnp.float32)
    aggregate = (summed.reshape(-1, feat_width) / degree[:, None]).astype(jnp.bfloat16)
    preact = (
        jnp.dot(features, w_self, preferred_element_type=jnp.float32)
        + jnp.dot(aggregate, w_neigh, preferred_element_type=jnp.float32)
        + bias
    )
    sigma = jax.nn.sigmoid(preact)
    output = (preact * sigma).astype(jnp.bfloat16)
    delta = (cotangent.astype(jnp.float32) * sigma * (1.0 + preact * (1.0 - sigma))).astype(
        jnp.bfloat16
    )
    vert_total = features.shape[0] * devices
    grad_scale = 1.0 / math.sqrt(vert_total)
    self_term = (
        jnp.einsum("vf,vh->fh", features, delta, preferred_element_type=jnp.float32) * grad_scale
    )
    neigh_term = (
        jnp.einsum("vf,vh->fh", aggregate, delta, preferred_element_type=jnp.float32) * grad_scale
    )
    bias_term = jnp.sum(delta.astype(jnp.float32), axis=0) * grad_scale
    grad_self, grad_neigh, grad_bias = lax.psum((self_term, neigh_term, bias_term), "row")
    back_agg = (
        jnp.einsum("vh,fh->vf", delta, w_neigh, preferred_element_type=jnp.float32)
        / degree[:, None]
    ).astype(jnp.bfloat16)
    gathered = lax.all_gather(back_agg, "row", axis=0, tiled=True).reshape(
        devices * nblocks, tile_rows, feat_width
    )
    picked = jnp.take(gathered, target * nblocks + tile_dst_block, axis=0)
    contrib = jnp.einsum("tsd,tdf->tsf", pattern, picked, preferred_element_type=jnp.float32)
    src_select = (tile_src_block[:, None] == jnp.arange(nblocks, dtype=jnp.int32)[None, :]).astype(
        jnp.float32
    )
    spread = jnp.einsum("tb,tsf->bsf", src_select, contrib, precision=lax.Precision.HIGHEST)
    grad_feat = (
        jnp.einsum("vh,fh->vf", delta, w_self, preferred_element_type=jnp.float32)
        + spread.reshape(-1, feat_width)
    ).astype(jnp.bfloat16)
    return (output, grad_feat, grad_self, grad_neigh, grad_bias)


def solution(mesh):
    return jax.shard_map(
        on_device,
        mesh=mesh,
        in_specs=(
            P(("grp", "row"), None),
            P(("grp", "row"), None, None),
            P(("grp", "row"), None),
            P(("grp", "row")),
            P(("grp", "row")),
            P(("grp", "row")),
            P(),
            P(),
            P(),
            P(("grp", "row"), None),
        ),
        out_specs=(
            P(("grp", "row"), None),
            P(("grp", "row"), None),
            P("grp", None),
            P("grp", None),
            P("grp"),
        ),
        check_vma=False,
    )
```

profile of v0, /device:TPU:0, one launch (start us, length us, event | category | flops | bytes accessed | tf_op | source)
XLA Modules:
  0.0 352.6 jit_solution(8924304795996100422)
XLA Ops:
  8.1 0.8 select_reduce_fusion
  9.6 1.1 scatter_custom_fusion
  11.4 7.4 %all-to-all-start = ((s32[16,1,9]{2,1,0:T(1,128)}), s32[16,1,9]{2,1,0:T(1,128)S(1)}, u32[]{:S(2)}, u32[]{:S(2)}) async-start(s32[16,1,9]{2,1,0:T(1,128)} %bitcast.3), calls=%async_computation | async-start | bytes 16384 | tf_op jit(solution)/shard_map/all_to_all | solution.py:52
  20.2 3.1 gather_fusion
  23.2 8.4 %convert_bitcast_fusion = bf16[128,128,128]{1,2,0:T(8,128)(2,1)} fusion(bf16[128,128,128]{2,1,0:T(8,128)(2,1)} %gather_fusion, pred[128]{0:T(512)(128)(4,1)S(1)} %compare_and_fusion.1, s32[128,128,128]{2,1,0:T(8,128)} %param.11), kind=kOutput, calls=%fused_computation.8 | convolution fusion | flops 543162368 | bytes 16777344 | tf_op jit(solution)/shard_map/tsd,tsf->tdf/dot_general | solution.py:30
  31.7 6.4 %copy.27 = bf16[128,128,128]{2,1,0:T(8,128)(2,1)} copy(bf16[128,128,128]{1,2,0:T(8,128)(2,1)} %convert_bitcast_fusion) | data formatting | bytes 8388608 | tf_op jit(solution)/shard_map/convert_element_type | solution.py:32
  38.1 3.3 broadcast_in_dim.38
  41.4 19.5 %scatter_fusion = bf16[144,128,128]{2,1,0:T(8,128)(2,1)} fusion(bf16[144,128,128]{2,1,0:T(8,128)(2,1)} %broadcast_in_dim.38, s32[128]{0:T(128)S(1)} %fusion.30, bf16[128,128,128]{2,1,0:T(8,128)(2,1)} %copy.27), kind=kCustom, calls=%fused_computation.3 | custom fusion | bytes 12583424 | tf_op jit(solution)/shard_map/scatter | solution.py:41
  60.9 6.2 %all-to-all-start.1 = ((bf16[16,9,128,128]{3,2,1,0:T(8,128)(2,1)}), bf16[16,9,128,128]{3,2,1,0:T(8,128)(2,1)}, u32[]{:S(2)}, u32[]{:S(2)}) async-start(bf16[16,9,128,128]{3,2,1,0:T(8,128)(2,1)} %bitcast.45), calls=%async_computation.1 | async-start | bytes 9437184 | tf_op jit(solution)/shard_map/all_to_all | solution.py:51
  68.8 85.2 %all-to-all-done.1 = bf16[16,9,128,128]{3,2,1,0:T(8,128)(2,1)} async-done(((bf16[16,9,128,128]{3,2,1,0:T(8,128)(2,1)}), bf16[16,9,128,128]{3,2,1,0:T(8,128)(2,1)}, u32[]{:S(2)}, u32[]{:S(2)}) %all-to-all-start.1) | async-done | bytes 4718624 | tf_op jit(solution)/shard_map/all_to_all | solution.py:51
  154.0 4.9 %fusion = f32[4,128,128]{2,0,1:T(4,128)S(1)} fusion(bf16[144,128,128]{2,1,0:T(8,128)(2,1)} %bitcast.8, s32[144]{0:T(256)S(1)} %eq.47), kind=kOutput, calls=%fused_computation.4 | convolution fusion | flops 18874944 | bytes 4981312 | tf_op jit(solution)/shard_map/sb,sdf->bdf/dot_general | solution.py:58
  159.1 1.1 convert_reduce_fusion
  160.2 0.9 fusion.20
  161.1 0.9 convolution_multiply_fusion
  162.1 0.9 fusion.19
  163.1 50.5 %psum.23 = f32[256]{0:T(256)} all-reduce(f32[256]{0:T(256)S(1)} %broadcast_multiply_fusion), channel_id=1, replica_groups=mesh['grp'=2,'row'=16] {'row'}, use_global_device_ids=true, to_apply=%region_7.8 | all-reduce | flops 256 | bytes 2048 | tf_op jit(solution)/shard_map/psum | solution.py:85
  213.6 54.7 %all-reduce.3.cloned.1.call-done = (f32[128,256]{0,1:T(8,128)}, f32[128,256]{1,0:T(8,128)}) async-done(((f32[128,256]{0,1:T(8,128)}, f32[128,256]{1,0:T(8,128)}), (f32[128,256]{0,1:T(8,128)}, f32[128,256]{1,0:T(8,128)})) %all-reduce.3.cloned.1.call-update) | async-done | bytes 262160 | tf_op jit(solution)/shard_map/psum | solution.py:85
  268.3 1.7 copy.33
  269.9 43.0 %all-gather.2.cloned.1.call-done = bf16[8192,128]{1,0:T(8,128)(2,1)} async-done(((bf16[512,128]{1,0:T(8,128)(2,1)}), bf16[8192,128]{1,0:T(8,128)(2,1)}) %all-gather.2.cloned.1.call-update) | async-done | bytes 2097168 | tf_op jit(solution)/shard_map/all_gather | solution.py:90
  312.9 4.6 %gather_fusion.1 = bf16[128,128,128]{2,1,0:T(8,128)(2,1)} fusion(bf16[64,128,128]{2,1,0:T(8,128)(2,1)} %bitcast.46, s32[1024]{0:T(1024)S(1)} %pad_clamp_fusion), kind=kCustom, calls=%fused_computation.1 | custom fusion | bytes 8389120 | tf_op jit(solution)/shard_map/jit(_take)/gather | solution.py:93
  317.6 11.1 %fusion.8 = f32[128,128,128]{1,2,0:T(8,128)} fusion(bf16[128,128,128]{2,1,0:T(8,128)(2,1)} %gather_fusion.1, pred[128]{0:T(512)(128)(4,1)S(1)} %get-tuple-element.24, s32[128,128,128]{2,1,0:T(8,128)} %param.11), kind=kOutput, calls=%fused_computation.13 | convolution fusion | flops 541065216 | bytes 20971648 | tf_op jit(solution)/shard_map/tsd,tdf->tsf/dot_general | solution.py:94
  328.7 9.3 %copy.31 = f32[128,128,128]{2,0,1:T(8,128)} copy(f32[128,128,128]{1,2,0:T(8,128)} %fusion.8) | data formatting | bytes 16777216 | tf_op jit(solution)/shard_map/tsd,tdf->tsf/dot_general | solution.py:94
  338.0 6.2 %fusion.27 = f32[4,128,128]{2,0,1:T(4,128)S(1)} fusion(f32[128,128,128]{2,0,1:T(8,128)} %copy.31, s32[128]{0:T(128)S(1)} %copy-done.5), kind=kOutput, calls=%fused_computation.47 | convolution fusion | flops 100663808 | bytes 8651264 | tf_op jit(solution)/shard_map/tb,tsf->bsf/dot_general | solution.py:98
  344.2 0.9 fusion.18
  (44 shorter events, 6.1 us)
Async XLA Ops:
  7.2 13.0 %copy-start = (bf16[512,128]{1,0:T(8,128)(2,1)S(1)}, bf16[512,128]{1,0:T(8,128)(2,1)}, u32[]{:S(2)}) copy-start(bf16[512,128]{1,0:T(8,128)(2,1)} %param.10) | copy-start | bytes 393220
  11.4 49.5 %all-to-all-start = ((s32[16,1,9]{2,1,0:T(1,128)}), s32[16,1,9]{2,1,0:T(1,128)S(1)}, u32[]{:S(2)}, u32[]{:S(2)}) async-start(s32[16,1,9]{2,1,0:T(1,128)} %bitcast.3), calls=%async_computation | async-start | bytes 16384 | tf_op jit(solution)/shard_map/all_to_all | solution.py:52
  60.9 6.3 %copy-start.4 = (s32[512]{0:T(512)S(1)}, s32[512]{0:T(512)}, u32[]{:S(2)}) copy-start(s32[512]{0:T(512)} %param.15) | copy-start | bytes 6148
  60.9 6.3 %copy-start.1 = (bf16[128,256]{1,0:T(8,128)(2,1)S(1)}, bf16[128,256]{1,0:T(8,128)(2,1)}, u32[]{:S(2)}) copy-start(bf16[128,256]{1,0:T(8,128)(2,1)} %param.16) | copy-start | bytes 196612
  60.9 93.0 %all-to-all-start.1 = ((bf16[16,9,128,128]{3,2,1,0:T(8,128)(2,1)}), bf16[16,9,128,128]{3,2,1,0:T(8,128)(2,1)}, u32[]{:S(2)}, u32[]{:S(2)}) async-start(bf16[16,9,128,128]{3,2,1,0:T(8,128)(2,1)} %bitcast.45), calls=%async_computation.1 | async-start | bytes 9437184 | tf_op jit(solution)/shard_map/all_to_all | solution.py:51
  67.2 91.9 %copy-start.7 = (bf16[512,256]{1,0:T(8,128)(2,1)S(1)}, bf16[512,256]{1,0:T(8,128)(2,1)}, u32[]{:S(2)}) copy-start(bf16[512,256]{1,0:T(8,128)(2,1)} %param.19) | copy-start | bytes 786436
  67.2 91.9 %copy-start.8 = (bf16[128,256]{1,0:T(8,128)(2,1)S(1)}, bf16[128,256]{1,0:T(8,128)(2,1)}, u32[]{:S(2)}) copy-start(bf16[128,256]{1,0:T(8,128)(2,1)} %param.17) | copy-start | bytes 196612
  67.2 91.9 %copy-start.9 = (f32[256]{0:T(256)S(1)}, f32[256]{0:T(256)}, u32[]{:S(2)}) copy-start(f32[256]{0:T(256)} %param.18) | copy-start | bytes 3076
  67.2 201.1 %all-reduce.3.cloned.1.call-start = ((), (), s32[]{:S(2)}) async-start(), calls=%async_computation.3 | async-start | bytes 524288 | tf_op jit(solution)/shard_map/psum | solution.py:85
  158.9 4.1 %copy-start.3 = (s32[128,1]{0,1:T(1,128)S(1)}, s32[128,1]{0,1:T(1,128)}, u32[]{:S(2)}) copy-start(s32[128,1]{0,1:T(1,128)} %param.12) | copy-start | bytes 1540
  158.9 4.1 %copy-start.6 = (s32[128]{0:T(128)S(1)}, s32[128]{0:T(128)}, u32[]{:S(2)}) copy-start(s32[128]{0:T(128)} %param.14) | copy-start | bytes 1540
  162.0 150.9 %all-gather.2.cloned.1.call-start = ((), (), s32[]{:S(2)}) async-start(), calls=%async_computation.2 | async-start | bytes 2228224 | tf_op jit(solution)/shard_map/all_gather | solution.py:90
  328.7 9.3 %copy-start.5 = (s32[128]{0:T(128)S(1)}, s32[128]{0:T(128)}, u32[]{:S(2)}) copy-start(s32[128]{0:T(128)} %param.13) | copy-start | bytes 1540
  338.0 7.1 %copy-start.2 = (f32[128,256]{1,0:T(8,128)S(1)}, f32[128,256]{1,0:T(8,128)}, u32[]{:S(2)}) copy-start(f32[128,256]{1,0:T(8,128)} %get-tuple-element.30) | copy-start | bytes 393220
Sparse Core Ops, SparseCore 0:
  162.2 106.0 all-reduce.2
  271.0 41.8 all-gather.1
where the time goes:
time: 353 us
  waiting for transfers between devices  183 us (52%)
  local copies, waits for them, and re-layouts  51 us (14%)
  blocking collectives  50.5 us (14%)
  matrix products  35.6 us (10%)
  between operations  14.2 us (4%)
  starting transfers between devices  13.7 us (4%)
  other arithmetic  4.6 us (1%)
    all_to_all x1, waiting for transfers between devices, on_device(): lax.all_to_all(outgoing, 'row', split_axis=0, concat_axis=0, tiled=True)  85.2 us
    psum x1, waiting for transfers between devices, on_device(): lax.psum((self_term, neigh_term, bias_term), 'row')  54.7 us
    psum x1, blocking collectives, on_device(): lax.psum((self_term, neigh_term, bias_term), 'row')  50.5 us
    all_gather x1, waiting for transfers between devices, on_device(): lax.all_gather(back_agg, 'row', axis=0, tiled=True)  43 us
    scatter x1, local copies, waits for them, and re-layouts, on_device(): outgoing = jnp.zeros((slots_all, tile_rows, feat_width), jnp.bfloat16).at...  19.5 us
    dot_general x1, matrix products, on_device(): jnp.einsum('tsd,tdf->tsf', pattern, picked, preferred_element_type=jnp.fl...  11.1 us
    dot_general x1, local copies, waits for them, and re-layouts, on_device(): jnp.einsum('tsd,tdf->tsf', pattern, picked, preferred_element_type=jnp.fl...  9.28 us
    dot_general x1, matrix products, on_device(): jnp.einsum('tsd,tsf->tdf', pattern, source, preferred_element_type=jnp.fl...  8.44 us
  transfers between devices with their start and end apart: 4, of which 3 were waited for; matrix products, arithmetic and copies ran while one was open for 13% of the time, Pallas kernels for 0%

commit v1 on v0

v1 whole, which is shorter than its diff:
```python
import functools
import math

import jax
import jax.numpy as jnp
from jax import lax
from jax.experimental import pallas as pl
from jax.experimental.pallas import tpu as pltpu
from jax.sharding import PartitionSpec as P

BF16 = jnp.bfloat16
F32 = jnp.float32
GROUP = 8
MIB = 1 << 20


def swap(value, bits, devices):
    return lax.ppermute(value, "row", [(i, i ^ bits) for i in range(devices)])


def forward_kernel(
    parity, nb, group, slot_ref, x_ref, pat_hbm, s_ref, a_hbm, buf, adj, sems, out_sem
):
    step = pl.program_id(0)
    tiles = slot_ref.shape[0]
    per_unit = nb * nb
    rows = x_ref.shape[0]

    def mine(t):
        slot = slot_ref[t]
        unit = slot // per_unit
        return (unit % 2 == parity) & (unit // (2 * group) == step), slot

    def fetch(t):
        return pltpu.make_async_copy(pat_hbm.at[t], buf.at[t], sems.at[t])

    def start(t, carry):
        hit, _ = mine(t)

        @pl.when(hit)
        def _():
            fetch(t).start()

        return carry

    lax.fori_loop(0, tiles, start, 0)
    xt = x_ref[...].T

    def clear(i, carry):
        adj[pl.ds(i * per_unit, per_unit)] = jnp.zeros((per_unit,) + adj.shape[1:], BF16)
        return carry

    lax.fori_loop(0, group, clear, 0)

    def add(t, carry):
        hit, slot = mine(t)

        @pl.when(hit)
        def _():
            fetch(t).wait()
            unit = slot // per_unit
            place = (unit // 2) % group * per_unit + slot % per_unit
            adj[place] += buf[t].astype(F32).astype(BF16)

        return carry

    lax.fori_loop(0, tiles, add, 0)
    out = pltpu.make_async_copy(
        adj, a_hbm.at[pl.ds(step * group * per_unit, group * per_unit)], out_sem
    )
    out.start()
    tile = adj.shape[1]
    width = 2 if nb % 2 == 0 else 1

    def multiply(m, carry):
        for k in range(0, nb, width):
            weight = jnp.concatenate(
                [
                    adj[pl.ds((m * nb + k + j) * nb, nb)].reshape(rows, tile)
                    for j in range(width)
                ],
                axis=1,
            )
            s_ref[m, :, k * tile : (k + width) * tile] = jnp.dot(
                xt, weight, preferred_element_type=F32
            ).astype(s_ref.dtype)
        return carry

    lax.fori_loop(0, group, multiply, 0)
    out.wait()


def forward_sums(parity, units, dtype, slot, features, patterns, nb):
    rows, feat = features.shape
    tiles, tile, _ = patterns.shape
    group = min(GROUP, units)
    per_unit = nb * nb
    kernel = functools.partial(forward_kernel, parity, nb, group)
    return pl.pallas_call(
        kernel,
        grid_spec=pltpu.PrefetchScalarGridSpec(
            num_scalar_prefetch=1,
            grid=(units // group,),
            in_specs=[
                pl.BlockSpec((rows, feat), lambda g, s: (0, 0)),
                pl.BlockSpec(memory_space=pl.ANY),
            ],
            out_specs=[
                pl.BlockSpec((group, feat, rows), lambda g, s: (g, 0, 0)),
                pl.BlockSpec(memory_space=pl.ANY),
            ],
            scratch_shapes=[
                pltpu.VMEM((tiles, tile, tile), jnp.int32),
                pltpu.VMEM((group * per_unit, tile, tile), BF16),
                pltpu.SemaphoreType.DMA((tiles,)),
                pltpu.SemaphoreType.DMA,
            ],
        ),
        out_shape=[
            jax.ShapeDtypeStruct((units, feat, rows), dtype),
            jax.ShapeDtypeStruct((units * per_unit, tile, tile), BF16),
        ],
        compiler_params=pltpu.CompilerParams(vmem_limit_bytes=40 * MIB),
        cost_estimate=pl.CostEstimate(
            flops=2 * feat * rows * rows * units,
            bytes_accessed=tiles * tile * tile * 2 + units * rows * rows * 2,
            transcendentals=0,
        ),
        name="forward_sums",
    )(slot, features, patterns)


def layer_kernel(
    n_recv,
    own_ref,
    *refs,
):
    recv = refs[:n_recv]
    (deg_ref, x_ref, cot_ref, ws_ref, wn_ref, bias_ref) = refs[n_recv : n_recv + 6]
    out_ref, delta_ref, aggt_ref, back_ref = refs[n_recv + 6 :]
    total = own_ref[0].astype(F32)
    for r in recv:
        total += r[...].reshape(total.shape).astype(F32)
    degree = 1.0 + deg_ref[...].astype(F32)
    degree = jnp.broadcast_to(degree, total.shape)
    aggt = (total / degree).astype(BF16)
    aggt_ref[...] = aggt
    agg = aggt.T
    pre = (
        jnp.dot(x_ref[...], ws_ref[...], preferred_element_type=F32)
        + jnp.dot(agg, wn_ref[...], preferred_element_type=F32)
        + bias_ref[...]
    )
    sigma = jax.nn.sigmoid(pre)
    out_ref[...] = (pre * sigma).astype(BF16)
    delta = (cot_ref[...].astype(F32) * sigma * (1.0 + pre * (1.0 - sigma))).astype(BF16)
    delta_ref[...] = delta
    back = lax.dot_general(
        delta, wn_ref[...], (((1,), (1,)), ((), ())), preferred_element_type=F32
    )
    back_ref[...] = (back / degree.T).astype(BF16)


def layer(own, recv, in_degree, features, cotangent, w_self, w_neigh, bias):
    rows, feat = features.shape
    hidden = w_self.shape[1]

    def first(a):
        return pl.BlockSpec((1,) + a.shape[1:], lambda i: (0, 0, 0))

    def whole(a):
        return pl.BlockSpec(a.shape, lambda i, n=a.ndim: (0,) * n)

    rest = [in_degree, features, cotangent, w_self, w_neigh, bias]
    return pl.pallas_call(
        functools.partial(layer_kernel, len(recv)),
        grid=(1,),
        in_specs=[first(own)] + [first(r) for r in recv] + [whole(a) for a in rest],
        out_specs=[
            pl.BlockSpec((rows, hidden), lambda i: (0, 0)),
            pl.BlockSpec((rows, hidden), lambda i: (0, 0)),
            pl.BlockSpec((feat, rows), lambda i: (0, 0)),
            pl.BlockSpec((rows, feat), lambda i: (0, 0)),
        ],
        out_shape=[
            jax.ShapeDtypeStruct((rows, hidden), BF16),
            jax.ShapeDtypeStruct((rows, hidden), BF16),
            jax.ShapeDtypeStruct((feat, rows), BF16),
            jax.ShapeDtypeStruct((rows, feat), BF16),
        ],
        compiler_params=pltpu.CompilerParams(vmem_limit_bytes=24 * MIB),
        cost_estimate=pl.CostEstimate(
            flops=6 * rows * feat * hidden,
            bytes_accessed=4 * rows * hidden * 2,
            transcendentals=rows * hidden,
        ),
        name="layer",
    )(own, *recv, *rest)


def grad_kernel(scale, me_ref, x_ref, delta_ref, aggt_ref, ws_ref, g_ref, base_ref):
    delta = delta_ref[...]
    feat = x_ref.shape[1]
    gs = jnp.dot(x_ref[...].T, delta, preferred_element_type=F32) * scale
    gn = jnp.dot(aggt_ref[...], delta, preferred_element_type=F32) * scale
    gb = jnp.sum(delta.astype(F32), axis=0, keepdims=True) * scale
    gb = jnp.broadcast_to(gb, (8, gb.shape[1]))
    core = me_ref[0] % 2
    half = feat // 2
    for h in range(2):
        place = core ^ h
        g_ref[place, 0:half] = gs[h * half : (h + 1) * half]
        g_ref[place, half:feat] = gn[h * half : (h + 1) * half]
        g_ref[place, feat : feat + 8] = gb
    base_ref[...] = lax.dot_general(
        delta, ws_ref[...], (((1,), (1,)), ((), ())), preferred_element_type=F32
    )


def grad_terms(scale, me, features, delta, aggt, w_self):
    rows, feat = features.shape
    hidden = delta.shape[1]
    vm = pl.BlockSpec(memory_space=pltpu.VMEM)
    return pl.pallas_call(
        functools.partial(grad_kernel, scale),
        in_specs=[pl.BlockSpec(memory_space=pltpu.SMEM), vm, vm, vm, vm],
        out_specs=[vm, vm],
        out_shape=[
            jax.ShapeDtypeStruct((2, feat + 8, hidden), F32),
            jax.ShapeDtypeStruct((rows, feat), F32),
        ],
        compiler_params=pltpu.CompilerParams(vmem_limit_bytes=24 * MIB),
        cost_estimate=pl.CostEstimate(
            flops=6 * rows * feat * hidden, bytes_accessed=rows * hidden * 8, transcendentals=0
        ),
        name="grad_terms",
    )(me, features, delta, aggt, w_self)


def spread_kernel(places, nb, n_arrays, last, acc_ref, adj_hbm, *refs):
    backs = refs[:n_arrays]
    out_ref, adj, sems = refs[n_arrays:]
    per_unit = nb * nb
    copies = []
    for i, place in enumerate(places):
        copy = pltpu.make_async_copy(
            adj_hbm.at[pl.ds(place * per_unit, per_unit)], adj.at[i], sems.at[i]
        )
        copy.start()
        copies.append(copy)
    total = acc_ref[...]
    rows = total.shape[0]
    i = 0
    for back in backs:
        for j in range(back.shape[0]):
            copies[i].wait()
            tile = adj.shape[2]
            left = jnp.concatenate(
                [adj[i, k * nb : (k + 1) * nb].reshape(rows, tile) for k in range(nb)], axis=1
            )
            total += jnp.dot(left, back[j], preferred_element_type=F32)
            i += 1
    out_ref[...] = total.astype(out_ref.dtype)


def spread(acc, adjacency, places, backs, nb, dtype):
    vm = pl.BlockSpec(memory_space=pltpu.VMEM)
    rows, feat = acc.shape
    per_unit = nb * nb
    tile = adjacency.shape[1]
    n = len(places)
    return pl.pallas_call(
        functools.partial(spread_kernel, tuple(places), nb, len(backs), dtype != F32),
        in_specs=[vm, pl.BlockSpec(memory_space=pl.ANY)] + [vm] * len(backs),
        out_specs=vm,
        out_shape=jax.ShapeDtypeStruct((rows, feat), dtype),
        scratch_shapes=[
            pltpu.VMEM((n, per_unit, tile, tile), BF16),
            pltpu.SemaphoreType.DMA((n,)),
        ],
        compiler_params=pltpu.CompilerParams(vmem_limit_bytes=24 * MIB),
        cost_estimate=pl.CostEstimate(
            flops=2 * rows * rows * feat * n, bytes_accessed=rows * rows * 2 * n, transcendentals=0
        ),
        name="spread",
    )(acc, adjacency, *backs)


def stages_of(devices):
    bits = devices.bit_length() - 1
    assert 1 << bits == devices and bits >= 3
    rest = bits - 1
    return rest // 2, rest - rest // 2


def on_device(
    features,
    patterns,
    tile_dest,
    tile_src_block,
    tile_dst_block,
    in_degree,
    w_self,
    w_neigh,
    bias,
    cotangent,
):
    devices = lax.axis_size("row")
    me = lax.axis_index("row")
    tile = patterns.shape[1]
    rows, feat = features.shape
    nb = rows // tile
    y_bits, z_bits = stages_of(devices)
    ny, nz = 1 << y_bits, 1 << z_bits
    units = devices // 2
    small = devices <= 16

    unit = jnp.bitwise_xor(tile_dest[:, 0], me)
    slot = (unit * nb + tile_dst_block) * nb + tile_src_block

    s_other, a_other = forward_sums(1, units, BF16, slot, features, patterns, nb)
    s_recv = swap(s_other, 1, devices)
    s_own, a_own = forward_sums(0, units, F32 if small else BF16, slot, features, patterns, nb)

    def chip_sum(m):
        return s_own[m].astype(F32) + s_recv[m].astype(F32)

    if small:
        y_recv = [None] * nz
        for n in reversed(range(nz)):
            y_recv[n] = [
                swap(chip_sum(n * ny + k).astype(BF16), 2 * k, devices) for k in range(1, ny)
            ]
    else:
        s5 = s_own.reshape(nz, ny, feat, rows)
        r5 = s_recv.reshape(nz, ny, feat, rows)
        got = [
            swap((s5[:, k].astype(F32) + r5[:, k].astype(F32)).astype(BF16), 2 * k, devices)
            for k in range(1, ny)
        ]
        y_recv = [[g[n] for g in got] for n in range(nz)]
    z_recv = []
    for n in reversed(range(1, nz)):
        total = chip_sum(n * ny)
        for r in y_recv[n]:
            total = total + r.astype(F32)
        z_recv.append(swap(total.astype(BF16), 2 * ny * n, devices))

    output, delta, aggt, back = layer(
        s_own,
        [s_recv] + [r[None] for r in y_recv[0]] + [r[None] for r in z_recv],
        in_degree.reshape(1, rows),
        features,
        cotangent,
        w_self,
        w_neigh,
        bias.reshape(1, -1),
    )

    have = {0: back}
    for n in range(1, nz):
        have[n * ny] = swap(back, 2 * ny * n, devices)
    for n in range(nz):
        for k in range(1, ny):
            have[n * ny + k] = swap(have[n * ny], 2 * k, devices)
    other = {m: swap(have[m], 1, devices) for m in have}

    scale = 1.0 / math.sqrt(rows * devices)
    terms, base = grad_terms(scale, me.reshape(1).astype(jnp.int32), features, delta, aggt, w_self)
    half = terms[0] + swap(terms[1], 1, devices)
    bit = 2
    while bit < devices:
        half = half + swap(half, bit, devices)
        bit *= 2
    second = swap(half, 1, devices)
    even = me % 2 == 0
    low, high = jnp.where(even, half, second), jnp.where(even, second, half)
    h = feat // 2
    grad_self = jnp.concatenate([low[:h], high[:h]], axis=0)
    grad_neigh = jnp.concatenate([low[h:feat], high[h:feat]], axis=0)
    grad_bias = low[feat]

    acc = base
    order = sorted(have, key=lambda m: (m != 0, m))
    for at in range(0, units, GROUP):
        places = order[at : at + GROUP]
        acc = spread(acc, a_own, places, [have[m][None] for m in places], nb, F32)
    for at in range(0, units, GROUP):
        places = order[at : at + GROUP]
        dtype = BF16 if at + GROUP >= units else F32
        acc = spread(acc, a_other, places, [other[m][None] for m in places], nb, dtype)
    return (output, acc, grad_self, grad_neigh, grad_bias)


def solution(mesh):
    return jax.shard_map(
        on_device,
        mesh=mesh,
        in_specs=(
            P(("grp", "row"), None),
            P(("grp", "row"), None, None),
            P(("grp", "row"), None),
            P(("grp", "row")),
            P(("grp", "row")),
            P(("grp", "row")),
            P(),
            P(),
            P(),
            P(("grp", "row"), None),
        ),
        out_specs=(
            P(("grp", "row"), None),
            P(("grp", "row"), None),
            P("grp", None),
            P("grp", None),
            P("grp"),
        ),
        check_vma=False,
    )
```

time: 353 us -> 102 us (0.29)
  waiting for transfers between devices: 183 us -> 30.5 us
  blocking collectives: 50.5 us -> 0 us
  local copies, waits for them, and re-layouts: 51 us -> 7.26 us
  Pallas kernels: 0 us -> 37.1 us
  matrix products: 35.6 us -> 0 us
  between operations: 14.2 us -> 0.89 us
  starting transfers between devices: 13.7 us -> 23.9 us
    all_to_all x2 -> x0, waiting for transfers between devices: 85.2 us -> none  [the longest x1 85.2 us: on_device(): lax.all_to_all(outgoing, 'row', split_axis=0, concat_axis=0, tiled=True)]
    psum x1 -> x0, waiting for transfers between devices: 54.7 us -> none  [on_device(): lax.psum((self_term, neigh_term, bias_term), 'row')]
    psum x1 -> x0, blocking collectives: 50.5 us -> none  [on_device(): lax.psum((self_term, neigh_term, bias_term), 'row')]
    all_gather x1 -> x0, waiting for transfers between devices: 43 us -> none  [on_device(): lax.all_gather(back_agg, 'row', axis=0, tiled=True)]
    pallas_call x0 -> x6, Pallas kernels: none -> 37.1 us  [the longest x2 28.8 us: forward_sums(): pl.pallas_call(kernel, grid_spec=pltpu.PrefetchScalarGridSpec(num_scalar_...]
    dot_general x10 -> x0, matrix products: 35.6 us -> none  [the longest x1 11.1 us: on_device(): jnp.einsum('tsd,tdf->tsf', pattern, picked, preferred_element_type=jnp.fl...]
    ppermute x0 -> x28, waiting for transfers between devices: none -> 30.5 us  [swap(): return lax.ppermute(value, 'row', [(i, i ^ bits) for i in range(devices)])]
    ppermute x0 -> x28, starting transfers between devices: none -> 23.9 us  [swap(): return lax.ppermute(value, 'row', [(i, i ^ bits) for i in range(devices)])]
  transfers between devices with their start and end apart: 4 -> 28, of which waited for: 3 -> 14; matrix products, arithmetic and copies ran while one was open for 13% -> 0% of each run, Pallas kernels for 0% -> 18%
where the time goes in v1:
time: 102 us
  Pallas kernels  37.1 us (36%)
  waiting for transfers between devices  30.5 us (30%)
  starting transfers between devices  23.9 us (23%)
  local copies, waits for them, and re-layouts  7.26 us (7%)
  other arithmetic  2.49 us (2%)
    ppermute x28, waiting for transfers between devices, swap(): return lax.ppermute(value, 'row', [(i, i ^ bits) for i in range(devices)])  30.5 us
    pallas_call x2, Pallas kernels, forward_sums(): pl.pallas_call(kernel, grid_spec=pltpu.PrefetchScalarGridSpec(num_scalar_...  28.8 us
    ppermute x28, starting transfers between devices, swap(): return lax.ppermute(value, 'row', [(i, i ^ bits) for i in range(devices)])  23.9 us
    pallas_call x2, Pallas kernels, spread(): pl.pallas_call(functools.partial(spread_kernel, tuple(places), nb, len(ba...  6.72 us
    unnamed x22, local copies, waits for them, and re-layouts  6.67 us
  transfers between devices with their start and end apart: 28, of which 14 were waited for; matrix products, arithmetic and copies ran while one was open for 0% of the time, Pallas kernels for 18%

profile of v1, /device:TPU:0, one launch (start us, length us, event | category | flops | bytes accessed | tf_op | source)
XLA Modules:
  0.0 102.1 jit_solution(15730862181815127118)
XLA Ops:
  1.3 3.4 %copy-done = s32[128,128,128]{2,1,0:T(8,128)S(1)} copy-done((s32[128,128,128]{2,1,0:T(8,128)S(1)}, s32[128,128,128]{2,1,0:T(8,128)}, u32[]{:S(2)}) %copy-start) | copy-done | bytes 8388632
  5.6 17.4 %forward_sums.3 = (bf16[8,128,512]{2,1,0:T(8,128)(2,1)S(1)}, bf16[128,128,128]{2,1,0:T(8,128)(2,1)S(1)}) custom-call(s32[128]{0:T(128)S(1)} %fusion.8.slot_ref, bf16[512,128]{1,0:T(8,128)(2,1)S(1)} %copy-done.5, s32[128,128,128]{2,1,0:T(8,128)S(1)} %copy-done), custom_call_target="tpu_custom_call" | custom-call | flops 536870912 | bytes 8388608 | tf_op jit(solution)/shard_map/forward_sums/pallas_call | solution.py:99
  23.9 11.4 %forward_sums.2 = (f32[8,128,512]{2,1,0:T(8,128)S(1)}, bf16[128,128,128]{2,1,0:T(8,128)(2,1)S(1)}) custom-call(s32[128]{0:T(128)S(1)} %fusion.8.slot_ref, bf16[512,128]{1,0:T(8,128)(2,1)S(1)} %copy-done.5, s32[128,128,128]{2,1,0:T(8,128)} %pat_hbm.3), custom_call_target="tpu_custom_call" | custom-call | flops 536870912 | bytes 8388608 | tf_op jit(solution)/shard_map/forward_sums/pallas_call | solution.py:99
  35.4 2.7 %collective-permute-start.2 = (bf16[128,512]{1,0:T(8,128)(2,1)S(1)}, bf16[128,512]{1,0:T(8,128)(2,1)S(1)}, u32[]{:S(2)}, u32[]{:S(2)}) collective-permute-start(bf16[128,512]{1,0:T(8,128)(2,1)S(1)} %get-tuple-element.30), channel_id=1, source_target_pairs={{0,2},{1,3},{2,0},{3,1},{4,6},{5,7},{6,4},{7,5},{8,10},{9,11},{10,... | collective-permute-start | bytes 393224 | tf_op jit(solution)/shard_map/ppermute | solution.py:18
  38.2 1.9 %collective-permute-start.6 = (bf16[128,512]{1,0:T(8,128)(2,1)S(1)}, bf16[128,512]{1,0:T(8,128)(2,1)S(1)}, u32[]{:S(2)}, u32[]{:S(2)}) collective-permute-start(bf16[128,512]{1,0:T(8,128)(2,1)S(1)} %get-tuple-element.28), channel_id=1, source_target_pairs={{0,2},{1,3},{2,0},{3,1},{4,6},{5,7},{6,4},{7,5},{8,10},{9,11},{10,... | collective-permute-start | bytes 393224 | tf_op jit(solution)/shard_map/ppermute | solution.py:18
  40.2 2.2 %collective-permute-done.2 = bf16[128,512]{1,0:T(8,128)(2,1)S(1)} collective-permute-done((bf16[128,512]{1,0:T(8,128)(2,1)S(1)}, bf16[128,512]{1,0:T(8,128)(2,1)S(1)}, u32[]{:S(2)}, u32[]{:S(2)}) %collective-permute-start.2) | collective-permute-done | bytes 131104 | tf_op jit(solution)/shard_map/ppermute | solution.py:18
  42.4 2.8 %collective-permute-done.4 = bf16[128,512]{1,0:T(8,128)(2,1)S(1)} collective-permute-done((bf16[128,512]{1,0:T(8,128)(2,1)S(1)}, bf16[128,512]{1,0:T(8,128)(2,1)S(1)}, u32[]{:S(2)}, u32[]{:S(2)}) %collective-permute-start.4) | collective-permute-done | bytes 131104 | tf_op jit(solution)/shard_map/ppermute | solution.py:18
  45.2 2.8 %collective-permute-done.6 = bf16[128,512]{1,0:T(8,128)(2,1)S(1)} collective-permute-done((bf16[128,512]{1,0:T(8,128)(2,1)S(1)}, bf16[128,512]{1,0:T(8,128)(2,1)S(1)}, u32[]{:S(2)}, u32[]{:S(2)}) %collective-permute-start.6) | collective-permute-done | bytes 131104 | tf_op jit(solution)/shard_map/ppermute | solution.py:18
  48.2 2.2 %collective-permute-start.7 = (bf16[128,512]{1,0:T(8,128)(2,1)S(1)}, bf16[128,512]{1,0:T(8,128)(2,1)S(1)}, u32[]{:S(2)}, u32[]{:S(2)}) collective-permute-start(bf16[128,512]{1,0:T(8,128)(2,1)S(1)} %get-tuple-element.25), channel_id=1, source_target_pairs={{0,4},{1,5},{2,6},{3,7},{4,0},{5,1},{6,2},{7,3},{8,12},{9,13},{10,... | collective-permute-start | bytes 393224 | tf_op jit(solution)/shard_map/ppermute | solution.py:18
  50.4 2.4 %collective-permute-start.3 = (bf16[128,512]{1,0:T(8,128)(2,1)S(1)}, bf16[128,512]{1,0:T(8,128)(2,1)S(1)}, u32[]{:S(2)}, u32[]{:S(2)}) collective-permute-start(bf16[128,512]{1,0:T(8,128)(2,1)S(1)} %get-tuple-element.27), channel_id=1, source_target_pairs={{0,12},{1,13},{2,14},{3,15},{4,8},{5,9},{6,10},{7,11},{8,4},{9,5},... | collective-permute-start | bytes 393224 | tf_op jit(solution)/shard_map/ppermute | solution.py:18
  52.9 1.4 %collective-permute-done.7 = bf16[128,512]{1,0:T(8,128)(2,1)S(1)} collective-permute-done((bf16[128,512]{1,0:T(8,128)(2,1)S(1)}, bf16[128,512]{1,0:T(8,128)(2,1)S(1)}, u32[]{:S(2)}, u32[]{:S(2)}) %collective-permute-start.7) | collective-permute-done | bytes 131104 | tf_op jit(solution)/shard_map/ppermute | solution.py:18
  54.3 4.8 %collective-permute-done.3 = bf16[128,512]{1,0:T(8,128)(2,1)S(1)} collective-permute-done((bf16[128,512]{1,0:T(8,128)(2,1)S(1)}, bf16[128,512]{1,0:T(8,128)(2,1)S(1)}, u32[]{:S(2)}, u32[]{:S(2)}) %collective-permute-start.3) | collective-permute-done | bytes 131104 | tf_op jit(solution)/shard_map/ppermute | solution.py:18
  59.1 4.3 %collective-permute-done.5 = bf16[128,512]{1,0:T(8,128)(2,1)S(1)} collective-permute-done((bf16[128,512]{1,0:T(8,128)(2,1)S(1)}, bf16[128,512]{1,0:T(8,128)(2,1)S(1)}, u32[]{:S(2)}, u32[]{:S(2)}) %collective-permute-start.5) | collective-permute-done | bytes 131104 | tf_op jit(solution)/shard_map/ppermute | solution.py:18
  66.5 1.6 %collective-permute-start.24 = (f32[136,256]{1,0:T(8,128)S(1)}, f32[136,256]{1,0:T(8,128)S(1)}, u32[]{:S(2)}, u32[]{:S(2)}) collective-permute-start(f32[136,256]{1,0:T(8,128)S(1)} %bitcast_add_fusion.3), channel_id=1, source_target_pairs={{0,2},{1,3},{2,0},{3,1},{4,6},{5,7},{6,4},{7,5},{8,10},{9,11},{10,... | collective-permute-start | bytes 417800 | tf_op jit(solution)/shard_map/ppermute | solution.py:18
  68.1 3.2 %collective-permute-start.11 = (bf16[512,128]{1,0:T(8,128)(2,1)S(1)}, bf16[512,128]{1,0:T(8,128)(2,1)S(1)}, u32[]{:S(2)}, u32[]{:S(2)}) collective-permute-start(bf16[512,128]{1,0:T(8,128)(2,1)S(1)} %get-tuple-element.22), channel_id=1, source_target_pairs={{0,8},{1,9},{2,10},{3,11},{4,12},{5,13},{6,14},{7,15},{8,0},{9,1},... | collective-permute-start | bytes 393224 | tf_op jit(solution)/shard_map/ppermute | solution.py:18
  72.4 2.7 %collective-permute-start.13 = (bf16[512,128]{1,0:T(8,128)(2,1)S(1)}, bf16[512,128]{1,0:T(8,128)(2,1)S(1)}, u32[]{:S(2)}, u32[]{:S(2)}) collective-permute-start(bf16[512,128]{1,0:T(8,128)(2,1)S(1)} %get-tuple-element.22), channel_id=1, source_target_pairs={{0,12},{1,13},{2,14},{3,15},{4,8},{5,9},{6,10},{7,11},{8,4},{9,5},... | collective-permute-start | bytes 393224 | tf_op jit(solution)/shard_map/ppermute | solution.py:18
  75.1 1.5 %collective-permute-start.8 = (bf16[512,128]{1,0:T(8,128)(2,1)S(1)}, bf16[512,128]{1,0:T(8,128)(2,1)S(1)}, u32[]{:S(2)}, u32[]{:S(2)}) collective-permute-start(bf16[512,128]{1,0:T(8,128)(2,1)S(1)} %get-tuple-element.22), channel_id=1, source_target_pairs={{0,2},{1,3},{2,0},{3,1},{4,6},{5,7},{6,4},{7,5},{8,10},{9,11},{10,... | collective-permute-start | bytes 393224 | tf_op jit(solution)/shard_map/ppermute | solution.py:18
  77.6 1.5 %collective-permute-done.25 = f32[136,256]{1,0:T(8,128)S(1)} collective-permute-done((f32[136,256]{1,0:T(8,128)S(1)}, f32[136,256]{1,0:T(8,128)S(1)}, u32[]{:S(2)}, u32[]{:S(2)}) %collective-permute-start.25) | collective-permute-done | bytes 139296 | tf_op jit(solution)/shard_map/ppermute | solution.py:18
  79.7 3.3 %collective-permute-done.13 = bf16[512,128]{1,0:T(8,128)(2,1)S(1)} collective-permute-done((bf16[512,128]{1,0:T(8,128)(2,1)S(1)}, bf16[512,128]{1,0:T(8,128)(2,1)S(1)}, u32[]{:S(2)}, u32[]{:S(2)}) %collective-permute-start.13) | collective-permute-done | bytes 131104 | tf_op jit(solution)/shard_map/ppermute | solution.py:18
  83.0 1.5 %collective-permute-start.26 = (f32[136,256]{1,0:T(8,128)S(1)}, f32[136,256]{1,0:T(8,128)S(1)}, u32[]{:S(2)}, u32[]{:S(2)}) collective-permute-start(f32[136,256]{1,0:T(8,128)S(1)} %add.83), channel_id=1, source_target_pairs={{0,8},{1,9},{2,10},{3,11},{4,12},{5,13},{6,14},{7,15},{8,0},{9,1},... | collective-permute-start | bytes 417800 | tf_op jit(solution)/shard_map/ppermute | solution.py:18
  86.0 3.4 %collective-permute-done.14 = bf16[512,128]{1,0:T(8,128)(2,1)S(1)} collective-permute-done((bf16[512,128]{1,0:T(8,128)(2,1)S(1)}, bf16[512,128]{1,0:T(8,128)(2,1)S(1)}, u32[]{:S(2)}, u32[]{:S(2)}) %collective-permute-start.14) | collective-permute-done | bytes 131104 | tf_op jit(solution)/shard_map/ppermute | solution.py:18
  91.0 2.3 %copy-done.4 = bf16[128,128,128]{2,1,0:T(8,128)(2,1)S(1)} copy-done((bf16[128,128,128]{2,1,0:T(8,128)(2,1)S(1)}, bf16[128,128,128]{2,1,0:T(8,128)(2,1)}, u32[]{:S(2)}) %copy-start.4) | copy-done | bytes 4194328
  93.4 3.0 %spread.2.acc_ref = f32[512,128]{1,0:T(8,128)S(1)} custom-call(f32[512,128]{1,0:T(8,128)S(1)} %get-tuple-element.20.acc_ref, bf16[128,128,128]{2,1,0:T(8,128)(2,1)S(1)} %copy-done.4, bf16[1,512,128]{2,1,0:T(8,128)(2,1)S(1)} %bitcast.54, bf16[1,512,128]{2,1,0:T(8,128)(2,1)S(1)} %bitcast.59, bf16[1,512,128]{2,1,0:T(8,128)(2,1)S(1)} %bitcast.55, ...), custom_call_target="tpu_custom_call" | custom-call | flops 536870912 | bytes 4194304 | tf_op jit(solution)/shard_map/spread/pallas_call | solution.py:272
  96.5 3.7 %spread.3 = bf16[512,128]{1,0:T(8,128)(2,1)} custom-call(f32[512,128]{1,0:T(8,128)S(1)} %spread.2.acc_ref, bf16[128,128,128]{2,1,0:T(8,128)(2,1)S(1)} %copy-done.2, bf16[1,512,128]{2,1,0:T(8,128)(2,1)S(1)} %bitcast.57, bf16[1,512,128]{2,1,0:T(8,128)(2,1)S(1)} %bitcast.62, bf16[1,512,128]{2,1,0:T(8,128)(2,1)S(1)} %bitcast.64, ...), custom_call_target="tpu_custom_call" | custom-call | flops 536870912 | bytes 4194304 | tf_op jit(solution)/shard_map/spread/pallas_call | solution.py:272
  (73 shorter events, 13.7 us)
Async XLA Ops:
  23.1 12.1 %collective-permute-start = (bf16[8,128,512]{2,1,0:T(8,128)(2,1)S(1)}, bf16[8,128,512]{2,1,0:T(8,128)(2,1)S(1)}, u32[]{:S(2)}, u32[]{:S(2)}) collective-permute-start(bf16[8,128,512]{2,1,0:T(8,128)(2,1)S(1)} %get-tuple-element.16), channel_id=1, source_target_pairs={{0,1},{1,0},{2,3},{3,2},{4,5},{5,4},{6,7},{7,6},{8,9},{9,8},{10,11... | collective-permute-start | bytes 3145736 | tf_op jit(solution)/shard_map/ppermute | solution.py:18
  35.4 6.9 %collective-permute-start.2 = (bf16[128,512]{1,0:T(8,128)(2,1)S(1)}, bf16[128,512]{1,0:T(8,128)(2,1)S(1)}, u32[]{:S(2)}, u32[]{:S(2)}) collective-permute-start(bf16[128,512]{1,0:T(8,128)(2,1)S(1)} %get-tuple-element.30), channel_id=1, source_target_pairs={{0,2},{1,3},{2,0},{3,1},{4,6},{5,7},{6,4},{7,5},{8,10},{9,11},{10,... | collective-permute-start | bytes 393224 | tf_op jit(solution)/shard_map/ppermute | solution.py:18
  38.1 7.1 %collective-permute-start.4 = (bf16[128,512]{1,0:T(8,128)(2,1)S(1)}, bf16[128,512]{1,0:T(8,128)(2,1)S(1)}, u32[]{:S(2)}, u32[]{:S(2)}) collective-permute-start(bf16[128,512]{1,0:T(8,128)(2,1)S(1)} %get-tuple-element.29), channel_id=1, source_target_pairs={{0,2},{1,3},{2,0},{3,1},{4,6},{5,7},{6,4},{7,5},{8,10},{9,11},{10,... | collective-permute-start | bytes 393224 | tf_op jit(solution)/shard_map/ppermute | solution.py:18
  38.2 9.8 %collective-permute-start.6 = (bf16[128,512]{1,0:T(8,128)(2,1)S(1)}, bf16[128,512]{1,0:T(8,128)(2,1)S(1)}, u32[]{:S(2)}, u32[]{:S(2)}) collective-permute-start(bf16[128,512]{1,0:T(8,128)(2,1)S(1)} %get-tuple-element.28), channel_id=1, source_target_pairs={{0,2},{1,3},{2,0},{3,1},{4,6},{5,7},{6,4},{7,5},{8,10},{9,11},{10,... | collective-permute-start | bytes 393224 | tf_op jit(solution)/shard_map/ppermute | solution.py:18
  40.1 12.7 %collective-permute-start.1 = (bf16[128,512]{1,0:T(8,128)(2,1)S(1)}, bf16[128,512]{1,0:T(8,128)(2,1)S(1)}, u32[]{:S(2)}, u32[]{:S(2)}) collective-permute-start(bf16[128,512]{1,0:T(8,128)(2,1)S(1)} %get-tuple-element.31), channel_id=1, source_target_pairs={{0,2},{1,3},{2,0},{3,1},{4,6},{5,7},{6,4},{7,5},{8,10},{9,11},{10,... | collective-permute-start | bytes 393224 | tf_op jit(solution)/shard_map/ppermute | solution.py:18
  48.2 6.1 %collective-permute-start.7 = (bf16[128,512]{1,0:T(8,128)(2,1)S(1)}, bf16[128,512]{1,0:T(8,128)(2,1)S(1)}, u32[]{:S(2)}, u32[]{:S(2)}) collective-permute-start(bf16[128,512]{1,0:T(8,128)(2,1)S(1)} %get-tuple-element.25), channel_id=1, source_target_pairs={{0,4},{1,5},{2,6},{3,7},{4,0},{5,1},{6,2},{7,3},{8,12},{9,13},{10,... | collective-permute-start | bytes 393224 | tf_op jit(solution)/shard_map/ppermute | solution.py:18
  50.4 8.7 %collective-permute-start.3 = (bf16[128,512]{1,0:T(8,128)(2,1)S(1)}, bf16[128,512]{1,0:T(8,128)(2,1)S(1)}, u32[]{:S(2)}, u32[]{:S(2)}) collective-permute-start(bf16[128,512]{1,0:T(8,128)(2,1)S(1)} %get-tuple-element.27), channel_id=1, source_target_pairs={{0,12},{1,13},{2,14},{3,15},{4,8},{5,9},{6,10},{7,11},{8,4},{9,5},... | collective-permute-start | bytes 393224 | tf_op jit(solution)/shard_map/ppermute | solution.py:18
  52.8 10.7 %collective-permute-start.5 = (bf16[128,512]{1,0:T(8,128)(2,1)S(1)}, bf16[128,512]{1,0:T(8,128)(2,1)S(1)}, u32[]{:S(2)}, u32[]{:S(2)}) collective-permute-start(bf16[128,512]{1,0:T(8,128)(2,1)S(1)} %get-tuple-element.26), channel_id=1, source_target_pairs={{0,8},{1,9},{2,10},{3,11},{4,12},{5,13},{6,14},{7,15},{8,0},{9,1},... | collective-permute-start | bytes 393224 | tf_op jit(solution)/shard_map/ppermute | solution.py:18
  66.5 5.8 %collective-permute-start.24 = (f32[136,256]{1,0:T(8,128)S(1)}, f32[136,256]{1,0:T(8,128)S(1)}, u32[]{:S(2)}, u32[]{:S(2)}) collective-permute-start(f32[136,256]{1,0:T(8,128)S(1)} %bitcast_add_fusion.3), channel_id=1, source_target_pairs={{0,2},{1,3},{2,0},{3,1},{4,6},{5,7},{6,4},{7,5},{8,10},{9,11},{10,... | collective-permute-start | bytes 417800 | tf_op jit(solution)/shard_map/ppermute | solution.py:18
  68.1 9.2 %collective-permute-start.9 = (bf16[512,128]{1,0:T(8,128)(2,1)S(1)}, bf16[512,128]{1,0:T(8,128)(2,1)S(1)}, u32[]{:S(2)}, u32[]{:S(2)}) collective-permute-start(bf16[512,128]{1,0:T(8,128)(2,1)S(1)} %get-tuple-element.22), channel_id=1, source_target_pairs={{0,4},{1,5},{2,6},{3,7},{4,0},{5,1},{6,2},{7,3},{8,12},{9,13},{10,... | collective-permute-start | bytes 393224 | tf_op jit(solution)/shard_map/ppermute | solution.py:18
  68.1 9.2 %collective-permute-start.11 = (bf16[512,128]{1,0:T(8,128)(2,1)S(1)}, bf16[512,128]{1,0:T(8,128)(2,1)S(1)}, u32[]{:S(2)}, u32[]{:S(2)}) collective-permute-start(bf16[512,128]{1,0:T(8,128)(2,1)S(1)} %get-tuple-element.22), channel_id=1, source_target_pairs={{0,8},{1,9},{2,10},{3,11},{4,12},{5,13},{6,14},{7,15},{8,0},{9,1},... | collective-permute-start | bytes 393224 | tf_op jit(solution)/shard_map/ppermute | solution.py:18
  72.3 6.8 %collective-permute-start.25 = (f32[136,256]{1,0:T(8,128)S(1)}, f32[136,256]{1,0:T(8,128)S(1)}, u32[]{:S(2)}, u32[]{:S(2)}) collective-permute-start(f32[136,256]{1,0:T(8,128)S(1)} %add.82), channel_id=1, source_target_pairs={{0,4},{1,5},{2,6},{3,7},{4,0},{5,1},{6,2},{7,3},{8,12},{9,13},{10,... | collective-permute-start | bytes 417800 | tf_op jit(solution)/shard_map/ppermute | solution.py:18
  72.4 10.6 %collective-permute-start.13 = (bf16[512,128]{1,0:T(8,128)(2,1)S(1)}, bf16[512,128]{1,0:T(8,128)(2,1)S(1)}, u32[]{:S(2)}, u32[]{:S(2)}) collective-permute-start(bf16[512,128]{1,0:T(8,128)(2,1)S(1)} %get-tuple-element.22), channel_id=1, source_target_pairs={{0,12},{1,13},{2,14},{3,15},{4,8},{5,9},{6,10},{7,11},{8,4},{9,5},... | collective-permute-start | bytes 393224 | tf_op jit(solution)/shard_map/ppermute | solution.py:18
  75.1 9.4 %collective-permute-start.8 = (bf16[512,128]{1,0:T(8,128)(2,1)S(1)}, bf16[512,128]{1,0:T(8,128)(2,1)S(1)}, u32[]{:S(2)}, u32[]{:S(2)}) collective-permute-start(bf16[512,128]{1,0:T(8,128)(2,1)S(1)} %get-tuple-element.22), channel_id=1, source_target_pairs={{0,2},{1,3},{2,0},{3,1},{4,6},{5,7},{6,4},{7,5},{8,10},{9,11},{10,... | collective-permute-start | bytes 393224 | tf_op jit(solution)/shard_map/ppermute | solution.py:18
  77.2 7.7 %collective-permute-start.15 = (bf16[512,128]{1,0:T(8,128)(2,1)S(1)}, bf16[512,128]{1,0:T(8,128)(2,1)S(1)}, u32[]{:S(2)}, u32[]{:S(2)}) collective-permute-start(bf16[512,128]{1,0:T(8,128)(2,1)S(1)} %get-tuple-element.22), channel_id=1, source_target_pairs={{0,1},{1,0},{2,3},{3,2},{4,5},{5,4},{6,7},{7,6},{8,9},{9,8},{10,11... | collective-permute-start | bytes 393224 | tf_op jit(solution)/shard_map/ppermute | solution.py:18
  77.3 7.7 %collective-permute-start.10 = (bf16[512,128]{1,0:T(8,128)(2,1)S(1)}, bf16[512,128]{1,0:T(8,128)(2,1)S(1)}, u32[]{:S(2)}, u32[]{:S(2)}) collective-permute-start(bf16[512,128]{1,0:T(8,128)(2,1)S(1)} %collective-permute-done.9), channel_id=1, source_target_pairs={{0,2},{1,3},{2,0},{3,1},{4,6},{5,7},{6,4},{7,5},{8,10},{9,11},{10,... | collective-permute-start | bytes 393224 | tf_op jit(solution)/shard_map/ppermute | solution.py:18
  79.1 6.9 %collective-permute-start.12 = (bf16[512,128]{1,0:T(8,128)(2,1)S(1)}, bf16[512,128]{1,0:T(8,128)(2,1)S(1)}, u32[]{:S(2)}, u32[]{:S(2)}) collective-permute-start(bf16[512,128]{1,0:T(8,128)(2,1)S(1)} %collective-permute-done.11), channel_id=1, source_target_pairs={{0,2},{1,3},{2,0},{3,1},{4,6},{5,7},{6,4},{7,5},{8,10},{9,11},{10,... | collective-permute-start | bytes 393224 | tf_op jit(solution)/shard_map/ppermute | solution.py:18
  83.0 7.4 %collective-permute-start.26 = (f32[136,256]{1,0:T(8,128)S(1)}, f32[136,256]{1,0:T(8,128)S(1)}, u32[]{:S(2)}, u32[]{:S(2)}) collective-permute-start(f32[136,256]{1,0:T(8,128)S(1)} %add.83), channel_id=1, source_target_pairs={{0,8},{1,9},{2,10},{3,11},{4,12},{5,13},{6,14},{7,15},{8,0},{9,1},... | collective-permute-start | bytes 417800 | tf_op jit(solution)/shard_map/ppermute | solution.py:18
  84.5 5.0 %collective-permute-start.14 = (bf16[512,128]{1,0:T(8,128)(2,1)S(1)}, bf16[512,128]{1,0:T(8,128)(2,1)S(1)}, u32[]{:S(2)}, u32[]{:S(2)}) collective-permute-start(bf16[512,128]{1,0:T(8,128)(2,1)S(1)} %collective-permute-done.13), channel_id=1, source_target_pairs={{0,2},{1,3},{2,0},{3,1},{4,6},{5,7},{6,4},{7,5},{8,10},{9,11},{10,... | collective-permute-start | bytes 393224 | tf_op jit(solution)/shard_map/ppermute | solution.py:18
  89.4 7.0 %collective-permute-start.21 = (bf16[512,128]{1,0:T(8,128)(2,1)S(1)}, bf16[512,128]{1,0:T(8,128)(2,1)S(1)}, u32[]{:S(2)}, u32[]{:S(2)}) collective-permute-start(bf16[512,128]{1,0:T(8,128)(2,1)S(1)} %collective-permute-done.13), channel_id=1, source_target_pairs={{0,1},{1,0},{2,3},{3,2},{4,5},{5,4},{6,7},{7,6},{8,9},{9,8},{10,11... | collective-permute-start | bytes 393224 | tf_op jit(solution)/shard_map/ppermute | solution.py:18
  89.4 7.0 %collective-permute-start.18 = (bf16[512,128]{1,0:T(8,128)(2,1)S(1)}, bf16[512,128]{1,0:T(8,128)(2,1)S(1)}, u32[]{:S(2)}, u32[]{:S(2)}) collective-permute-start(bf16[512,128]{1,0:T(8,128)(2,1)S(1)} %collective-permute-done.10), channel_id=1, source_target_pairs={{0,1},{1,0},{2,3},{3,2},{4,5},{5,4},{6,7},{7,6},{8,9},{9,8},{10,11... | collective-permute-start | bytes 393224 | tf_op jit(solution)/shard_map/ppermute | solution.py:18
  89.9 6.5 %collective-permute-start.20 = (bf16[512,128]{1,0:T(8,128)(2,1)S(1)}, bf16[512,128]{1,0:T(8,128)(2,1)S(1)}, u32[]{:S(2)}, u32[]{:S(2)}) collective-permute-start(bf16[512,128]{1,0:T(8,128)(2,1)S(1)} %collective-permute-done.12), channel_id=1, source_target_pairs={{0,1},{1,0},{2,3},{3,2},{4,5},{5,4},{6,7},{7,6},{8,9},{9,8},{10,11... | collective-permute-start | bytes 393224 | tf_op jit(solution)/shard_map/ppermute | solution.py:18
  90.4 6.0 %collective-permute-start.22 = (bf16[512,128]{1,0:T(8,128)(2,1)S(1)}, bf16[512,128]{1,0:T(8,128)(2,1)S(1)}, u32[]{:S(2)}, u32[]{:S(2)}) collective-permute-start(bf16[512,128]{1,0:T(8,128)(2,1)S(1)} %collective-permute-done.14), channel_id=1, source_target_pairs={{0,1},{1,0},{2,3},{3,2},{4,5},{5,4},{6,7},{7,6},{8,9},{9,8},{10,11... | collective-permute-start | bytes 393224 | tf_op jit(solution)/shard_map/ppermute | solution.py:18
  90.5 9.7 %collective-permute-start.27 = (f32[136,256]{1,0:T(8,128)S(1)}, f32[136,256]{1,0:T(8,128)S(1)}, u32[]{:S(2)}, u32[]{:S(2)}) collective-permute-start(f32[136,256]{1,0:T(8,128)S(1)} %add.84), channel_id=1, source_target_pairs={{0,1},{1,0},{2,3},{3,2},{4,5},{5,4},{6,7},{7,6},{8,9},{9,8},{10,11... | collective-permute-start | bytes 417800 | tf_op jit(solution)/shard_map/ppermute | solution.py:18
  (15 other events, 271.0 us)

commit v2 on v1

v2 whole, which is shorter than its diff:
```python
import functools
import math

import jax
import jax.numpy as jnp
from jax import lax
from jax.experimental import pallas as pl
from jax.experimental.pallas import tpu as pltpu
from jax.sharding import PartitionSpec as P

BF16 = jnp.bfloat16
F32 = jnp.float32
GROUP = 8
CHUNKS = 8
MIB = 1 << 20
LIGHT = pl.CostEstimate(flops=0, bytes_accessed=0, transcendentals=0)
HEAVY = pl.CostEstimate(flops=20_000_000_000, bytes_accessed=0, transcendentals=0)


def swap(value, bits, devices):
    return lax.ppermute(value, "row", [(i, i ^ bits) for i in range(devices)])


def build(nb, group, split, dest_ref, src_ref, dst_ref, pat_hbm, buf, adj, sems):
    step = pl.program_id(0)
    tiles = dest_ref.shape[0]
    per_unit = nb * nb
    chunks = sems.shape[0]
    size = tiles // chunks
    me = lax.axis_index("row")

    def fetch(c):
        part = pl.ds(c * size, size)
        return pltpu.make_async_copy(pat_hbm.at[part], buf.at[part], sems.at[c])

    @pl.when(step == 0)
    def _():
        for c in range(chunks):
            fetch(c).start()

    def clear(i, carry):
        adj[pl.ds(i * per_unit, per_unit)] = jnp.zeros((per_unit,) + adj.shape[1:], BF16)
        return carry

    lax.fori_loop(0, group, clear, 0)
    for c in range(chunks):

        @pl.when(step == 0)
        def _(c=c):
            fetch(c).wait()

        def add(i, carry, c=c):
            t = c * size + i
            unit = dest_ref[t] ^ me
            place = ((unit - step * group) * nb + dst_ref[t]) * nb + src_ref[t]

            def store():
                adj[place] += buf[t].astype(F32).astype(BF16)

            if split:
                pl.when((place >= 0) & (place < group * per_unit))(store)
            else:
                store()
            return carry

        lax.fori_loop(0, size, add, 0)


def forward_kernel(
    nb, group, split, dest_ref, src_ref, dst_ref, x_hbm, pat_hbm, odd_ref, even_ref, *scratch
):
    x_vmem, buf, adj, sems, x_sem = scratch
    tile = adj.shape[1]
    rows = x_vmem.shape[0]

    copy = pltpu.make_async_copy(x_hbm, x_vmem, x_sem)
    copy.start()
    build(nb, group, split, dest_ref, src_ref, dst_ref, pat_hbm, buf, adj, sems)
    copy.wait()
    xt = x_vmem[...].T
    width = 2 if nb % 2 == 0 else 1
    for parity, out_ref in ((1, odd_ref), (0, even_ref)):

        def multiply(m, carry, parity=parity, out_ref=out_ref):
            for k in range(0, nb, width):
                weight = jnp.concatenate(
                    [
                        adj[pl.ds(((2 * m + parity) * nb + k + j) * nb, nb)].reshape(rows, tile)
                        for j in range(width)
                    ],
                    axis=1,
                )
                out_ref[m, :, k * tile : (k + width) * tile] = jnp.dot(
                    xt, weight, preferred_element_type=F32
                ).astype(out_ref.dtype)
            return carry

        lax.fori_loop(0, group // 2, multiply, 0, unroll=True)


def forward_sums(units, own_dtype, tiles_at, features, patterns, nb):
    rows, feat = features.shape
    tiles, tile, _ = patterns.shape
    group = min(2 * GROUP, units)
    any_space = pl.BlockSpec(memory_space=pl.ANY)
    block = pl.BlockSpec((group // 2, feat, rows), lambda g: (g, 0, 0))
    return pl.pallas_call(
        functools.partial(forward_kernel, nb, group, units > group),
        grid=(units // group,),
        in_specs=[pl.BlockSpec(memory_space=pltpu.SMEM)] * 3 + [any_space, any_space],
        out_specs=[block, block],
        scratch_shapes=[
            pltpu.VMEM((rows, feat), BF16),
            pltpu.VMEM((tiles, tile, tile), jnp.int32),
            pltpu.VMEM((group * nb * nb, tile, tile), BF16),
            pltpu.SemaphoreType.DMA((CHUNKS,)),
            pltpu.SemaphoreType.DMA,
        ],
        out_shape=[
            jax.ShapeDtypeStruct((units // 2, feat, rows), BF16),
            jax.ShapeDtypeStruct((units // 2, feat, rows), own_dtype),
        ],
        compiler_params=pltpu.CompilerParams(vmem_limit_bytes=55 * MIB),
        cost_estimate=LIGHT,
        name="forward_sums",
    )(*tiles_at, features, patterns)


def adjacency_kernel(
    nb, group, split, dest_ref, src_ref, dst_ref, pat_hbm, after_hbm, a_hbm, made_ref, *scratch
):
    buf, adj, sems, out_sem = scratch
    made_ref[...] = jnp.zeros(made_ref.shape, F32)
    build(nb, group, split, dest_ref, src_ref, dst_ref, pat_hbm, buf, adj, sems)
    size = group * nb * nb
    out = pltpu.make_async_copy(adj, a_hbm.at[pl.ds(pl.program_id(0) * size, size)], out_sem)
    out.start()
    out.wait()


def adjacency(units, tiles_at, patterns, nb, after):
    tiles, tile, _ = patterns.shape
    group = min(2 * GROUP, units)
    any_space = pl.BlockSpec(memory_space=pl.ANY)
    return pl.pallas_call(
        functools.partial(adjacency_kernel, nb, group, units > group),
        grid=(units // group,),
        in_specs=[pl.BlockSpec(memory_space=pltpu.SMEM)] * 3 + [any_space, any_space],
        out_specs=[any_space, pl.BlockSpec((8, 128), lambda g: (0, 0))],
        scratch_shapes=[
            pltpu.VMEM((tiles, tile, tile), jnp.int32),
            pltpu.VMEM((group * nb * nb, tile, tile), BF16),
            pltpu.SemaphoreType.DMA((CHUNKS,)),
            pltpu.SemaphoreType.DMA,
        ],
        out_shape=[
            jax.ShapeDtypeStruct((units * nb * nb, tile, tile), BF16),
            jax.ShapeDtypeStruct((8, 128), F32),
        ],
        compiler_params=pltpu.CompilerParams(vmem_limit_bytes=20 * MIB),
        cost_estimate=LIGHT,
        name="adjacency",
    )(*tiles_at, patterns, after)


def add_kernel(n, total_ref, *refs):
    total = total_ref[0].astype(F32)
    for r in refs[:n]:
        total += r[0].astype(F32)
    refs[-1][0] = total


def add_first(total, parts, after):
    block = (1,) + total.shape[1:]
    spec = pl.BlockSpec(block, lambda i: (0, 0, 0))
    return pl.pallas_call(
        functools.partial(add_kernel, len(parts)),
        grid=(1,),
        in_specs=[spec] * (1 + len(parts)) + [pl.BlockSpec(memory_space=pl.ANY)],
        out_specs=spec,
        out_shape=jax.ShapeDtypeStruct(block, F32),
        compiler_params=pltpu.CompilerParams(vmem_limit_bytes=8 * MIB),
        cost_estimate=HEAVY,
        name="add_first",
    )(total, *parts, after)


def layer_kernel(n_recv, own_ref, *refs):
    recv = refs[:n_recv]
    (deg_ref, x_ref, cot_ref, ws_ref, wn_ref, bias_ref) = refs[n_recv : n_recv + 6]
    out_ref, delta_ref, aggt_ref, back_ref = refs[n_recv + 6 :]
    total = own_ref[0].astype(F32)
    for r in recv:
        total += r[...].reshape(total.shape).astype(F32)
    degree = 1.0 + deg_ref[...].astype(F32)
    degree = jnp.broadcast_to(degree, total.shape)
    aggt = (total / degree).astype(BF16)
    aggt_ref[...] = aggt
    agg = aggt.T
    pre = (
        jnp.dot(x_ref[...], ws_ref[...], preferred_element_type=F32)
        + jnp.dot(agg, wn_ref[...], preferred_element_type=F32)
        + bias_ref[...]
    )
    sigma = jax.nn.sigmoid(pre)
    out_ref[...] = (pre * sigma).astype(BF16)
    delta = (cot_ref[...].astype(F32) * sigma * (1.0 + pre * (1.0 - sigma))).astype(BF16)
    delta_ref[...] = delta
    back = lax.dot_general(
        delta, wn_ref[...], (((1,), (1,)), ((), ())), preferred_element_type=F32
    )
    back_ref[...] = (back / degree.T).astype(BF16)


def layer(own, recv, in_degree, features, cotangent, w_self, w_neigh, bias):
    rows, feat = features.shape
    hidden = w_self.shape[1]

    def first(a):
        return pl.BlockSpec((1,) + a.shape[1:], lambda i: (0, 0, 0))

    def whole(a):
        return pl.BlockSpec(a.shape, lambda i, n=a.ndim: (0,) * n)

    rest = [in_degree, features, cotangent, w_self, w_neigh, bias]
    return pl.pallas_call(
        functools.partial(layer_kernel, len(recv)),
        grid=(1,),
        in_specs=[first(own)] + [first(r) for r in recv] + [whole(a) for a in rest],
        out_specs=[
            pl.BlockSpec((rows, hidden), lambda i: (0, 0)),
            pl.BlockSpec((rows, hidden), lambda i: (0, 0)),
            pl.BlockSpec((feat, rows), lambda i: (0, 0)),
            pl.BlockSpec((rows, feat), lambda i: (0, 0)),
        ],
        out_shape=[
            jax.ShapeDtypeStruct((rows, hidden), BF16),
            jax.ShapeDtypeStruct((rows, hidden), BF16),
            jax.ShapeDtypeStruct((feat, rows), BF16),
            jax.ShapeDtypeStruct((rows, feat), BF16),
        ],
        compiler_params=pltpu.CompilerParams(vmem_limit_bytes=8 * MIB),
        cost_estimate=LIGHT,
        name="layer",
    )(own, *recv, *rest)


def grad_kernel(scale, me_ref, x_ref, delta_ref, aggt_ref, ws_ref, g_ref, base_ref):
    delta = delta_ref[...]
    feat = x_ref.shape[1]
    gs = jnp.dot(x_ref[...].T, delta, preferred_element_type=F32) * scale
    gn = jnp.dot(aggt_ref[...], delta, preferred_element_type=F32) * scale
    gb = jnp.sum(delta.astype(F32), axis=0, keepdims=True) * scale
    gb = jnp.broadcast_to(gb, (8, gb.shape[1]))
    core = me_ref[0] % 2
    half = feat // 2
    for h in range(2):
        place = core ^ h
        g_ref[place, 0:half] = gs[h * half : (h + 1) * half]
        g_ref[place, half:feat] = gn[h * half : (h + 1) * half]
        g_ref[place, feat : feat + 8] = gb
    base_ref[...] = lax.dot_general(
        delta, ws_ref[...], (((1,), (1,)), ((), ())), preferred_element_type=F32
    )


def grad_terms(scale, me, features, delta, aggt, w_self):
    rows, feat = features.shape
    hidden = delta.shape[1]
    vm = pl.BlockSpec(memory_space=pltpu.VMEM)
    return pl.pallas_call(
        functools.partial(grad_kernel, scale),
        in_specs=[pl.BlockSpec(memory_space=pltpu.SMEM), vm, vm, vm, vm],
        out_specs=[vm, vm],
        out_shape=[
            jax.ShapeDtypeStruct((2, feat + 8, hidden), F32),
            jax.ShapeDtypeStruct((rows, feat), F32),
        ],
        compiler_params=pltpu.CompilerParams(vmem_limit_bytes=8 * MIB),
        cost_estimate=LIGHT,
        name="grad_terms",
    )(me, features, delta, aggt, w_self)


def spread_kernel(places, nb, n_arrays, acc_ref, adj_hbm, *refs):
    backs = refs[:n_arrays]
    out_ref, adj, sems = refs[n_arrays], *refs[-2:]
    per_unit = nb * nb
    copies = []
    for i, place in enumerate(places):
        copy = pltpu.make_async_copy(
            adj_hbm.at[pl.ds(place * per_unit, per_unit)], adj.at[i], sems.at[i]
        )
        copy.start()
        copies.append(copy)
    total = acc_ref[...]
    rows = total.shape[0]
    i = 0
    for back in backs:
        for j in range(back.shape[0]):
            copies[i].wait()
            tile = adj.shape[2]
            left = jnp.concatenate(
                [adj[i, k * nb : (k + 1) * nb].reshape(rows, tile) for k in range(nb)], axis=1
            )
            total += jnp.dot(left, back[j], preferred_element_type=F32)
            i += 1
    out_ref[...] = total.astype(out_ref.dtype)


def finish_kernel(me_ref, mine_ref, theirs_ref, gs_ref, gn_ref, gb_ref):
    feat = gs_ref.shape[0]
    half = feat // 2
    core = me_ref[0] % 2
    for other, ref in ((0, mine_ref), (1, theirs_ref)):
        at = pl.ds(pl.multiple_of((core ^ other) * half, half), half)
        gs_ref[at] = ref[0:half]
        gn_ref[at] = ref[half:feat]
    gb_ref[...] = mine_ref[feat : feat + 1]


def finish(me, mine, theirs):
    vm = pl.BlockSpec(memory_space=pltpu.VMEM)
    rows, hidden = mine.shape
    feat = rows - 8
    return pl.pallas_call(
        finish_kernel,
        in_specs=[pl.BlockSpec(memory_space=pltpu.SMEM), vm, vm],
        out_specs=[vm] * 3,
        out_shape=[
            jax.ShapeDtypeStruct((feat, hidden), F32),
            jax.ShapeDtypeStruct((feat, hidden), F32),
            jax.ShapeDtypeStruct((1, hidden), F32),
        ],
        compiler_params=pltpu.CompilerParams(vmem_limit_bytes=4 * MIB),
        cost_estimate=LIGHT,
        name="finish",
    )(me, mine, theirs)


def spread(acc, adjacency, places, backs, nb, dtype):
    vm = pl.BlockSpec(memory_space=pltpu.VMEM)
    rows, feat = acc.shape
    per_unit = nb * nb
    tile = adjacency.shape[1]
    n = len(places)
    return pl.pallas_call(
        functools.partial(spread_kernel, tuple(places), nb, len(backs)),
        in_specs=[vm, pl.BlockSpec(memory_space=pl.ANY)] + [vm] * len(backs),
        out_specs=vm,
        out_shape=jax.ShapeDtypeStruct((rows, feat), dtype),
        scratch_shapes=[
            pltpu.VMEM((n, per_unit, tile, tile), BF16),
            pltpu.SemaphoreType.DMA((n,)),
        ],
        compiler_params=pltpu.CompilerParams(vmem_limit_bytes=12 * MIB),
        cost_estimate=HEAVY,
        name="spread",
    )(acc, adjacency, *backs)


def tree_sum(values):
    while len(values) > 1:
        values = [values[i] + values[i + 1] for i in range(0, len(values), 2)]
    return values[0]


def stages_of(devices):
    bits = devices.bit_length() - 1
    assert 1 << bits == devices and bits >= 3
    rest = bits - 1
    return rest // 2, rest - rest // 2


def on_device(
    features,
    patterns,
    tile_dest,
    tile_src_block,
    tile_dst_block,
    in_degree,
    w_self,
    w_neigh,
    bias,
    cotangent,
):
    devices = lax.axis_size("row")
    me = lax.axis_index("row")
    tile = patterns.shape[1]
    rows, feat = features.shape
    nb = rows // tile
    y_bits, z_bits = stages_of(devices)
    ny, nz = 1 << y_bits, 1 << z_bits
    units = devices // 2
    small = devices == 16

    tiles_at = (tile_dest.reshape(-1), tile_src_block, tile_dst_block)

    s_other, s_own = forward_sums(devices, F32 if small else BF16, tiles_at, features, patterns, nb)
    s_recv = swap(s_other, 1, devices)

    def chip_sum(m):
        return s_own[m].astype(F32) + s_recv[m].astype(F32)

    if small:
        y_recv = [None] * nz
        sent = None
        for n in reversed(range(nz)):
            y_recv[n] = []
            for k in range(1, ny):
                own, recv = s_own[n * ny + k], s_recv[n * ny + k]
                if sent is not None:
                    own, recv, sent = lax.optimization_barrier((own, recv, sent))
                sent = (own.astype(F32) + recv.astype(F32)).astype(BF16)
                y_recv[n].append(swap(sent, 2 * k, devices))
    else:
        s5 = s_own.reshape(nz, ny, feat, rows)
        r5 = s_recv.reshape(nz, ny, feat, rows)
        got = [
            swap((s5[:, k].astype(F32) + r5[:, k].astype(F32)).astype(BF16), 2 * k, devices)
            for k in range(1, ny)
        ]
        y_recv = [[g[n] for g in got] for n in range(nz)]
    z_recv = {}
    sent = None
    for n in reversed(range(1, nz)):
        arrived = y_recv[n]
        if sent is not None:
            arrived, sent = lax.optimization_barrier((arrived, sent))
        total = chip_sum(n * ny)
        for r in arrived:
            total = total + r.astype(F32)
        sent = total.astype(BF16)
        z_recv[n] = swap(sent, 2 * ny * n, devices)[None]
    adj, made = adjacency(devices, tiles_at, patterns, nb, sent)
    total = add_first(s_own, [s_recv, z_recv[nz - 1]], made)
    for n in reversed(range(2, nz - 1)):
        total = add_first(total, [z_recv[n]], made)

    output, delta, aggt, back = layer(
        total,
        [r[None] for r in y_recv[0]] + [z_recv[1]],
        in_degree.reshape(1, rows),
        features,
        cotangent,
        w_self,
        w_neigh,
        bias.reshape(1, -1),
    )
    me = me.reshape(1).astype(jnp.int32)
    scale = 1.0 / math.sqrt(rows * devices)
    terms, base = grad_terms(scale, me, features, delta, aggt, w_self)

    have = {0: back}
    for n in reversed(range(1, nz)):
        have[n * ny] = swap(back, 2 * ny * n, devices)
    for n in range(nz):
        for k in range(1, ny):
            have[n * ny + k] = swap(have[n * ny], 2 * k, devices)
    if small:
        pairs = [(0, 1), (2, 3), (4, 6), (5, 7)]
    else:
        pairs = [(m,) for m in sorted(have)]
    own = {2 * m: have[m][None] for m in have}
    across = {
        tuple(2 * m + 1 for m in pair): swap(jnp.stack([have[m] for m in pair]), 1, devices)
        for pair in pairs
    }

    half = terms[0] + swap(terms[1], 1, devices)
    half = tree_sum([half] + [swap(half, 2 * k, devices) for k in range(1, ny)])
    rounded = half.astype(BF16)
    half = tree_sum(
        [rounded.astype(F32)]
        + [swap(rounded, 2 * ny * n, devices).astype(F32) for n in range(1, nz)]
    )
    second = swap(half, 1, devices)

    if small:
        groups = [[0], [12, 8, 2, 4], [6, (1, 3)], [14, 10, (5, 7), (9, 13)], [(11, 15)]]
    else:
        singles = list(own) + list(across)
        groups = [singles[at : at + GROUP] for at in range(0, devices, GROUP)]
    grad_feat = base
    for i, group in enumerate(groups):
        dtype = BF16 if i == len(groups) - 1 else F32
        parts = [((u,), own[u]) if u in own else (u, across[u]) for u in group]
        places = [u for us, _ in parts for u in us]
        grad_feat = spread(grad_feat, adj, places, [b for _, b in parts], nb, dtype)
    grad_self, grad_neigh, grad_bias = finish(me, half, second)
    return (output, grad_feat, grad_self, grad_neigh, grad_bias.reshape(-1))


def solution(mesh):
    return jax.shard_map(
        on_device,
        mesh=mesh,
        in_specs=(
            P(("grp", "row"), None),
            P(("grp", "row"), None, None),
            P(("grp", "row"), None),
            P(("grp", "row")),
            P(("grp", "row")),
            P(("grp", "row")),
            P(),
            P(),
            P(),
            P(("grp", "row"), None),
        ),
        out_specs=(
            P(("grp", "row"), None),
            P(("grp", "row"), None),
            P("grp", None),
            P("grp", None),
            P("grp"),
        ),
        check_vma=False,
    )
```

time: 102 us -> 79.5 us (0.78)
  Pallas kernels: 37.1 us -> 21.2 us
  waiting for transfers between devices: 30.5 us -> 23.5 us
  starting transfers between devices: 23.9 us -> 28.3 us
  local copies, waits for them, and re-layouts: 7.26 us -> 3.48 us
    pallas_call x2 -> x5, Pallas kernels: 28.8 us -> 12.6 us  [the longest x1 7.07 us: forward_sums(): pl.pallas_call(functools.partial(forward_kernel, nb, group, units > group...]
    ppermute x28 -> x25, waiting for transfers between devices: 30.5 us -> 23.5 us  [swap(): return lax.ppermute(value, 'row', [(i, i ^ bits) for i in range(devices)])]
    ppermute x28 -> x25, starting transfers between devices: 23.9 us -> 28.3 us  [swap(): return lax.ppermute(value, 'row', [(i, i ^ bits) for i in range(devices)])]
    unnamed x22, local copies, waits for them, and re-layouts: 6.67 us -> 3.44 us
    squeeze x0 -> x1, other arithmetic: none -> 1.42 us  [on_device(): own, recv = (s_own[n * ny + k], s_recv[n * ny + k])]
    concatenate x2 -> x0, other arithmetic: 1.33 us -> none  [the longest x1 0.66 us: on_device(): grad_neigh = jnp.concatenate([low[h:feat], high[h:feat]], axis=0)]
    pallas_call x2 -> x5, Pallas kernels: 6.72 us -> 7.1 us  [spread(): pl.pallas_call(functools.partial(spread_kernel, tuple(places), nb, len(ba...]
  transfers between devices with their start and end apart: 28 -> 25, of which waited for: 14 -> 12; matrix products, arithmetic and copies ran while one was open for 0% -> 1% of each run, Pallas kernels for 18% -> 14%
where the time goes in v2:
time: 79.5 us; the launch traced here: 79.3 us
  starting transfers between devices  28.3 us (36%)
  waiting for transfers between devices  23.5 us (30%)
  Pallas kernels  21.2 us (27%)
  local copies, waits for them, and re-layouts  3.48 us (4%)
  other arithmetic  1.85 us (2%)
  between operations  0.99 us (1%)
    ppermute x25, starting transfers between devices, swap(): return lax.ppermute(value, 'row', [(i, i ^ bits) for i in range(devices)])  28.3 us
    ppermute x25, waiting for transfers between devices, swap(): return lax.ppermute(value, 'row', [(i, i ^ bits) for i in range(devices)])  23.5 us
    pallas_call x5, Pallas kernels, spread(): pl.pallas_call(functools.partial(spread_kernel, tuple(places), nb, len(ba...  7.1 us
    pallas_call x1, Pallas kernels, forward_sums(): pl.pallas_call(functools.partial(forward_kernel, nb, group, units > group...  7.07 us
    pallas_call x1, Pallas kernels, adjacency(): pl.pallas_call(functools.partial(adjacency_kernel, nb, group, units > gro...  4.7 us
    unnamed x22, local copies, waits for them, and re-layouts  3.44 us
  transfers between devices with their start and end apart: 25, of which 12 were waited for; matrix products, arithmetic and copies ran while one was open for 1% of the time, Pallas kernels for 14%

profile of v2, /device:TPU:0, one launch (start us, length us, event | category | flops | bytes accessed | tf_op | source)
XLA Modules:
  0.0 79.3 jit_solution(18051439162846118159)
XLA Ops:
  0.6 7.1 %forward_sums.1 = (bf16[8,128,512]{2,1,0:T(8,128)(2,1)}, f32[8,128,512]{2,1,0:T(8,128)}) custom-call(s32[128]{0:T(128)} %bitcast.66, s32[128]{0:T(128)} %src_ref.3, s32[128]{0:T(128)} %dst_ref.3, bf16[512,128]{1,0:T(8,128)(2,1)} %x_ref.1, s32[128,128,128]{2,1,0:T(8,128)} %pat_hbm.3), custom_call_target="tpu_custom_call" | custom-call | tf_op jit(solution)/shard_map/forward_sums/pallas_call | solution.py:107
  8.2 2.5 %collective-permute-done.refs_0_ = bf16[8,128,512]{2,1,0:T(8,128)(2,1)S(1)} collective-permute-done((bf16[8,128,512]{2,1,0:T(8,128)(2,1)}, bf16[8,128,512]{2,1,0:T(8,128)(2,1)S(1)}, u32[]{:S(2)}, u32[]{:S(2)}) %collective-permute-start) | collective-permute-done | bytes 1048608 | tf_op jit(solution)/shard_map/ppermute | solution.py:21
  12.2 3.0 %collective-permute-start.1 = (bf16[128,512]{1,0:T(8,128)(2,1)S(1)}, bf16[128,512]{1,0:T(8,128)(2,1)S(1)}, u32[]{:S(2)}, u32[]{:S(2)}) collective-permute-start(bf16[128,512]{1,0:T(8,128)(2,1)S(1)} %get-tuple-element.50), channel_id=1, source_target_pairs={{0,2},{1,3},{2,0},{3,1},{4,6},{5,7},{6,4},{7,5},{8,10},{9,11},{10,... | collective-permute-start | bytes 393224 | tf_op jit(solution)/shard_map/ppermute | solution.py:21
  15.3 2.1 %collective-permute-start.3 = (bf16[128,512]{1,0:T(8,128)(2,1)S(1)}, bf16[128,512]{1,0:T(8,128)(2,1)S(1)}, u32[]{:S(2)}, u32[]{:S(2)}) collective-permute-start(bf16[128,512]{1,0:T(8,128)(2,1)S(1)} %add_convert_fusion.1), channel_id=1, source_target_pairs={{0,2},{1,3},{2,0},{3,1},{4,6},{5,7},{6,4},{7,5},{8,10},{9,11},{10,... | collective-permute-start | bytes 393224 | tf_op jit(solution)/shard_map/ppermute | solution.py:21
  17.5 1.9 %collective-permute-done.1 = bf16[128,512]{1,0:T(8,128)(2,1)S(1)} collective-permute-done((bf16[128,512]{1,0:T(8,128)(2,1)S(1)}, bf16[128,512]{1,0:T(8,128)(2,1)S(1)}, u32[]{:S(2)}, u32[]{:S(2)}) %collective-permute-start.1) | collective-permute-done | bytes 131104 | tf_op jit(solution)/shard_map/ppermute | solution.py:21
  19.5 4.2 %collective-permute-start.2 = (bf16[128,512]{1,0:T(8,128)(2,1)S(1)}, bf16[128,512]{1,0:T(8,128)(2,1)S(1)}, u32[]{:S(2)}, u32[]{:S(2)}) collective-permute-start(bf16[128,512]{1,0:T(8,128)(2,1)S(1)} %fusion.2), channel_id=1, source_target_pairs={{0,12},{1,13},{2,14},{3,15},{4,8},{5,9},{6,10},{7,11},{8,4},{9,5},... | collective-permute-start | bytes 393224 | tf_op jit(solution)/shard_map/ppermute | solution.py:21
  23.8 1.7 %collective-permute-start.5 = (bf16[128,512]{1,0:T(8,128)(2,1)S(1)}, bf16[128,512]{1,0:T(8,128)(2,1)S(1)}, u32[]{:S(2)}, u32[]{:S(2)}) collective-permute-start(bf16[128,512]{1,0:T(8,128)(2,1)S(1)} %fusion), channel_id=1, source_target_pairs={{0,8},{1,9},{2,10},{3,11},{4,12},{5,13},{6,14},{7,15},{8,0},{9,1},... | collective-permute-start | bytes 393224 | tf_op jit(solution)/shard_map/ppermute | solution.py:21
  25.6 3.4 %copy-done = s32[128,128,128]{2,1,0:T(8,128)S(1)} copy-done((s32[128,128,128]{2,1,0:T(8,128)S(1)}, s32[128,128,128]{2,1,0:T(8,128)}, u32[]{:S(2)}) %copy-start) | copy-done | bytes 8388632
  29.0 4.7 %adjacency.1 = (bf16[256,128,128]{2,1,0:T(8,128)(2,1)S(1)}, f32[8,128]{1,0:T(8,128)S(1)}) custom-call(s32[128]{0:T(128)S(1)} %bitcast.67, s32[128]{0:T(128)S(1)} %copy-done.8, s32[128]{0:T(128)S(1)} %copy-done.9, s32[128,128,128]{2,1,0:T(8,128)S(1)} %copy-done, bf16[128,512]{1,0:T(8,128)(2,1)S(1)} %fusion.1.after_hbm), custom_call_target="tpu_custom_call" | custom-call | tf_op jit(solution)/shard_map/adjacency/pallas_call | solution.py:145
  33.7 1.7 %collective-permute-start.7 = (bf16[128,512]{1,0:T(8,128)(2,1)S(1)}, bf16[128,512]{1,0:T(8,128)(2,1)S(1)}, u32[]{:S(2)}, u32[]{:S(2)}) collective-permute-start(bf16[128,512]{1,0:T(8,128)(2,1)S(1)} %fusion.1.after_hbm), channel_id=1, source_target_pairs={{0,4},{1,5},{2,6},{3,7},{4,0},{5,1},{6,2},{7,3},{8,12},{9,13},{10,... | collective-permute-start | bytes 393224 | tf_op jit(solution)/shard_map/ppermute | solution.py:21
  35.6 3.1 %collective-permute-done.7 = bf16[128,512]{1,0:T(8,128)(2,1)S(1)} collective-permute-done((bf16[128,512]{1,0:T(8,128)(2,1)S(1)}, bf16[128,512]{1,0:T(8,128)(2,1)S(1)}, u32[]{:S(2)}, u32[]{:S(2)}) %collective-permute-start.7) | collective-permute-done | bytes 131104 | tf_op jit(solution)/shard_map/ppermute | solution.py:21
  40.0 3.7 %collective-permute-start.8 = (bf16[512,128]{1,0:T(8,128)(2,1)S(1)}, bf16[512,128]{1,0:T(8,128)(2,1)S(1)}, u32[]{:S(2)}, u32[]{:S(2)}) collective-permute-start(bf16[512,128]{1,0:T(8,128)(2,1)S(1)} %get-tuple-element.42), channel_id=1, source_target_pairs={{0,12},{1,13},{2,14},{3,15},{4,8},{5,9},{6,10},{7,11},{8,4},{9,5},... | collective-permute-start | bytes 393224 | tf_op jit(solution)/shard_map/ppermute | solution.py:21
  44.3 1.6 %collective-permute-start.10 = (bf16[512,128]{1,0:T(8,128)(2,1)S(1)}, bf16[512,128]{1,0:T(8,128)(2,1)S(1)}, u32[]{:S(2)}, u32[]{:S(2)}) collective-permute-start(bf16[512,128]{1,0:T(8,128)(2,1)S(1)} %get-tuple-element.42), channel_id=1, source_target_pairs={{0,2},{1,3},{2,0},{3,1},{4,6},{5,7},{6,4},{7,5},{8,10},{9,11},{10,... | collective-permute-start | bytes 393224 | tf_op jit(solution)/shard_map/ppermute | solution.py:21
  48.0 4.2 %collective-permute-done.9 = bf16[512,128]{1,0:T(8,128)(2,1)S(1)} collective-permute-done((bf16[512,128]{1,0:T(8,128)(2,1)S(1)}, bf16[512,128]{1,0:T(8,128)(2,1)S(1)}, u32[]{:S(2)}, u32[]{:S(2)}) %collective-permute-start.9) | collective-permute-done | bytes 131104 | tf_op jit(solution)/shard_map/ppermute | solution.py:21
  53.0 1.5 %collective-permute-start.12 = (bf16[512,128]{1,0:T(8,128)(2,1)S(1)}, bf16[512,128]{1,0:T(8,128)(2,1)S(1)}, u32[]{:S(2)}, u32[]{:S(2)}) collective-permute-start(bf16[512,128]{1,0:T(8,128)(2,1)S(1)} %collective-permute-done.11), channel_id=1, source_target_pairs={{0,2},{1,3},{2,0},{3,1},{4,6},{5,7},{6,4},{7,5},{8,10},{9,11},{10,... | collective-permute-start | bytes 393224 | tf_op jit(solution)/shard_map/ppermute | solution.py:21
  55.1 1.6 %spread.6.acc_ref = f32[512,128]{1,0:T(8,128)S(1)} custom-call(f32[512,128]{1,0:T(8,128)S(1)} %spread.5.acc_ref, bf16[256,128,128]{2,1,0:T(8,128)(2,1)S(1)} %get-tuple-element.41.adj_hbm, bf16[1,512,128]{2,1,0:T(8,128)(2,1)S(1)} %bitcast.52, bf16[1,512,128]{2,1,0:T(8,128)(2,1)S(1)} %bitcast.50, bf16[1,512,128]{2,1,0:T(8,128)(2,1)S(1)} %bitcast.64, ...), custom_call_target="tpu_custom_call" | custom-call | flops 20000000000 | tf_op jit(solution)/shard_map/spread/pallas_call | solution.py:347
  56.7 1.6 %collective-permute-start.14 = (bf16[512,128]{1,0:T(8,128)(2,1)S(1)}, bf16[512,128]{1,0:T(8,128)(2,1)S(1)}, u32[]{:S(2)}, u32[]{:S(2)}) collective-permute-start(bf16[512,128]{1,0:T(8,128)(2,1)S(1)} %collective-permute-done.8), channel_id=1, source_target_pairs={{0,2},{1,3},{2,0},{3,1},{4,6},{5,7},{6,4},{7,5},{8,10},{9,11},{10,... | collective-permute-start | bytes 393224 | tf_op jit(solution)/shard_map/ppermute | solution.py:21
  59.3 1.5 %collective-permute-start.15 = (bf16[512,128]{1,0:T(8,128)(2,1)S(1)}, bf16[512,128]{1,0:T(8,128)(2,1)S(1)}, u32[]{:S(2)}, u32[]{:S(2)}) collective-permute-start(bf16[512,128]{1,0:T(8,128)(2,1)S(1)} %collective-permute-done.9), channel_id=1, source_target_pairs={{0,2},{1,3},{2,0},{3,1},{4,6},{5,7},{6,4},{7,5},{8,10},{9,11},{10,... | collective-permute-start | bytes 393224 | tf_op jit(solution)/shard_map/ppermute | solution.py:21
  62.4 2.7 %collective-permute-done.14 = bf16[512,128]{1,0:T(8,128)(2,1)S(1)} collective-permute-done((bf16[512,128]{1,0:T(8,128)(2,1)S(1)}, bf16[512,128]{1,0:T(8,128)(2,1)S(1)}, u32[]{:S(2)}, u32[]{:S(2)}) %collective-permute-start.14) | collective-permute-done | bytes 131104 | tf_op jit(solution)/shard_map/ppermute | solution.py:21
  65.4 1.6 %collective-permute-done.15 = bf16[512,128]{1,0:T(8,128)(2,1)S(1)} collective-permute-done((bf16[512,128]{1,0:T(8,128)(2,1)S(1)}, bf16[512,128]{1,0:T(8,128)(2,1)S(1)}, u32[]{:S(2)}, u32[]{:S(2)}) %collective-permute-start.15) | collective-permute-done | bytes 131104 | tf_op jit(solution)/shard_map/ppermute | solution.py:21
  67.0 2.5 %collective-permute-start.23 = (bf16[136,256]{1,0:T(8,128)(2,1)S(1)}, bf16[136,256]{1,0:T(8,128)(2,1)S(1)}, u32[]{:S(2)}, u32[]{:S(2)}) collective-permute-start(bf16[136,256]{1,0:T(8,128)(2,1)S(1)} %add_convert_fusion.4), channel_id=1, source_target_pairs={{0,12},{1,13},{2,14},{3,15},{4,8},{5,9},{6,10},{7,11},{8,4},{9,5},... | collective-permute-start | bytes 208904 | tf_op jit(solution)/shard_map/ppermute | solution.py:21
  70.6 2.5 %collective-permute-done.23 = bf16[136,256]{1,0:T(8,128)(2,1)S(1)} collective-permute-done((bf16[136,256]{1,0:T(8,128)(2,1)S(1)}, bf16[136,256]{1,0:T(8,128)(2,1)S(1)}, u32[]{:S(2)}, u32[]{:S(2)}) %collective-permute-start.23) | collective-permute-done | bytes 69664 | tf_op jit(solution)/shard_map/ppermute | solution.py:21
  75.4 2.3 %spread.8.acc_ref = f32[512,128]{1,0:T(8,128)S(1)} custom-call(f32[512,128]{1,0:T(8,128)S(1)} %spread.7.acc_ref, bf16[256,128,128]{2,1,0:T(8,128)(2,1)S(1)} %get-tuple-element.41.adj_hbm, bf16[1,512,128]{2,1,0:T(8,128)(2,1)S(1)} %bitcast.54, bf16[1,512,128]{2,1,0:T(8,128)(2,1)S(1)} %bitcast.58, bf16[2,512,128]{2,1,0:T(8,128)(2,1)S(1)} %collective-permute-done.16.refs_2_, ...), custom_call_target="tpu_custom_call" | custom-call | flops 20000000000 | tf_op jit(solution)/shard_map/spread/pallas_call | solution.py:347
  77.7 1.6 %spread.9 = bf16[512,128]{1,0:T(8,128)(2,1)} custom-call(f32[512,128]{1,0:T(8,128)S(1)} %spread.8.acc_ref, bf16[256,128,128]{2,1,0:T(8,128)(2,1)S(1)} %get-tuple-element.41.adj_hbm, bf16[2,512,128]{2,1,0:T(8,128)(2,1)S(1)} %collective-permute-done.18.refs_0_), custom_call_target="tpu_custom_call" | custom-call | flops 20000000000 | tf_op jit(solution)/shard_map/spread/pallas_call | solution.py:347
  (76 shorter events, 13.9 us)
Async XLA Ops:
  7.7 3.0 %collective-permute-start = (bf16[8,128,512]{2,1,0:T(8,128)(2,1)}, bf16[8,128,512]{2,1,0:T(8,128)(2,1)S(1)}, u32[]{:S(2)}, u32[]{:S(2)}) collective-permute-start(bf16[8,128,512]{2,1,0:T(8,128)(2,1)} %get-tuple-element.27), channel_id=1, source_target_pairs={{0,1},{1,0},{2,3},{3,2},{4,5},{5,4},{6,7},{7,6},{8,9},{9,8},{10,11... | collective-permute-start | bytes 3145736 | tf_op jit(solution)/shard_map/ppermute | solution.py:21
  12.2 7.2 %collective-permute-start.1 = (bf16[128,512]{1,0:T(8,128)(2,1)S(1)}, bf16[128,512]{1,0:T(8,128)(2,1)S(1)}, u32[]{:S(2)}, u32[]{:S(2)}) collective-permute-start(bf16[128,512]{1,0:T(8,128)(2,1)S(1)} %get-tuple-element.50), channel_id=1, source_target_pairs={{0,2},{1,3},{2,0},{3,1},{4,6},{5,7},{6,4},{7,5},{8,10},{9,11},{10,... | collective-permute-start | bytes 393224 | tf_op jit(solution)/shard_map/ppermute | solution.py:21
  15.2 8.5 %collective-permute-start.4 = (bf16[128,512]{1,0:T(8,128)(2,1)S(1)}, bf16[128,512]{1,0:T(8,128)(2,1)S(1)}, u32[]{:S(2)}, u32[]{:S(2)}) collective-permute-start(bf16[128,512]{1,0:T(8,128)(2,1)S(1)} %add_convert_fusion.2), channel_id=1, source_target_pairs={{0,2},{1,3},{2,0},{3,1},{4,6},{5,7},{6,4},{7,5},{8,10},{9,11},{10,... | collective-permute-start | bytes 393224 | tf_op jit(solution)/shard_map/ppermute | solution.py:21
  15.3 10.2 %collective-permute-start.3 = (bf16[128,512]{1,0:T(8,128)(2,1)S(1)}, bf16[128,512]{1,0:T(8,128)(2,1)S(1)}, u32[]{:S(2)}, u32[]{:S(2)}) collective-permute-start(bf16[128,512]{1,0:T(8,128)(2,1)S(1)} %add_convert_fusion.1), channel_id=1, source_target_pairs={{0,2},{1,3},{2,0},{3,1},{4,6},{5,7},{6,4},{7,5},{8,10},{9,11},{10,... | collective-permute-start | bytes 393224 | tf_op jit(solution)/shard_map/ppermute | solution.py:21
  17.5 18.1 %collective-permute-start.6 = (bf16[128,512]{1,0:T(8,128)(2,1)S(1)}, bf16[128,512]{1,0:T(8,128)(2,1)S(1)}, u32[]{:S(2)}, u32[]{:S(2)}) collective-permute-start(bf16[128,512]{1,0:T(8,128)(2,1)S(1)} %add_convert_fusion), channel_id=1, source_target_pairs={{0,2},{1,3},{2,0},{3,1},{4,6},{5,7},{6,4},{7,5},{8,10},{9,11},{10,... | collective-permute-start | bytes 393224 | tf_op jit(solution)/shard_map/ppermute | solution.py:21
  19.5 15.9 %collective-permute-start.2 = (bf16[128,512]{1,0:T(8,128)(2,1)S(1)}, bf16[128,512]{1,0:T(8,128)(2,1)S(1)}, u32[]{:S(2)}, u32[]{:S(2)}) collective-permute-start(bf16[128,512]{1,0:T(8,128)(2,1)S(1)} %fusion.2), channel_id=1, source_target_pairs={{0,12},{1,13},{2,14},{3,15},{4,8},{5,9},{6,10},{7,11},{8,4},{9,5},... | collective-permute-start | bytes 393224 | tf_op jit(solution)/shard_map/ppermute | solution.py:21
  23.8 11.7 %collective-permute-start.5 = (bf16[128,512]{1,0:T(8,128)(2,1)S(1)}, bf16[128,512]{1,0:T(8,128)(2,1)S(1)}, u32[]{:S(2)}, u32[]{:S(2)}) collective-permute-start(bf16[128,512]{1,0:T(8,128)(2,1)S(1)} %fusion), channel_id=1, source_target_pairs={{0,8},{1,9},{2,10},{3,11},{4,12},{5,13},{6,14},{7,15},{8,0},{9,1},... | collective-permute-start | bytes 393224 | tf_op jit(solution)/shard_map/ppermute | solution.py:21
  33.7 5.0 %collective-permute-start.7 = (bf16[128,512]{1,0:T(8,128)(2,1)S(1)}, bf16[128,512]{1,0:T(8,128)(2,1)S(1)}, u32[]{:S(2)}, u32[]{:S(2)}) collective-permute-start(bf16[128,512]{1,0:T(8,128)(2,1)S(1)} %fusion.1.after_hbm), channel_id=1, source_target_pairs={{0,4},{1,5},{2,6},{3,7},{4,0},{5,1},{6,2},{7,3},{8,12},{9,13},{10,... | collective-permute-start | bytes 393224 | tf_op jit(solution)/shard_map/ppermute | solution.py:21
  40.0 8.1 %collective-permute-start.8 = (bf16[512,128]{1,0:T(8,128)(2,1)S(1)}, bf16[512,128]{1,0:T(8,128)(2,1)S(1)}, u32[]{:S(2)}, u32[]{:S(2)}) collective-permute-start(bf16[512,128]{1,0:T(8,128)(2,1)S(1)} %get-tuple-element.42), channel_id=1, source_target_pairs={{0,12},{1,13},{2,14},{3,15},{4,8},{5,9},{6,10},{7,11},{8,4},{9,5},... | collective-permute-start | bytes 393224 | tf_op jit(solution)/shard_map/ppermute | solution.py:21
  43.6 8.6 %collective-permute-start.9 = (bf16[512,128]{1,0:T(8,128)(2,1)S(1)}, bf16[512,128]{1,0:T(8,128)(2,1)S(1)}, u32[]{:S(2)}, u32[]{:S(2)}) collective-permute-start(bf16[512,128]{1,0:T(8,128)(2,1)S(1)} %get-tuple-element.42), channel_id=1, source_target_pairs={{0,8},{1,9},{2,10},{3,11},{4,12},{5,13},{6,14},{7,15},{8,0},{9,1},... | collective-permute-start | bytes 393224 | tf_op jit(solution)/shard_map/ppermute | solution.py:21
  43.7 9.3 %collective-permute-start.11 = (bf16[512,128]{1,0:T(8,128)(2,1)S(1)}, bf16[512,128]{1,0:T(8,128)(2,1)S(1)}, u32[]{:S(2)}, u32[]{:S(2)}) collective-permute-start(bf16[512,128]{1,0:T(8,128)(2,1)S(1)} %get-tuple-element.42), channel_id=1, source_target_pairs={{0,4},{1,5},{2,6},{3,7},{4,0},{5,1},{6,2},{7,3},{8,12},{9,13},{10,... | collective-permute-start | bytes 393224 | tf_op jit(solution)/shard_map/ppermute | solution.py:21
  44.3 8.0 %collective-permute-start.10 = (bf16[512,128]{1,0:T(8,128)(2,1)S(1)}, bf16[512,128]{1,0:T(8,128)(2,1)S(1)}, u32[]{:S(2)}, u32[]{:S(2)}) collective-permute-start(bf16[512,128]{1,0:T(8,128)(2,1)S(1)} %get-tuple-element.42), channel_id=1, source_target_pairs={{0,2},{1,3},{2,0},{3,1},{4,6},{5,7},{6,4},{7,5},{8,10},{9,11},{10,... | collective-permute-start | bytes 393224 | tf_op jit(solution)/shard_map/ppermute | solution.py:21
  46.3 8.2 %collective-permute-start.19 = (f32[136,256]{1,0:T(8,128)S(1)}, f32[136,256]{1,0:T(8,128)S(1)}, u32[]{:S(2)}, u32[]{:S(2)}) collective-permute-start(f32[136,256]{1,0:T(8,128)S(1)} %slice_bitcast_fusion.3), channel_id=1, source_target_pairs={{0,1},{1,0},{2,3},{3,2},{4,5},{5,4},{6,7},{7,6},{8,9},{9,8},{10,11... | collective-permute-start | bytes 417800 | tf_op jit(solution)/shard_map/ppermute | solution.py:21
  52.3 23.1 %collective-permute-start.17 = (bf16[2,512,128]{2,1,0:T(8,128)(2,1)S(1)}, bf16[2,512,128]{2,1,0:T(8,128)(2,1)S(1)}, u32[]{:S(2)}, u32[]{:S(2)}) collective-permute-start(bf16[2,512,128]{2,1,0:T(8,128)(2,1)S(1)} %pad_maximum_fusion.2), channel_id=1, source_target_pairs={{0,1},{1,0},{2,3},{3,2},{4,5},{5,4},{6,7},{7,6},{8,9},{9,8},{10,11... | collective-permute-start | bytes 786440 | tf_op jit(solution)/shard_map/ppermute | solution.py:21
  52.4 20.9 %collective-permute-start.13 = (bf16[2,512,128]{2,1,0:T(8,128)(2,1)S(1)}, bf16[2,512,128]{2,1,0:T(8,128)(2,1)S(1)}, u32[]{:S(2)}, u32[]{:S(2)}) collective-permute-start(bf16[2,512,128]{2,1,0:T(8,128)(2,1)S(1)} %pad_maximum_fusion), channel_id=1, source_target_pairs={{0,1},{1,0},{2,3},{3,2},{4,5},{5,4},{6,7},{7,6},{8,9},{9,8},{10,11... | collective-permute-start | bytes 786440 | tf_op jit(solution)/shard_map/ppermute | solution.py:21
  53.0 6.4 %collective-permute-start.12 = (bf16[512,128]{1,0:T(8,128)(2,1)S(1)}, bf16[512,128]{1,0:T(8,128)(2,1)S(1)}, u32[]{:S(2)}, u32[]{:S(2)}) collective-permute-start(bf16[512,128]{1,0:T(8,128)(2,1)S(1)} %collective-permute-done.11), channel_id=1, source_target_pairs={{0,2},{1,3},{2,0},{3,1},{4,6},{5,7},{6,4},{7,5},{8,10},{9,11},{10,... | collective-permute-start | bytes 393224 | tf_op jit(solution)/shard_map/ppermute | solution.py:21
  54.5 7.8 %collective-permute-start.20 = (f32[136,256]{1,0:T(8,128)S(1)}, f32[136,256]{1,0:T(8,128)S(1)}, u32[]{:S(2)}, u32[]{:S(2)}) collective-permute-start(f32[136,256]{1,0:T(8,128)S(1)} %bitcast_add_fusion.3), channel_id=1, source_target_pairs={{0,2},{1,3},{2,0},{3,1},{4,6},{5,7},{6,4},{7,5},{8,10},{9,11},{10,... | collective-permute-start | bytes 417800 | tf_op jit(solution)/shard_map/ppermute | solution.py:21
  56.7 8.4 %collective-permute-start.14 = (bf16[512,128]{1,0:T(8,128)(2,1)S(1)}, bf16[512,128]{1,0:T(8,128)(2,1)S(1)}, u32[]{:S(2)}, u32[]{:S(2)}) collective-permute-start(bf16[512,128]{1,0:T(8,128)(2,1)S(1)} %collective-permute-done.8), channel_id=1, source_target_pairs={{0,2},{1,3},{2,0},{3,1},{4,6},{5,7},{6,4},{7,5},{8,10},{9,11},{10,... | collective-permute-start | bytes 393224 | tf_op jit(solution)/shard_map/ppermute | solution.py:21
  59.3 7.7 %collective-permute-start.15 = (bf16[512,128]{1,0:T(8,128)(2,1)S(1)}, bf16[512,128]{1,0:T(8,128)(2,1)S(1)}, u32[]{:S(2)}, u32[]{:S(2)}) collective-permute-start(bf16[512,128]{1,0:T(8,128)(2,1)S(1)} %collective-permute-done.9), channel_id=1, source_target_pairs={{0,2},{1,3},{2,0},{3,1},{4,6},{5,7},{6,4},{7,5},{8,10},{9,11},{10,... | collective-permute-start | bytes 393224 | tf_op jit(solution)/shard_map/ppermute | solution.py:21
  62.3 7.2 %collective-permute-start.21 = (bf16[136,256]{1,0:T(8,128)(2,1)S(1)}, bf16[136,256]{1,0:T(8,128)(2,1)S(1)}, u32[]{:S(2)}, u32[]{:S(2)}) collective-permute-start(bf16[136,256]{1,0:T(8,128)(2,1)S(1)} %add_convert_fusion.4), channel_id=1, source_target_pairs={{0,4},{1,5},{2,6},{3,7},{4,0},{5,1},{6,2},{7,3},{8,12},{9,13},{10,... | collective-permute-start | bytes 208904 | tf_op jit(solution)/shard_map/ppermute | solution.py:21
  65.1 5.5 %collective-permute-start.22 = (bf16[136,256]{1,0:T(8,128)(2,1)S(1)}, bf16[136,256]{1,0:T(8,128)(2,1)S(1)}, u32[]{:S(2)}, u32[]{:S(2)}) collective-permute-start(bf16[136,256]{1,0:T(8,128)(2,1)S(1)} %add_convert_fusion.4), channel_id=1, source_target_pairs={{0,8},{1,9},{2,10},{3,11},{4,12},{5,13},{6,14},{7,15},{8,0},{9,1},... | collective-permute-start | bytes 208904 | tf_op jit(solution)/shard_map/ppermute | solution.py:21
  67.0 6.1 %collective-permute-start.23 = (bf16[136,256]{1,0:T(8,128)(2,1)S(1)}, bf16[136,256]{1,0:T(8,128)(2,1)S(1)}, u32[]{:S(2)}, u32[]{:S(2)}) collective-permute-start(bf16[136,256]{1,0:T(8,128)(2,1)S(1)} %add_convert_fusion.4), channel_id=1, source_target_pairs={{0,12},{1,13},{2,14},{3,15},{4,8},{5,9},{6,10},{7,11},{8,4},{9,5},... | collective-permute-start | bytes 208904 | tf_op jit(solution)/shard_map/ppermute | solution.py:21
  69.6 8.1 %collective-permute-start.18 = (bf16[2,512,128]{2,1,0:T(8,128)(2,1)S(1)}, bf16[2,512,128]{2,1,0:T(8,128)(2,1)S(1)}, u32[]{:S(2)}, u32[]{:S(2)}) collective-permute-start(bf16[2,512,128]{2,1,0:T(8,128)(2,1)S(1)} %pad_maximum_fusion.3), channel_id=1, source_target_pairs={{0,1},{1,0},{2,3},{3,2},{4,5},{5,4},{6,7},{7,6},{8,9},{9,8},{10,11... | collective-permute-start | bytes 786440 | tf_op jit(solution)/shard_map/ppermute | solution.py:21
  70.6 4.7 %collective-permute-start.16 = (bf16[2,512,128]{2,1,0:T(8,128)(2,1)S(1)}, bf16[2,512,128]{2,1,0:T(8,128)(2,1)S(1)}, u32[]{:S(2)}, u32[]{:S(2)}) collective-permute-start(bf16[2,512,128]{2,1,0:T(8,128)(2,1)S(1)} %pad_maximum_fusion.1), channel_id=1, source_target_pairs={{0,1},{1,0},{2,3},{3,2},{4,5},{5,4},{6,7},{7,6},{8,9},{9,8},{10,11... | collective-permute-start | bytes 786440 | tf_op jit(solution)/shard_map/ppermute | solution.py:21
  (12 other events, 73.0 us)

commit v3 on v2

--- a/solution.py
+++ b/solution.py
@@ -13,6 +13,8 @@
 GROUP = 8
 CHUNKS = 8
 MIB = 1 << 20
+ADJ_LIMIT = 38
+PLAN = {'z': (1, 3, 2), 'y': (3, 2, 1, 0), 'parts': (), 'token': 0, 'after': 4, 'adj': 1, 'ysep': 1, 'agz': (3, 2, 1), 'groups': ((0,), (12, 4, 2, 8), (6, (1,), (3,), (5,)), (14, 10, (13,), (9,), (7,)), ((15,), (11,))), 'heavy': (1, 1, 1, 1, 1), 'pairs': ((0,), (2,), (4,), (6,), (8,), (12,), (10,), (14,)), 'terms': None, 'gy': None, 'gz': None, 'butter': 0, 'fin': 1, 'ph': 0, 'findep': 0, 'gyb': 1, 'direct': (1,), 'yfs': 0, 'agd': (1,), 'dsep': 0}
 LIGHT = pl.CostEstimate(flops=0, bytes_accessed=0, transcendentals=0)
 HEAVY = pl.CostEstimate(flops=20_000_000_000, bytes_accessed=0, transcendentals=0)
 
@@ -67,21 +69,22 @@
 
 
 def forward_kernel(
-    nb, group, split, dest_ref, src_ref, dst_ref, x_hbm, pat_hbm, odd_ref, even_ref, *scratch
+    nb, group, split, dest_ref, src_ref, dst_ref, x_hbm, pat_hbm, odd_hbm, even_hbm, *scratch
 ):
-    x_vmem, buf, adj, sems, x_sem = scratch
+    x_vmem, buf, adj, odd, even, sems, x_sem, out_sems = scratch
     tile = adj.shape[1]
     rows = x_vmem.shape[0]
-
     copy = pltpu.make_async_copy(x_hbm, x_vmem, x_sem)
     copy.start()
     build(nb, group, split, dest_ref, src_ref, dst_ref, pat_hbm, buf, adj, sems)
     copy.wait()
     xt = x_vmem[...].T
     width = 2 if nb % 2 == 0 else 1
-    for parity, out_ref in ((1, odd_ref), (0, even_ref)):
-
-        def multiply(m, carry, parity=parity, out_ref=out_ref):
+    half = group // 2
+    step = pl.program_id(0)
+    outs = []
+    for parity, sums, out_hbm in ((1, odd, odd_hbm), (0, even, even_hbm)):
+        for m in range(half):
             for k in range(0, nb, width):
                 weight = jnp.concatenate(
                     [
@@ -90,12 +93,21 @@
                     ],
                     axis=1,
                 )
-                out_ref[m, :, k * tile : (k + width) * tile] = jnp.dot(
+                sums[m, :, k * tile : (k + width) * tile] = jnp.dot(
                     xt, weight, preferred_element_type=F32
-                ).astype(out_ref.dtype)
-            return carry
-
-        lax.fori_loop(0, group // 2, multiply, 0, unroll=True)
+                ).astype(sums.dtype)
+            if m % 2 == 1 or m == half - 1:
+                first = m - m % 2
+                part = pl.ds(first, m + 1 - first)
+                out = pltpu.make_async_copy(
+                    sums.at[part],
+                    out_hbm.at[pl.ds(step * half + first, m + 1 - first)],
+                    out_sems.at[parity, m // 2],
+                )
+                out.start()
+                outs.append(out)
+    for out in outs:
+        out.wait()
 
 
 def forward_sums(units, own_dtype, tiles_at, features, patterns, nb):
@@ -103,18 +115,20 @@
     tiles, tile, _ = patterns.shape
     group = min(2 * GROUP, units)
     any_space = pl.BlockSpec(memory_space=pl.ANY)
-    block = pl.BlockSpec((group // 2, feat, rows), lambda g: (g, 0, 0))
     return pl.pallas_call(
         functools.partial(forward_kernel, nb, group, units > group),
         grid=(units // group,),
         in_specs=[pl.BlockSpec(memory_space=pltpu.SMEM)] * 3 + [any_space, any_space],
-        out_specs=[block, block],
+        out_specs=[any_space, any_space],
         scratch_shapes=[
             pltpu.VMEM((rows, feat), BF16),
             pltpu.VMEM((tiles, tile, tile), jnp.int32),
             pltpu.VMEM((group * nb * nb, tile, tile), BF16),
+            pltpu.VMEM((group // 2, feat, rows), BF16),
+            pltpu.VMEM((group // 2, feat, rows), own_dtype),
             pltpu.SemaphoreType.DMA((CHUNKS,)),
             pltpu.SemaphoreType.DMA,
+            pltpu.SemaphoreType.DMA((2, -(-group // 4))),
         ],
         out_shape=[
             jax.ShapeDtypeStruct((units // 2, feat, rows), BF16),
@@ -127,38 +141,37 @@
 
 
 def adjacency_kernel(
-    nb, group, split, dest_ref, src_ref, dst_ref, pat_hbm, after_hbm, a_hbm, made_ref, *scratch
+    nb, group, split, dest_ref, src_ref, dst_ref, pat_hbm, after_hbm, adj, made_ref, *scratch
 ):
-    buf, adj, sems, out_sem = scratch
+    buf, sems = scratch
     made_ref[...] = jnp.zeros(made_ref.shape, F32)
     build(nb, group, split, dest_ref, src_ref, dst_ref, pat_hbm, buf, adj, sems)
-    size = group * nb * nb
-    out = pltpu.make_async_copy(adj, a_hbm.at[pl.ds(pl.program_id(0) * size, size)], out_sem)
-    out.start()
-    out.wait()
 
 
 def adjacency(units, tiles_at, patterns, nb, after):
     tiles, tile, _ = patterns.shape
     group = min(2 * GROUP, units)
     any_space = pl.BlockSpec(memory_space=pl.ANY)
+    blocks = group * nb * nb
+    if units > group:
+        out_spec = pl.BlockSpec((blocks, tile, tile), lambda g: (g, 0, 0))
+    else:
+        out_spec = pl.BlockSpec(memory_space=pltpu.VMEM)
     return pl.pallas_call(
         functools.partial(adjacency_kernel, nb, group, units > group),
         grid=(units // group,),
         in_specs=[pl.BlockSpec(memory_space=pltpu.SMEM)] * 3 + [any_space, any_space],
-        out_specs=[any_space, pl.BlockSpec((8, 128), lambda g: (0, 0))],
+        out_specs=[out_spec, pl.BlockSpec((8, 128), lambda g: (0, 0))],
         scratch_shapes=[
             pltpu.VMEM((tiles, tile, tile), jnp.int32),
-            pltpu.VMEM((group * nb * nb, tile, tile), BF16),
             pltpu.SemaphoreType.DMA((CHUNKS,)),
-            pltpu.SemaphoreType.DMA,
         ],
         out_shape=[
             jax.ShapeDtypeStruct((units * nb * nb, tile, tile), BF16),
             jax.ShapeDtypeStruct((8, 128), F32),
         ],
-        compiler_params=pltpu.CompilerParams(vmem_limit_bytes=20 * MIB),
-        cost_estimate=LIGHT,
+        compiler_params=pltpu.CompilerParams(vmem_limit_bytes=ADJ_LIMIT * MIB),
+        cost_estimate=HEAVY if PLAN["adj"] else LIGHT,
         name="adjacency",
     )(*tiles_at, patterns, after)
 
@@ -180,7 +193,7 @@
         out_specs=spec,
         out_shape=jax.ShapeDtypeStruct(block, F32),
         compiler_params=pltpu.CompilerParams(vmem_limit_bytes=8 * MIB),
-        cost_estimate=HEAVY,
+        cost_estimate=HEAVY if PLAN["ph"] else LIGHT,
         name="add_first",
     )(total, *parts, after)
 
@@ -308,7 +321,8 @@
     out_ref[...] = total.astype(out_ref.dtype)
 
 
-def finish_kernel(me_ref, mine_ref, theirs_ref, gs_ref, gn_ref, gb_ref):
+def finish_kernel(me_ref, mine_ref, theirs_ref, *refs):
+    gs_ref, gn_ref, gb_ref = refs[-3:]
     feat = gs_ref.shape[0]
     half = feat // 2
     core = me_ref[0] % 2
@@ -319,13 +333,14 @@
     gb_ref[...] = mine_ref[feat : feat + 1]
 
 
-def finish(me, mine, theirs):
+def finish(me, mine, theirs, after):
     vm = pl.BlockSpec(memory_space=pltpu.VMEM)
     rows, hidden = mine.shape
     feat = rows - 8
     return pl.pallas_call(
         finish_kernel,
-        in_specs=[pl.BlockSpec(memory_space=pltpu.SMEM), vm, vm],
+        in_specs=[pl.BlockSpec(memory_space=pltpu.SMEM), vm, vm]
+        + [pl.BlockSpec(memory_space=pl.ANY)] * len(after),
         out_specs=[vm] * 3,
         out_shape=[
             jax.ShapeDtypeStruct((feat, hidden), F32),
@@ -335,28 +350,48 @@
         compiler_params=pltpu.CompilerParams(vmem_limit_bytes=4 * MIB),
         cost_estimate=LIGHT,
         name="finish",
-    )(me, mine, theirs)
-
-
-def spread(acc, adjacency, places, backs, nb, dtype):
+    )(me, mine, theirs, *after)
+
+
+def last_kernel(places, nb, n_arrays, me_ref, mine_ref, theirs_ref, acc_ref, adj_hbm, *refs):
+    backs, out_ref, grads, scratch = refs[:n_arrays], refs[n_arrays], refs[-5:-2], refs[-2:]
+    finish_kernel(me_ref, mine_ref, theirs_ref, *grads)
+    spread_kernel(places, nb, n_arrays, acc_ref, adj_hbm, *backs, out_ref, *scratch)
+
+
+def spread(acc, adjacency, places, backs, nb, dtype, heavy=True, grads=None):
     vm = pl.BlockSpec(memory_space=pltpu.VMEM)
     rows, feat = acc.shape
     per_unit = nb * nb
     tile = adjacency.shape[1]
     n = len(places)
+    in_specs = [vm, pl.BlockSpec(memory_space=pl.ANY)] + [vm] * len(backs)
+    inputs = [acc, adjacency, *backs]
+    kernel, out_shape = spread_kernel, jax.ShapeDtypeStruct((rows, feat), dtype)
+    if grads is not None:
+        in_specs = [pl.BlockSpec(memory_space=pltpu.SMEM), vm, vm] + in_specs
+        inputs = [*grads, *inputs]
+        hidden = grads[1].shape[1]
+        kernel = last_kernel
+        out_shape = [
+            out_shape,
+            jax.ShapeDtypeStruct((feat, hidden), F32),
+            jax.ShapeDtypeStruct((feat, hidden), F32),
+            jax.ShapeDtypeStruct((1, hidden), F32),
+        ]
     return pl.pallas_call(
-        functools.partial(spread_kernel, tuple(places), nb, len(backs)),
-        in_specs=[vm, pl.BlockSpec(memory_space=pl.ANY)] + [vm] * len(backs),
-        out_specs=vm,
-        out_shape=jax.ShapeDtypeStruct((rows, feat), dtype),
+        functools.partial(kernel, tuple(places), nb, len(backs)),
+        in_specs=in_specs,
+        out_specs=jax.tree.map(lambda _: vm, out_shape),
+        out_shape=out_shape,
         scratch_shapes=[
             pltpu.VMEM((n, per_unit, tile, tile), BF16),
             pltpu.SemaphoreType.DMA((n,)),
         ],
         compiler_params=pltpu.CompilerParams(vmem_limit_bytes=12 * MIB),
-        cost_estimate=HEAVY,
+        cost_estimate=HEAVY if heavy else LIGHT,
         name="spread",
-    )(acc, adjacency, *backs)
+    )(*inputs)
 
 
 def tree_sum(values):
@@ -405,11 +440,13 @@
     if small:
         y_recv = [None] * nz
         sent = None
-        for n in reversed(range(nz)):
+        for n in PLAN["y"]:
             y_recv[n] = []
+            if n in PLAN["direct"]:
+                continue
             for k in range(1, ny):
                 own, recv = s_own[n * ny + k], s_recv[n * ny + k]
-                if sent is not None:
+                if sent is not None and PLAN["ysep"]:
                     own, recv, sent = lax.optimization_barrier((own, recv, sent))
                 sent = (own.astype(F32) + recv.astype(F32)).astype(BF16)
                 y_recv[n].append(swap(sent, 2 * k, devices))
@@ -423,23 +460,45 @@
         y_recv = [[g[n] for g in got] for n in range(nz)]
     z_recv = {}
     sent = None
-    for n in reversed(range(1, nz)):
+    sums, first_sent, sent = {}, sent if small else None, None
+    for n in PLAN["z"] if small else reversed(range(1, nz)):
         arrived = y_recv[n]
+        if small and n in PLAN["direct"]:
+            for k in range(ny):
+                m = n * ny + k
+                mine, recv, sent = s_own[m], s_recv[m], first_sent
+                if PLAN["dsep"]:
+                    mine, recv, sent = lax.optimization_barrier((mine, recv, sent))
+                direct = (mine.astype(F32) + recv.astype(F32)).astype(BF16)
+                z_recv[m / ny] = swap(direct, 2 * m, devices)[None]
+            continue
         if sent is not None:
             arrived, sent = lax.optimization_barrier((arrived, sent))
         total = chip_sum(n * ny)
         for r in arrived:
             total = total + r.astype(F32)
-        sent = total.astype(BF16)
+        sums[n] = sent = total.astype(BF16)
         z_recv[n] = swap(sent, 2 * ny * n, devices)[None]
-    adj, made = adjacency(devices, tiles_at, patterns, nb, sent)
-    total = add_first(s_own, [s_recv, z_recv[nz - 1]], made)
-    for n in reversed(range(2, nz - 1)):
-        total = add_first(total, [z_recv[n]], made)
+    after = PLAN["after"] if small else 1
+    made = s_recv
+    if after == 4:
+        adj, made = adjacency(devices, tiles_at, patterns, nb, z_recv[3])
+        in_degree, made = lax.optimization_barrier((in_degree, made))
+    elif after:
+        adj, made = adjacency(devices, tiles_at, patterns, nb, sums[after])
+    total, summed = s_own, ()
+    parts = PLAN["parts"] if small else [(n,) for n in range(2, nz)]
+    for i, part in enumerate(parts):
+        extra = [s_recv] if i == 0 else []
+        total = add_first(total, extra + [z_recv[n] for n in part], made)
+        summed += part
+    if not parts:
+        summed = ()
+    rest = [z_recv[n] for n in z_recv if n not in summed]
 
     output, delta, aggt, back = layer(
         total,
-        [r[None] for r in y_recv[0]] + [z_recv[1]],
+        ([s_recv] if not parts else []) + [r[None] for r in y_recv[0]] + rest,
         in_degree.reshape(1, rows),
         features,
         cotangent,
@@ -447,47 +506,95 @@
         w_neigh,
         bias.reshape(1, -1),
     )
+    if not after:
+        adj, made = adjacency(devices, tiles_at, patterns, nb, back)
     me = me.reshape(1).astype(jnp.int32)
     scale = 1.0 / math.sqrt(rows * devices)
     terms, base = grad_terms(scale, me, features, delta, aggt, w_self)
 
     have = {0: back}
-    for n in reversed(range(1, nz)):
+    for n in PLAN["agz"] if small else range(1, nz):
         have[n * ny] = swap(back, 2 * ny * n, devices)
+    own = {0: back[None]}
+    onward = []
     for n in range(nz):
+        own[2 * n * ny] = have[n * ny][None]
         for k in range(1, ny):
-            have[n * ny + k] = swap(have[n * ny], 2 * k, devices)
+            m = n * ny + k
+            if small and n in PLAN["agd"]:
+                own[2 * m] = swap(back, 2 * m, devices)[None]
+            elif small and PLAN["yfs"] and n > 0:
+                onward.append(n)
+            else:
+                own[2 * m] = swap(have[n * ny], 2 * k, devices)[None]
+    if onward:
+        key = tuple(2 * n * ny + 2 for n in onward)
+        own[key] = swap(jnp.stack([have[n * ny] for n in onward]), 2, devices)
+
+    def plus_one(key):
+        return tuple(u + 1 for u in key) if isinstance(key, tuple) else (key + 1,)
+
+    across = {}
+    for keys in PLAN["pairs"] if small else [(key,) for key in own]:
+        name = sum((plus_one(key) for key in keys), ())
+        parts = [own[key] for key in keys]
+        whole = jnp.concatenate(parts, axis=0) if len(parts) > 1 else parts[0]
+        across[name] = swap(whole, 1, devices)
+
+    def later(value, what):
+        key = PLAN[what]
+        if key is None or not small:
+            return value
+        value, own[key] = lax.optimization_barrier((value, own[key]))
+        return value
+
+    terms = later(terms, "terms")
+    half = terms[0] + swap(terms[1], 1, devices)
+    half = later(half, "gy")
+    if PLAN["gyb"]:
+        half = half.astype(BF16)
+    half = tree_sum(
+        [half.astype(F32)] + [swap(half, 2 * k, devices).astype(F32) for k in range(1, ny)]
+    )
+    half = later(half, "gz")
+    if PLAN["butter"] and small:
+        for n in (1, 2):
+            rounded = half.astype(BF16)
+            half = rounded.astype(F32) + swap(rounded, 2 * ny * n, devices).astype(F32)
+    else:
+        rounded = half.astype(BF16)
+        half = tree_sum(
+            [rounded.astype(F32)]
+            + [swap(rounded, 2 * ny * n, devices).astype(F32) for n in range(1, nz)]
+        )
+    second = swap(half, 1, devices)
+
     if small:
-        pairs = [(0, 1), (2, 3), (4, 6), (5, 7)]
-    else:
-        pairs = [(m,) for m in sorted(have)]
-    own = {2 * m: have[m][None] for m in have}
-    across = {
-        tuple(2 * m + 1 for m in pair): swap(jnp.stack([have[m] for m in pair]), 1, devices)
-        for pair in pairs
-    }
-
-    half = terms[0] + swap(terms[1], 1, devices)
-    half = tree_sum([half] + [swap(half, 2 * k, devices) for k in range(1, ny)])
-    rounded = half.astype(BF16)
-    half = tree_sum(
-        [rounded.astype(F32)]
-        + [swap(rounded, 2 * ny * n, devices).astype(F32) for n in range(1, nz)]
-    )
-    second = swap(half, 1, devices)
-
-    if small:
-        groups = [[0], [12, 8, 2, 4], [6, (1, 3)], [14, 10, (5, 7), (9, 13)], [(11, 15)]]
+        groups, heavy = PLAN["groups"], PLAN["heavy"]
     else:
         singles = list(own) + list(across)
         groups = [singles[at : at + GROUP] for at in range(0, devices, GROUP)]
+        heavy = [1] * len(groups)
     grad_feat = base
     for i, group in enumerate(groups):
-        dtype = BF16 if i == len(groups) - 1 else F32
-        parts = [((u,), own[u]) if u in own else (u, across[u]) for u in group]
+        last = i == len(groups) - 1
+        parts = [(u, own[u]) if u in own else (u, across[u]) for u in group]
+        parts = [(u if isinstance(u, tuple) else (u,), b) for u, b in parts]
         places = [u for us, _ in parts for u in us]
-        grad_feat = spread(grad_feat, adj, places, [b for _, b in parts], nb, dtype)
-    grad_self, grad_neigh, grad_bias = finish(me, half, second)
+        grad_feat = spread(
+            grad_feat,
+            adj,
+            places,
+            [b for _, b in parts],
+            nb,
+            BF16 if last else F32,
+            heavy[i],
+            (me, half, second) if last and PLAN["fin"] else None,
+        )
+    if PLAN["fin"]:
+        grad_feat, grad_self, grad_neigh, grad_bias = grad_feat
+    else:
+        grad_self, grad_neigh, grad_bias = finish(me, half, second, [grad_feat] if PLAN["findep"] else [])
     return (output, grad_feat, grad_self, grad_neigh, grad_bias.reshape(-1))
 
 

time: 79.5 us -> 68.1 us (0.86)
  waiting for transfers between devices: 23.5 us -> 14.6 us
  local copies, waits for them, and re-layouts: 3.48 us -> 0.09 us
  starting transfers between devices: 28.3 us -> 30.2 us
  Pallas kernels: 21.2 us -> 20.2 us
    ppermute x25 -> x29, waiting for transfers between devices: 23.5 us -> 14.6 us  [swap(): return lax.ppermute(value, 'row', [(i, i ^ bits) for i in range(devices)])]
    unnamed x22 -> x20, local copies, waits for them, and re-layouts: 3.44 us -> 0.06 us
    ppermute x25 -> x29, starting transfers between devices: 28.3 us -> 30.2 us  [swap(): return lax.ppermute(value, 'row', [(i, i ^ bits) for i in range(devices)])]
    convert_element_type x3 -> x4, other arithmetic: 0.15 us -> 1.69 us  [the longest x1 1.59 us: on_device(): direct = (mine.astype(F32) + recv.astype(F32)).astype(BF16)]
    squeeze x1 -> x0, other arithmetic: 1.42 us -> none  [on_device(): own, recv = (s_own[n * ny + k], s_recv[n * ny + k])]
    pallas_call x8 -> x5, Pallas kernels: 7.9 us -> 7.14 us  [spread(): pl.pallas_call(functools.partial(kernel, tuple(places), nb, len(backs)),...]
  transfers between devices with their start and end apart: 25 -> 29, of which waited for: 12 -> 9; matrix products, arithmetic and copies ran while one was open for 1% -> 0% of each run, Pallas kernels for 14% -> 16%
where the time goes in v3:
time: 68.1 us; the launch traced here: 67.9 us
  starting transfers between devices  30.2 us (44%)
  Pallas kernels  20.2 us (30%)
  waiting for transfers between devices  14.6 us (21%)
  other arithmetic  1.81 us (3%)
  between operations  1.01 us (1%)
    ppermute x29, starting transfers between devices, swap(): return lax.ppermute(value, 'row', [(i, i ^ bits) for i in range(devices)])  30.2 us
    ppermute x29, waiting for transfers between devices, swap(): return lax.ppermute(value, 'row', [(i, i ^ bits) for i in range(devices)])  14.6 us
    pallas_call x5, Pallas kernels, spread(): pl.pallas_call(functools.partial(kernel, tuple(places), nb, len(backs)),...  7.14 us
    pallas_call x1, Pallas kernels, forward_sums(): pl.pallas_call(functools.partial(forward_kernel, nb, group, units > group...  6.72 us
    pallas_call x1, Pallas kernels, adjacency(): pl.pallas_call(functools.partial(adjacency_kernel, nb, group, units > gro...  4.83 us
    convert_element_type x1, other arithmetic, on_device(): direct = (mine.astype(F32) + recv.astype(F32)).astype(BF16)  1.59 us
  transfers between devices with their start and end apart: 29, of which 9 were waited for; matrix products, arithmetic and copies ran while one was open for 0% of the time, Pallas kernels for 16%

profile of v3, /device:TPU:0, one launch (start us, length us, event | category | flops | bytes accessed | tf_op | source)
XLA Modules:
  0.0 67.9 jit_solution(1042215281365471543)
XLA Ops:
  0.6 6.7 %forward_sums.1 = (bf16[8,128,512]{2,1,0:T(8,128)(2,1)}, f32[8,128,512]{2,1,0:T(8,128)}) custom-call(s32[128]{0:T(128)} %bitcast.54, s32[128]{0:T(128)} %src_ref.3, s32[128]{0:T(128)} %dst_ref.3, bf16[512,128]{1,0:T(8,128)(2,1)} %x_ref.1, s32[128,128,128]{2,1,0:T(8,128)} %pat_hbm.3), custom_call_target="tpu_custom_call" | custom-call | tf_op jit(solution)/shard_map/forward_sums/pallas_call | solution.py:118
  7.9 2.5 %collective-permute-done.refs_0_ = bf16[8,128,512]{2,1,0:T(8,128)(2,1)S(1)} collective-permute-done((bf16[8,128,512]{2,1,0:T(8,128)(2,1)}, bf16[8,128,512]{2,1,0:T(8,128)(2,1)S(1)}, u32[]{:S(2)}, u32[]{:S(2)}) %collective-permute-start) | collective-permute-done | bytes 1048608 | tf_op jit(solution)/shard_map/ppermute | solution.py:23
  10.4 1.6 %fusion.5 = (bf16[128,512]{1,0:T(8,128)(2,1)S(1)}, bf16[128,512]{1,0:T(8,128)(2,1)S(1)}, bf16[128,512]{1,0:T(8,128)(2,1)S(1)}, f32[128,512]{1,0:T(8,128)S(1)}, f32[128,512]{1,0:T(8,128)S(1)}) fusion(f32[8,128,512]{2,1,0:T(8,128)} %get-tuple-element.23.own_ref, bf16[8,128,512]{2,1,0:T(8,128)(2,1)S(1)} %collective-permute-done.refs_0_), kind=kLoop, calls=%fused_computation.18 | loop fusion | flops 589824 | bytes 2621440 | tf_op jit(solution)/shard_map/convert_element_type | solution.py:472
  12.0 3.0 %collective-permute-start.4 = (bf16[128,512]{1,0:T(8,128)(2,1)S(1)}, bf16[128,512]{1,0:T(8,128)(2,1)S(1)}, u32[]{:S(2)}, u32[]{:S(2)}) collective-permute-start(bf16[128,512]{1,0:T(8,128)(2,1)S(1)} %get-tuple-element.43), channel_id=1, source_target_pairs={{0,2},{1,3},{2,0},{3,1},{4,6},{5,7},{6,4},{7,5},{8,10},{9,11},{10,... | collective-permute-start | bytes 393224 | tf_op jit(solution)/shard_map/ppermute | solution.py:23
  15.1 2.1 %collective-permute-start.1 = (bf16[128,512]{1,0:T(8,128)(2,1)S(1)}, bf16[128,512]{1,0:T(8,128)(2,1)S(1)}, u32[]{:S(2)}, u32[]{:S(2)}) collective-permute-start(bf16[128,512]{1,0:T(8,128)(2,1)S(1)} %add_convert_fusion.2), channel_id=1, source_target_pairs={{0,2},{1,3},{2,0},{3,1},{4,6},{5,7},{6,4},{7,5},{8,10},{9,11},{10,... | collective-permute-start | bytes 393224 | tf_op jit(solution)/shard_map/ppermute | solution.py:23
  17.2 1.6 %collective-permute-start.2 = (bf16[128,512]{1,0:T(8,128)(2,1)S(1)}, bf16[128,512]{1,0:T(8,128)(2,1)S(1)}, u32[]{:S(2)}, u32[]{:S(2)}) collective-permute-start(bf16[128,512]{1,0:T(8,128)(2,1)S(1)} %get-tuple-element.42), channel_id=1, source_target_pairs={{0,4},{1,5},{2,6},{3,7},{4,0},{5,1},{6,2},{7,3},{8,12},{9,13},{10,... | collective-permute-start | bytes 393224 | tf_op jit(solution)/shard_map/ppermute | solution.py:23
  19.3 4.2 %collective-permute-start.5 = (bf16[128,512]{1,0:T(8,128)(2,1)S(1)}, bf16[128,512]{1,0:T(8,128)(2,1)S(1)}, u32[]{:S(2)}, u32[]{:S(2)}) collective-permute-start(bf16[128,512]{1,0:T(8,128)(2,1)S(1)} %fusion.1), channel_id=1, source_target_pairs={{0,12},{1,13},{2,14},{3,15},{4,8},{5,9},{6,10},{7,11},{8,4},{9,5},... | collective-permute-start | bytes 393224 | tf_op jit(solution)/shard_map/ppermute | solution.py:23
  23.5 1.4 %collective-permute-done.6 = bf16[128,512]{1,0:T(8,128)(2,1)S(1)} collective-permute-done((bf16[128,512]{1,0:T(8,128)(2,1)S(1)}, bf16[128,512]{1,0:T(8,128)(2,1)S(1)}, u32[]{:S(2)}, u32[]{:S(2)}) %collective-permute-start.6) | collective-permute-done | bytes 131104 | tf_op jit(solution)/shard_map/ppermute | solution.py:23
  24.9 2.5 %collective-permute-start.7 = (bf16[128,512]{1,0:T(8,128)(2,1)S(1)}, bf16[128,512]{1,0:T(8,128)(2,1)S(1)}, u32[]{:S(2)}, u32[]{:S(2)}) collective-permute-start(bf16[128,512]{1,0:T(8,128)(2,1)S(1)} %fusion), channel_id=1, source_target_pairs={{0,8},{1,9},{2,10},{3,11},{4,12},{5,13},{6,14},{7,15},{8,0},{9,1},... | collective-permute-start | bytes 393224 | tf_op jit(solution)/shard_map/ppermute | solution.py:23
  27.4 3.7 %collective-permute-done.5 = bf16[128,512]{1,0:T(8,128)(2,1)S(1)} collective-permute-done((bf16[128,512]{1,0:T(8,128)(2,1)S(1)}, bf16[128,512]{1,0:T(8,128)(2,1)S(1)}, u32[]{:S(2)}, u32[]{:S(2)}) %collective-permute-start.5) | collective-permute-done | bytes 131104 | tf_op jit(solution)/shard_map/ppermute | solution.py:23
  31.1 4.8 %adjacency.1 = (bf16[256,128,128]{2,1,0:T(8,128)(2,1)S(1)}, f32[8,128]{1,0:T(8,128)}) custom-call(s32[128]{0:T(128)S(1)} %bitcast.55, s32[128]{0:T(128)S(1)} %copy-done.8, s32[128]{0:T(128)S(1)} %copy-done.9, s32[128,128,128]{2,1,0:T(8,128)} %pat_hbm.3, bf16[1,128,512]{2,1,0:T(8,128)(2,1)S(1)} %bitcast.49), custom_call_target="tpu_custom_call" | custom-call | flops 20000000000 | tf_op jit(solution)/shard_map/adjacency/pallas_call | solution.py:160
  36.1 1.2 %layer.1 = (bf16[512,256]{1,0:T(8,128)(2,1)}, bf16[512,256]{1,0:T(8,128)(2,1)S(1)}, bf16[128,512]{1,0:T(8,128)(2,1)S(1)}, bf16[512,128]{1,0:T(8,128)(2,1)S(1)}) custom-call(f32[8,128,512]{2,1,0:T(8,128)S(1)} %copy-done, bf16[8,128,512]{2,1,0:T(8,128)(2,1)S(1)} %collective-permute-done.refs_0_, bf16[1,128,512]{2,1,0:T(8,128)(2,1)S(1)} %bitcast.46, ...), custom_call_target="tpu_custom_call" | custom-call | tf_op jit(solution)/shard_map/layer/pallas_call | solution.py:239
  37.3 1.3 %collective-permute-start.14 = (bf16[512,128]{1,0:T(8,128)(2,1)S(1)}, bf16[512,128]{1,0:T(8,128)(2,1)S(1)}, u32[]{:S(2)}, u32[]{:S(2)}) collective-permute-start(bf16[512,128]{1,0:T(8,128)(2,1)S(1)} %get-tuple-element.36), channel_id=1, source_target_pairs={{0,12},{1,13},{2,14},{3,15},{4,8},{5,9},{6,10},{7,11},{8,4},{9,5},... | collective-permute-start | bytes 393224 | tf_op jit(solution)/shard_map/ppermute | solution.py:23
  38.6 3.1 %collective-permute-start.16 = (bf16[512,128]{1,0:T(8,128)(2,1)S(1)}, bf16[512,128]{1,0:T(8,128)(2,1)S(1)}, u32[]{:S(2)}, u32[]{:S(2)}) collective-permute-start(bf16[512,128]{1,0:T(8,128)(2,1)S(1)} %get-tuple-element.36), channel_id=1, source_target_pairs={{0,2},{1,3},{2,0},{3,1},{4,6},{5,7},{6,4},{7,5},{8,10},{9,11},{10,... | collective-permute-start | bytes 393224 | tf_op jit(solution)/shard_map/ppermute | solution.py:23
  46.1 3.0 %collective-permute-done.17 = bf16[512,128]{1,0:T(8,128)(2,1)S(1)} collective-permute-done((bf16[512,128]{1,0:T(8,128)(2,1)S(1)}, bf16[512,128]{1,0:T(8,128)(2,1)S(1)}, u32[]{:S(2)}, u32[]{:S(2)}) %collective-permute-start.17) | collective-permute-done | bytes 131104 | tf_op jit(solution)/shard_map/ppermute | solution.py:23
  49.1 1.8 %collective-permute-start.9 = (bf16[136,256]{1,0:T(8,128)(2,1)S(1)}, bf16[136,256]{1,0:T(8,128)(2,1)S(1)}, u32[]{:S(2)}, u32[]{:S(2)}) collective-permute-start(bf16[136,256]{1,0:T(8,128)(2,1)S(1)} %fusion.2), channel_id=1, source_target_pairs={{0,2},{1,3},{2,0},{3,1},{4,6},{5,7},{6,4},{7,5},{8,10},{9,11},{10,... | collective-permute-start | bytes 208904 | tf_op jit(solution)/shard_map/ppermute | solution.py:23
  50.9 1.6 %spread.6.acc_ref = f32[512,128]{1,0:T(8,128)S(1)} custom-call(f32[512,128]{1,0:T(8,128)S(1)} %spread.5.acc_ref, bf16[256,128,128]{2,1,0:T(8,128)(2,1)S(1)} %get-tuple-element.35.adj_hbm, bf16[1,512,128]{2,1,0:T(8,128)(2,1)S(1)} %bitcast.56, bf16[1,512,128]{2,1,0:T(8,128)(2,1)S(1)} %bitcast.67, bf16[1,512,128]{2,1,0:T(8,128)(2,1)S(1)} %bitcast.71, ...), custom_call_target="tpu_custom_call" | custom-call | flops 20000000000 | tf_op jit(solution)/shard_map/spread/pallas_call | solution.py:382
  53.4 1.8 %collective-permute-start.22 = (bf16[512,128]{1,0:T(8,128)(2,1)S(1)}, bf16[512,128]{1,0:T(8,128)(2,1)S(1)}, u32[]{:S(2)}, u32[]{:S(2)}) collective-permute-start(bf16[512,128]{1,0:T(8,128)(2,1)S(1)} %collective-permute-done.14), channel_id=1, source_target_pairs={{0,2},{1,3},{2,0},{3,1},{4,6},{5,7},{6,4},{7,5},{8,10},{9,11},{10,... | collective-permute-start | bytes 393224 | tf_op jit(solution)/shard_map/ppermute | solution.py:23
  55.5 3.0 %collective-permute-start.12 = (bf16[136,256]{1,0:T(8,128)(2,1)S(1)}, bf16[136,256]{1,0:T(8,128)(2,1)S(1)}, u32[]{:S(2)}, u32[]{:S(2)}) collective-permute-start(bf16[136,256]{1,0:T(8,128)(2,1)S(1)} %add_convert_fusion.5), channel_id=1, source_target_pairs={{0,12},{1,13},{2,14},{3,15},{4,8},{5,9},{6,10},{7,11},{8,4},{9,5},... | collective-permute-start | bytes 208904 | tf_op jit(solution)/shard_map/ppermute | solution.py:23
  58.5 1.4 %collective-permute-start.10 = (bf16[136,256]{1,0:T(8,128)(2,1)S(1)}, bf16[136,256]{1,0:T(8,128)(2,1)S(1)}, u32[]{:S(2)}, u32[]{:S(2)}) collective-permute-start(bf16[136,256]{1,0:T(8,128)(2,1)S(1)} %add_convert_fusion.5), channel_id=1, source_target_pairs={{0,4},{1,5},{2,6},{3,7},{4,0},{5,1},{6,2},{7,3},{8,12},{9,13},{10,... | collective-permute-start | bytes 208904 | tf_op jit(solution)/shard_map/ppermute | solution.py:23
  59.9 1.6 %spread.7.acc_ref = f32[512,128]{1,0:T(8,128)S(1)} custom-call(f32[512,128]{1,0:T(8,128)S(1)} %spread.6.acc_ref, bf16[256,128,128]{2,1,0:T(8,128)(2,1)S(1)} %get-tuple-element.35.adj_hbm, bf16[1,512,128]{2,1,0:T(8,128)(2,1)S(1)} %bitcast.60, bf16[1,512,128]{2,1,0:T(8,128)(2,1)S(1)} %collective-permute-done.19.refs_1_, ...), custom_call_target="tpu_custom_call" | custom-call | flops 20000000000 | tf_op jit(solution)/shard_map/spread/pallas_call | solution.py:382
  62.3 1.5 %collective-permute-done.11 = bf16[136,256]{1,0:T(8,128)(2,1)S(1)} collective-permute-done((bf16[136,256]{1,0:T(8,128)(2,1)S(1)}, bf16[136,256]{1,0:T(8,128)(2,1)S(1)}, u32[]{:S(2)}, u32[]{:S(2)}) %collective-permute-start.11) | collective-permute-done | bytes 69664 | tf_op jit(solution)/shard_map/ppermute | solution.py:23
  64.4 1.9 %spread.8.acc_ref = f32[512,128]{1,0:T(8,128)S(1)} custom-call(f32[512,128]{1,0:T(8,128)S(1)} %spread.7.acc_ref, bf16[256,128,128]{2,1,0:T(8,128)(2,1)S(1)} %get-tuple-element.35.adj_hbm, bf16[1,512,128]{2,1,0:T(8,128)(2,1)S(1)} %bitcast.63, bf16[1,512,128]{2,1,0:T(8,128)(2,1)S(1)} %bitcast.69, bf16[1,512,128]{2,1,0:T(8,128)(2,1)S(1)} %collective-permute-done.24.refs_2_, ...), custom_call_target="tpu_custom_call" | custom-call | flops 20000000000 | tf_op jit(solution)/shard_map/spread/pallas_call | solution.py:382
  66.3 1.6 %spread.9 = (bf16[512,128]{1,0:T(8,128)(2,1)}, f32[128,256]{1,0:T(8,128)}, f32[128,256]{1,0:T(8,128)}, f32[1,256]{1,0:T(1,128)}) custom-call(s32[1]{0:T(128)} %bitcast.17.me_ref, f32[136,256]{1,0:T(8,128)S(1)} %add_add_fusion.mine_ref, f32[136,256]{1,0:T(8,128)S(1)} %collective-permute-done.13.theirs_ref, f32[512,128]{1,0:T(8,128)S(1)} %spread.8.acc_ref, ...), custom_call_target="tpu_custom_call" | custom-call | flops 20000000000 | tf_op jit(solution)/shard_map/spread/pallas_call | solution.py:382
  (73 shorter events, 8.1 us)
Async XLA Ops:
  7.4 3.0 %collective-permute-start = (bf16[8,128,512]{2,1,0:T(8,128)(2,1)}, bf16[8,128,512]{2,1,0:T(8,128)(2,1)S(1)}, u32[]{:S(2)}, u32[]{:S(2)}) collective-permute-start(bf16[8,128,512]{2,1,0:T(8,128)(2,1)} %get-tuple-element.24), channel_id=1, source_target_pairs={{0,1},{1,0},{2,3},{3,2},{4,5},{5,4},{6,7},{7,6},{8,9},{9,8},{10,11... | collective-permute-start | bytes 3145736 | tf_op jit(solution)/shard_map/ppermute | solution.py:23
  12.0 7.2 %collective-permute-start.4 = (bf16[128,512]{1,0:T(8,128)(2,1)S(1)}, bf16[128,512]{1,0:T(8,128)(2,1)S(1)}, u32[]{:S(2)}, u32[]{:S(2)}) collective-permute-start(bf16[128,512]{1,0:T(8,128)(2,1)S(1)} %get-tuple-element.43), channel_id=1, source_target_pairs={{0,2},{1,3},{2,0},{3,1},{4,6},{5,7},{6,4},{7,5},{8,10},{9,11},{10,... | collective-permute-start | bytes 393224 | tf_op jit(solution)/shard_map/ppermute | solution.py:23
  15.0 9.8 %collective-permute-start.6 = (bf16[128,512]{1,0:T(8,128)(2,1)S(1)}, bf16[128,512]{1,0:T(8,128)(2,1)S(1)}, u32[]{:S(2)}, u32[]{:S(2)}) collective-permute-start(bf16[128,512]{1,0:T(8,128)(2,1)S(1)} %add_convert_fusion.3), channel_id=1, source_target_pairs={{0,2},{1,3},{2,0},{3,1},{4,6},{5,7},{6,4},{7,5},{8,10},{9,11},{10,... | collective-permute-start | bytes 393224 | tf_op jit(solution)/shard_map/ppermute | solution.py:23
  15.1 20.8 %collective-permute-start.1 = (bf16[128,512]{1,0:T(8,128)(2,1)S(1)}, bf16[128,512]{1,0:T(8,128)(2,1)S(1)}, u32[]{:S(2)}, u32[]{:S(2)}) collective-permute-start(bf16[128,512]{1,0:T(8,128)(2,1)S(1)} %add_convert_fusion.2), channel_id=1, source_target_pairs={{0,2},{1,3},{2,0},{3,1},{4,6},{5,7},{6,4},{7,5},{8,10},{9,11},{10,... | collective-permute-start | bytes 393224 | tf_op jit(solution)/shard_map/ppermute | solution.py:23
  17.2 18.8 %collective-permute-start.2 = (bf16[128,512]{1,0:T(8,128)(2,1)S(1)}, bf16[128,512]{1,0:T(8,128)(2,1)S(1)}, u32[]{:S(2)}, u32[]{:S(2)}) collective-permute-start(bf16[128,512]{1,0:T(8,128)(2,1)S(1)} %get-tuple-element.42), channel_id=1, source_target_pairs={{0,4},{1,5},{2,6},{3,7},{4,0},{5,1},{6,2},{7,3},{8,12},{9,13},{10,... | collective-permute-start | bytes 393224 | tf_op jit(solution)/shard_map/ppermute | solution.py:23
  18.8 17.2 %collective-permute-start.3 = (bf16[128,512]{1,0:T(8,128)(2,1)S(1)}, bf16[128,512]{1,0:T(8,128)(2,1)S(1)}, u32[]{:S(2)}, u32[]{:S(2)}) collective-permute-start(bf16[128,512]{1,0:T(8,128)(2,1)S(1)} %get-tuple-element.41), channel_id=1, source_target_pairs={{0,6},{1,7},{2,4},{3,5},{4,2},{5,3},{6,0},{7,1},{8,14},{9,15},{10,... | collective-permute-start | bytes 393224 | tf_op jit(solution)/shard_map/ppermute | solution.py:23
  19.3 11.8 %collective-permute-start.5 = (bf16[128,512]{1,0:T(8,128)(2,1)S(1)}, bf16[128,512]{1,0:T(8,128)(2,1)S(1)}, u32[]{:S(2)}, u32[]{:S(2)}) collective-permute-start(bf16[128,512]{1,0:T(8,128)(2,1)S(1)} %fusion.1), channel_id=1, source_target_pairs={{0,12},{1,13},{2,14},{3,15},{4,8},{5,9},{6,10},{7,11},{8,4},{9,5},... | collective-permute-start | bytes 393224 | tf_op jit(solution)/shard_map/ppermute | solution.py:23
  24.9 11.1 %collective-permute-start.7 = (bf16[128,512]{1,0:T(8,128)(2,1)S(1)}, bf16[128,512]{1,0:T(8,128)(2,1)S(1)}, u32[]{:S(2)}, u32[]{:S(2)}) collective-permute-start(bf16[128,512]{1,0:T(8,128)(2,1)S(1)} %fusion), channel_id=1, source_target_pairs={{0,8},{1,9},{2,10},{3,11},{4,12},{5,13},{6,14},{7,15},{8,0},{9,1},... | collective-permute-start | bytes 393224 | tf_op jit(solution)/shard_map/ppermute | solution.py:23
  37.3 7.9 %collective-permute-start.14 = (bf16[512,128]{1,0:T(8,128)(2,1)S(1)}, bf16[512,128]{1,0:T(8,128)(2,1)S(1)}, u32[]{:S(2)}, u32[]{:S(2)}) collective-permute-start(bf16[512,128]{1,0:T(8,128)(2,1)S(1)} %get-tuple-element.36), channel_id=1, source_target_pairs={{0,12},{1,13},{2,14},{3,15},{4,8},{5,9},{6,10},{7,11},{8,4},{9,5},... | collective-permute-start | bytes 393224 | tf_op jit(solution)/shard_map/ppermute | solution.py:23
  38.6 7.5 %collective-permute-start.15 = (bf16[512,128]{1,0:T(8,128)(2,1)S(1)}, bf16[512,128]{1,0:T(8,128)(2,1)S(1)}, u32[]{:S(2)}, u32[]{:S(2)}) collective-permute-start(bf16[512,128]{1,0:T(8,128)(2,1)S(1)} %get-tuple-element.36), channel_id=1, source_target_pairs={{0,4},{1,5},{2,6},{3,7},{4,0},{5,1},{6,2},{7,3},{8,12},{9,13},{10,... | collective-permute-start | bytes 393224 | tf_op jit(solution)/shard_map/ppermute | solution.py:23
  38.6 6.7 %collective-permute-start.16 = (bf16[512,128]{1,0:T(8,128)(2,1)S(1)}, bf16[512,128]{1,0:T(8,128)(2,1)S(1)}, u32[]{:S(2)}, u32[]{:S(2)}) collective-permute-start(bf16[512,128]{1,0:T(8,128)(2,1)S(1)} %get-tuple-element.36), channel_id=1, source_target_pairs={{0,2},{1,3},{2,0},{3,1},{4,6},{5,7},{6,4},{7,5},{8,10},{9,11},{10,... | collective-permute-start | bytes 393224 | tf_op jit(solution)/shard_map/ppermute | solution.py:23
  41.7 7.4 %collective-permute-start.17 = (bf16[512,128]{1,0:T(8,128)(2,1)S(1)}, bf16[512,128]{1,0:T(8,128)(2,1)S(1)}, u32[]{:S(2)}, u32[]{:S(2)}) collective-permute-start(bf16[512,128]{1,0:T(8,128)(2,1)S(1)} %get-tuple-element.36), channel_id=1, source_target_pairs={{0,8},{1,9},{2,10},{3,11},{4,12},{5,13},{6,14},{7,15},{8,0},{9,1},... | collective-permute-start | bytes 393224 | tf_op jit(solution)/shard_map/ppermute | solution.py:23
  44.0 11.2 %collective-permute-start.18 = (bf16[512,128]{1,0:T(8,128)(2,1)S(1)}, bf16[512,128]{1,0:T(8,128)(2,1)S(1)}, u32[]{:S(2)}, u32[]{:S(2)}) collective-permute-start(bf16[512,128]{1,0:T(8,128)(2,1)S(1)} %get-tuple-element.36), channel_id=1, source_target_pairs={{0,6},{1,7},{2,4},{3,5},{4,2},{5,3},{6,0},{7,1},{8,14},{9,15},{10,... | collective-permute-start | bytes 393224 | tf_op jit(solution)/shard_map/ppermute | solution.py:23
  45.2 10.3 %collective-permute-start.19 = (bf16[1,512,128]{2,1,0:T(8,128)(2,1)S(1)}, bf16[1,512,128]{2,1,0:T(8,128)(2,1)S(1)}, u32[]{:S(2)}, u32[]{:S(2)}) collective-permute-start(bf16[1,512,128]{2,1,0:T(8,128)(2,1)S(1)} %bitcast.65), channel_id=1, source_target_pairs={{0,1},{1,0},{2,3},{3,2},{4,5},{5,4},{6,7},{7,6},{8,9},{9,8},{10,11... | collective-permute-start | bytes 393224 | tf_op jit(solution)/shard_map/ppermute | solution.py:23
  45.3 13.2 %collective-permute-start.20 = (bf16[1,512,128]{2,1,0:T(8,128)(2,1)S(1)}, bf16[1,512,128]{2,1,0:T(8,128)(2,1)S(1)}, u32[]{:S(2)}, u32[]{:S(2)}) collective-permute-start(bf16[1,512,128]{2,1,0:T(8,128)(2,1)S(1)} %bitcast.70), channel_id=1, source_target_pairs={{0,1},{1,0},{2,3},{3,2},{4,5},{5,4},{6,7},{7,6},{8,9},{9,8},{10,11... | collective-permute-start | bytes 393224 | tf_op jit(solution)/shard_map/ppermute | solution.py:23
  46.1 12.4 %collective-permute-start.21 = (bf16[1,512,128]{2,1,0:T(8,128)(2,1)S(1)}, bf16[1,512,128]{2,1,0:T(8,128)(2,1)S(1)}, u32[]{:S(2)}, u32[]{:S(2)}) collective-permute-start(bf16[1,512,128]{2,1,0:T(8,128)(2,1)S(1)} %bitcast.66), channel_id=1, source_target_pairs={{0,1},{1,0},{2,3},{3,2},{4,5},{5,4},{6,7},{7,6},{8,9},{9,8},{10,11... | collective-permute-start | bytes 393224 | tf_op jit(solution)/shard_map/ppermute | solution.py:23
  49.1 4.3 %collective-permute-start.9 = (bf16[136,256]{1,0:T(8,128)(2,1)S(1)}, bf16[136,256]{1,0:T(8,128)(2,1)S(1)}, u32[]{:S(2)}, u32[]{:S(2)}) collective-permute-start(bf16[136,256]{1,0:T(8,128)(2,1)S(1)} %fusion.2), channel_id=1, source_target_pairs={{0,2},{1,3},{2,0},{3,1},{4,6},{5,7},{6,4},{7,5},{8,10},{9,11},{10,... | collective-permute-start | bytes 208904 | tf_op jit(solution)/shard_map/ppermute | solution.py:23
  53.4 8.2 %collective-permute-start.22 = (bf16[512,128]{1,0:T(8,128)(2,1)S(1)}, bf16[512,128]{1,0:T(8,128)(2,1)S(1)}, u32[]{:S(2)}, u32[]{:S(2)}) collective-permute-start(bf16[512,128]{1,0:T(8,128)(2,1)S(1)} %collective-permute-done.14), channel_id=1, source_target_pairs={{0,2},{1,3},{2,0},{3,1},{4,6},{5,7},{6,4},{7,5},{8,10},{9,11},{10,... | collective-permute-start | bytes 393224 | tf_op jit(solution)/shard_map/ppermute | solution.py:23
  55.3 6.4 %collective-permute-start.23 = (bf16[512,128]{1,0:T(8,128)(2,1)S(1)}, bf16[512,128]{1,0:T(8,128)(2,1)S(1)}, u32[]{:S(2)}, u32[]{:S(2)}) collective-permute-start(bf16[512,128]{1,0:T(8,128)(2,1)S(1)} %collective-permute-done.17), channel_id=1, source_target_pairs={{0,2},{1,3},{2,0},{3,1},{4,6},{5,7},{6,4},{7,5},{8,10},{9,11},{10,... | collective-permute-start | bytes 393224 | tf_op jit(solution)/shard_map/ppermute | solution.py:23
  55.5 6.6 %collective-permute-start.12 = (bf16[136,256]{1,0:T(8,128)(2,1)S(1)}, bf16[136,256]{1,0:T(8,128)(2,1)S(1)}, u32[]{:S(2)}, u32[]{:S(2)}) collective-permute-start(bf16[136,256]{1,0:T(8,128)(2,1)S(1)} %add_convert_fusion.5), channel_id=1, source_target_pairs={{0,12},{1,13},{2,14},{3,15},{4,8},{5,9},{6,10},{7,11},{8,4},{9,5},... | collective-permute-start | bytes 208904 | tf_op jit(solution)/shard_map/ppermute | solution.py:23
  58.5 5.2 %collective-permute-start.11 = (bf16[136,256]{1,0:T(8,128)(2,1)S(1)}, bf16[136,256]{1,0:T(8,128)(2,1)S(1)}, u32[]{:S(2)}, u32[]{:S(2)}) collective-permute-start(bf16[136,256]{1,0:T(8,128)(2,1)S(1)} %add_convert_fusion.5), channel_id=1, source_target_pairs={{0,8},{1,9},{2,10},{3,11},{4,12},{5,13},{6,14},{7,15},{8,0},{9,1},... | collective-permute-start | bytes 208904 | tf_op jit(solution)/shard_map/ppermute | solution.py:23
  58.5 5.2 %collective-permute-start.10 = (bf16[136,256]{1,0:T(8,128)(2,1)S(1)}, bf16[136,256]{1,0:T(8,128)(2,1)S(1)}, u32[]{:S(2)}, u32[]{:S(2)}) collective-permute-start(bf16[136,256]{1,0:T(8,128)(2,1)S(1)} %add_convert_fusion.5), channel_id=1, source_target_pairs={{0,4},{1,5},{2,6},{3,7},{4,0},{5,1},{6,2},{7,3},{8,12},{9,13},{10,... | collective-permute-start | bytes 208904 | tf_op jit(solution)/shard_map/ppermute | solution.py:23
  61.6 2.7 %collective-permute-start.24 = (bf16[1,512,128]{2,1,0:T(8,128)(2,1)S(1)}, bf16[1,512,128]{2,1,0:T(8,128)(2,1)S(1)}, u32[]{:S(2)}, u32[]{:S(2)}) collective-permute-start(bf16[1,512,128]{2,1,0:T(8,128)(2,1)S(1)} %bitcast.57), channel_id=1, source_target_pairs={{0,1},{1,0},{2,3},{3,2},{4,5},{5,4},{6,7},{7,6},{8,9},{9,8},{10,11... | collective-permute-start | bytes 393224 | tf_op jit(solution)/shard_map/ppermute | solution.py:23
  61.7 2.7 %collective-permute-start.25 = (bf16[1,512,128]{2,1,0:T(8,128)(2,1)S(1)}, bf16[1,512,128]{2,1,0:T(8,128)(2,1)S(1)}, u32[]{:S(2)}, u32[]{:S(2)}) collective-permute-start(bf16[1,512,128]{2,1,0:T(8,128)(2,1)S(1)} %bitcast.59), channel_id=1, source_target_pairs={{0,1},{1,0},{2,3},{3,2},{4,5},{5,4},{6,7},{7,6},{8,9},{9,8},{10,11... | collective-permute-start | bytes 393224 | tf_op jit(solution)/shard_map/ppermute | solution.py:23
  (15 other events, 106.5 us)

commit v4 on v3

--- a/solution.py
+++ b/solution.py
@@ -13,8 +13,7 @@
 GROUP = 8
 CHUNKS = 8
 MIB = 1 << 20
-ADJ_LIMIT = 38
-PLAN = {'z': (1, 3, 2), 'y': (3, 2, 1, 0), 'parts': (), 'token': 0, 'after': 4, 'adj': 1, 'ysep': 1, 'agz': (3, 2, 1), 'groups': ((0,), (12, 4, 2, 8), (6, (1,), (3,), (5,)), (14, 10, (13,), (9,), (7,)), ((15,), (11,))), 'heavy': (1, 1, 1, 1, 1), 'pairs': ((0,), (2,), (4,), (6,), (8,), (12,), (10,), (14,)), 'terms': None, 'gy': None, 'gz': None, 'butter': 0, 'fin': 1, 'ph': 0, 'findep': 0, 'gyb': 1, 'direct': (1,), 'yfs': 0, 'agd': (1,), 'dsep': 0}
+PLAN = {'z': (1, 3, 2), 'y': (3, 2, 1, 0), 'parts': (), 'token': 0, 'after': 4, 'adj': 1, 'ysep': 1, 'agz': (3, 2, 1), 'groups': ((0,), (12, 4, 2, 8, 6, (1,), (3,), (5,)), (14, 10, (13,), (9,), (7,)), ((15,), (11,))), 'heavy': (1, 1, 1, 1), 'pairs': ((0,), (2,), (4,), (6,), (8,), (12,), (10,), (14,)), 'terms': None, 'gy': None, 'gz': None, 'butter': 0, 'fin': 1, 'ph': 0, 'findep': 0, 'gyb': 1, 'direct': (1,), 'yfs': 0, 'agd': (1,), 'dsep': 0, 'k1l': 55, 'adjl': 38, 'gates': ((1, (12, 4, 2, 8), 1),), 'halves': ((7, 5, 2, 3), (0, 6, 4, 1))}
 LIGHT = pl.CostEstimate(flops=0, bytes_accessed=0, transcendentals=0)
 HEAVY = pl.CostEstimate(flops=20_000_000_000, bytes_accessed=0, transcendentals=0)
 
@@ -69,9 +68,9 @@
 
 
 def forward_kernel(
-    nb, group, split, dest_ref, src_ref, dst_ref, x_hbm, pat_hbm, odd_hbm, even_hbm, *scratch
+    nb, group, split, parts, dest_ref, src_ref, dst_ref, x_hbm, pat_hbm, *refs
 ):
-    x_vmem, buf, adj, odd, even, sems, x_sem, out_sems = scratch
+    outs, (x_vmem, buf, adj, odd, even, sems, x_sem, out_sems) = refs[:-8], refs[-8:]
     tile = adj.shape[1]
     rows = x_vmem.shape[0]
     copy = pltpu.make_async_copy(x_hbm, x_vmem, x_sem)
@@ -82,9 +81,11 @@
     width = 2 if nb % 2 == 0 else 1
     half = group // 2
     step = pl.program_id(0)
-    outs = []
-    for parity, sums, out_hbm in ((1, odd, odd_hbm), (0, even, even_hbm)):
-        for m in range(half):
+    copies = []
+    for units, out_hbm in zip((*parts, range(half)), outs, strict=True):
+        parity = 0 if out_hbm is outs[-1] else 1
+        sums = odd if parity else even
+        for place, m in enumerate(units):
             for k in range(0, nb, width):
                 weight = jnp.concatenate(
                     [
@@ -96,30 +97,26 @@
                 sums[m, :, k * tile : (k + width) * tile] = jnp.dot(
                     xt, weight, preferred_element_type=F32
                 ).astype(sums.dtype)
-            if m % 2 == 1 or m == half - 1:
-                first = m - m % 2
-                part = pl.ds(first, m + 1 - first)
-                out = pltpu.make_async_copy(
-                    sums.at[part],
-                    out_hbm.at[pl.ds(step * half + first, m + 1 - first)],
-                    out_sems.at[parity, m // 2],
-                )
-                out.start()
-                outs.append(out)
-    for out in outs:
-        out.wait()
-
-
-def forward_sums(units, own_dtype, tiles_at, features, patterns, nb):
+            copy = pltpu.make_async_copy(
+                sums.at[m], out_hbm.at[step * half + place], out_sems.at[parity, m]
+            )
+            copy.start()
+            copies.append(copy)
+    for copy in copies:
+        copy.wait()
+
+
+def forward_sums(units, own_dtype, tiles_at, features, patterns, nb, parts):
     rows, feat = features.shape
     tiles, tile, _ = patterns.shape
     group = min(2 * GROUP, units)
     any_space = pl.BlockSpec(memory_space=pl.ANY)
-    return pl.pallas_call(
-        functools.partial(forward_kernel, nb, group, units > group),
-        grid=(units // group,),
+    steps = units // group
+    return pl.pallas_call(
+        functools.partial(forward_kernel, nb, group, units > group, parts),
+        grid=(steps,),
         in_specs=[pl.BlockSpec(memory_space=pltpu.SMEM)] * 3 + [any_space, any_space],
-        out_specs=[any_space, any_space],
+        out_specs=[any_space] * (len(parts) + 1),
         scratch_shapes=[
             pltpu.VMEM((rows, feat), BF16),
             pltpu.VMEM((tiles, tile, tile), jnp.int32),
@@ -128,13 +125,11 @@
             pltpu.VMEM((group // 2, feat, rows), own_dtype),
             pltpu.SemaphoreType.DMA((CHUNKS,)),
             pltpu.SemaphoreType.DMA,
-            pltpu.SemaphoreType.DMA((2, -(-group // 4))),
-        ],
-        out_shape=[
-            jax.ShapeDtypeStruct((units // 2, feat, rows), BF16),
-            jax.ShapeDtypeStruct((units // 2, feat, rows), own_dtype),
-        ],
-        compiler_params=pltpu.CompilerParams(vmem_limit_bytes=55 * MIB),
+            pltpu.SemaphoreType.DMA((2, group // 2)),
+        ],
+        out_shape=[jax.ShapeDtypeStruct((len(p) * steps, feat, rows), BF16) for p in parts]
+        + [jax.ShapeDtypeStruct((units // 2, feat, rows), own_dtype)],
+        compiler_params=pltpu.CompilerParams(vmem_limit_bytes=PLAN["k1l"] * MIB),
         cost_estimate=LIGHT,
         name="forward_sums",
     )(*tiles_at, features, patterns)
@@ -170,7 +165,7 @@
             jax.ShapeDtypeStruct((units * nb * nb, tile, tile), BF16),
             jax.ShapeDtypeStruct((8, 128), F32),
         ],
-        compiler_params=pltpu.CompilerParams(vmem_limit_bytes=ADJ_LIMIT * MIB),
+        compiler_params=pltpu.CompilerParams(vmem_limit_bytes=PLAN["adjl"] * MIB),
         cost_estimate=HEAVY if PLAN["adj"] else LIGHT,
         name="adjacency",
     )(*tiles_at, patterns, after)
@@ -198,7 +193,7 @@
     )(total, *parts, after)
 
 
-def layer_kernel(n_recv, own_ref, *refs):
+def layer_kernel(n_recv, made_hbm, own_ref, *refs):
     recv = refs[:n_recv]
     (deg_ref, x_ref, cot_ref, ws_ref, wn_ref, bias_ref) = refs[n_recv : n_recv + 6]
     out_ref, delta_ref, aggt_ref, back_ref = refs[n_recv + 6 :]
@@ -225,7 +220,7 @@
     back_ref[...] = (back / degree.T).astype(BF16)
 
 
-def layer(own, recv, in_degree, features, cotangent, w_self, w_neigh, bias):
+def layer(made, own, recv, in_degree, features, cotangent, w_self, w_neigh, bias):
     rows, feat = features.shape
     hidden = w_self.shape[1]
 
@@ -239,7 +234,9 @@
     return pl.pallas_call(
         functools.partial(layer_kernel, len(recv)),
         grid=(1,),
-        in_specs=[first(own)] + [first(r) for r in recv] + [whole(a) for a in rest],
+        in_specs=[pl.BlockSpec(memory_space=pl.ANY), first(own)]
+        + [first(r) for r in recv]
+        + [whole(a) for a in rest],
         out_specs=[
             pl.BlockSpec((rows, hidden), lambda i: (0, 0)),
             pl.BlockSpec((rows, hidden), lambda i: (0, 0)),
@@ -255,7 +252,7 @@
         compiler_params=pltpu.CompilerParams(vmem_limit_bytes=8 * MIB),
         cost_estimate=LIGHT,
         name="layer",
-    )(own, *recv, *rest)
+    )(made, own, *recv, *rest)
 
 
 def grad_kernel(scale, me_ref, x_ref, delta_ref, aggt_ref, ws_ref, g_ref, base_ref):
@@ -295,7 +292,8 @@
     )(me, features, delta, aggt, w_self)
 
 
-def spread_kernel(places, nb, n_arrays, acc_ref, adj_hbm, *refs):
+def spread_kernel(places, nb, n_arrays, marks, acc_ref, adj_hbm, *refs):
+    refs = refs[marks:]
     backs = refs[:n_arrays]
     out_ref, adj, sems = refs[n_arrays], *refs[-2:]
     per_unit = nb * nb
@@ -321,6 +319,22 @@
     out_ref[...] = total.astype(out_ref.dtype)
 
 
+def gate_kernel(*refs):
+    refs[-1][...] = jnp.zeros(refs[-1].shape, F32)
+
+
+def gate(*arrays):
+    return pl.pallas_call(
+        gate_kernel,
+        in_specs=[pl.BlockSpec(memory_space=pl.ANY)] * len(arrays),
+        out_specs=pl.BlockSpec(memory_space=pltpu.VMEM),
+        out_shape=jax.ShapeDtypeStruct((8, 128), F32),
+        compiler_params=pltpu.CompilerParams(vmem_limit_bytes=4 * MIB),
+        cost_estimate=HEAVY,
+        name="gate",
+    )(*arrays)
+
+
 def finish_kernel(me_ref, mine_ref, theirs_ref, *refs):
     gs_ref, gn_ref, gb_ref = refs[-3:]
     feat = gs_ref.shape[0]
@@ -353,20 +367,24 @@
     )(me, mine, theirs, *after)
 
 
-def last_kernel(places, nb, n_arrays, me_ref, mine_ref, theirs_ref, acc_ref, adj_hbm, *refs):
+def last_kernel(
+    places, nb, n_arrays, marks, me_ref, mine_ref, theirs_ref, acc_ref, adj_hbm, *refs
+):
+    refs = refs[marks:]
     backs, out_ref, grads, scratch = refs[:n_arrays], refs[n_arrays], refs[-5:-2], refs[-2:]
     finish_kernel(me_ref, mine_ref, theirs_ref, *grads)
-    spread_kernel(places, nb, n_arrays, acc_ref, adj_hbm, *backs, out_ref, *scratch)
-
-
-def spread(acc, adjacency, places, backs, nb, dtype, heavy=True, grads=None):
+    spread_kernel(places, nb, n_arrays, 0, acc_ref, adj_hbm, *backs, out_ref, *scratch)
+
+
+def spread(acc, adjacency, marks, places, backs, nb, dtype, heavy=True, grads=None):
     vm = pl.BlockSpec(memory_space=pltpu.VMEM)
     rows, feat = acc.shape
     per_unit = nb * nb
     tile = adjacency.shape[1]
     n = len(places)
-    in_specs = [vm, pl.BlockSpec(memory_space=pl.ANY)] + [vm] * len(backs)
-    inputs = [acc, adjacency, *backs]
+    any_space = pl.BlockSpec(memory_space=pl.ANY)
+    in_specs = [vm, any_space] + [any_space] * len(marks) + [vm] * len(backs)
+    inputs = [acc, adjacency, *marks, *backs]
     kernel, out_shape = spread_kernel, jax.ShapeDtypeStruct((rows, feat), dtype)
     if grads is not None:
         in_specs = [pl.BlockSpec(memory_space=pltpu.SMEM), vm, vm] + in_specs
@@ -380,7 +398,7 @@
             jax.ShapeDtypeStruct((1, hidden), F32),
         ]
     return pl.pallas_call(
-        functools.partial(kernel, tuple(places), nb, len(backs)),
+        functools.partial(kernel, tuple(places), nb, len(backs), len(marks)),
         in_specs=in_specs,
         out_specs=jax.tree.map(lambda _: vm, out_shape),
         out_shape=out_shape,
@@ -431,11 +449,21 @@
 
     tiles_at = (tile_dest.reshape(-1), tile_src_block, tile_dst_block)
 
-    s_other, s_own = forward_sums(devices, F32 if small else BF16, tiles_at, features, patterns, nb)
-    s_recv = swap(s_other, 1, devices)
+    parts = PLAN["halves"] if small else (tuple(range(min(GROUP, units))),)
+    *s_other, s_own = forward_sums(
+        devices, F32 if small else BF16, tiles_at, features, patterns, nb, parts
+    )
+    received = [swap(s, 1, devices) for s in s_other]
+    s_recv = received[-1]
+    from_other = {}
+    for units_of, got in zip(parts, received, strict=True):
+        if small:
+            from_other.update({m: got[i] for i, m in enumerate(units_of)})
+    if not small:
+        from_other = {m: s_recv[m] for m in range(units)}
 
     def chip_sum(m):
-        return s_own[m].astype(F32) + s_recv[m].astype(F32)
+        return s_own[m].astype(F32) + from_other[m].astype(F32)
 
     if small:
         y_recv = [None] * nz
@@ -445,7 +473,7 @@
             if n in PLAN["direct"]:
                 continue
             for k in range(1, ny):
-                own, recv = s_own[n * ny + k], s_recv[n * ny + k]
+                own, recv = s_own[n * ny + k], from_other[n * ny + k]
                 if sent is not None and PLAN["ysep"]:
                     own, recv, sent = lax.optimization_barrier((own, recv, sent))
                 sent = (own.astype(F32) + recv.astype(F32)).astype(BF16)
@@ -466,7 +494,7 @@
         if small and n in PLAN["direct"]:
             for k in range(ny):
                 m = n * ny + k
-                mine, recv, sent = s_own[m], s_recv[m], first_sent
+                mine, recv, sent = s_own[m], from_other[m], first_sent
                 if PLAN["dsep"]:
                     mine, recv, sent = lax.optimization_barrier((mine, recv, sent))
                 direct = (mine.astype(F32) + recv.astype(F32)).astype(BF16)
@@ -483,7 +511,6 @@
     made = s_recv
     if after == 4:
         adj, made = adjacency(devices, tiles_at, patterns, nb, z_recv[3])
-        in_degree, made = lax.optimization_barrier((in_degree, made))
     elif after:
         adj, made = adjacency(devices, tiles_at, patterns, nb, sums[after])
     total, summed = s_own, ()
@@ -497,6 +524,7 @@
     rest = [z_recv[n] for n in z_recv if n not in summed]
 
     output, delta, aggt, back = layer(
+        made,
         total,
         ([s_recv] if not parts else []) + [r[None] for r in y_recv[0]] + rest,
         in_degree.reshape(1, rows),
@@ -557,6 +585,7 @@
         [half.astype(F32)] + [swap(half, 2 * k, devices).astype(F32) for k in range(1, ny)]
     )
     half = later(half, "gz")
+    y_half = half
     if PLAN["butter"] and small:
         for n in (1, 2):
             rounded = half.astype(BF16)
@@ -581,9 +610,14 @@
         parts = [(u, own[u]) if u in own else (u, across[u]) for u in group]
         parts = [(u if isinstance(u, tuple) else (u,), b) for u, b in parts]
         places = [u for us, _ in parts for u in us]
+        marks = []
+        for at, keys, with_half in PLAN["gates"] if small else ():
+            if at == i:
+                marks.append(gate(*([grad_feat] if i else []), *[own[k] if k in own else across[k] for k in keys], *([y_half] if with_half else [])))
         grad_feat = spread(
             grad_feat,
             adj,
+            marks,
             places,
             [b for _, b in parts],
             nb,

time: 68.1 us -> 67.3 us (0.988)
  starting transfers between devices: 30.2 us -> 32.1 us
  waiting for transfers between devices: 14.6 us -> 12.7 us
  Pallas kernels: 20.2 us -> 19.4 us
    ppermute x29 -> x30, starting transfers between devices: 30.2 us -> 32.1 us  [swap(): return lax.ppermute(value, 'row', [(i, i ^ bits) for i in range(devices)])]
    ppermute x29 -> x30, waiting for transfers between devices: 14.6 us -> 12.7 us  [swap(): return lax.ppermute(value, 'row', [(i, i ^ bits) for i in range(devices)])]
  transfers between devices with their start and end apart: 29 -> 30, of which waited for: 9 -> 10; matrix products, arithmetic and copies ran while one was open for 0% -> 3% of each run, Pallas kernels for 16% -> 14%
where the time goes in v4:
time: 67.3 us; the launch traced here: 67.1 us
  starting transfers between devices  32.1 us (48%)
  Pallas kernels  19.4 us (29%)
  waiting for transfers between devices  12.7 us (19%)
  other arithmetic  1.81 us (3%)
  between operations  0.99 us (1%)
    ppermute x30, starting transfers between devices, swap(): return lax.ppermute(value, 'row', [(i, i ^ bits) for i in range(devices)])  32.1 us
    ppermute x30, waiting for transfers between devices, swap(): return lax.ppermute(value, 'row', [(i, i ^ bits) for i in range(devices)])  12.7 us
    pallas_call x4, Pallas kernels, spread(): pl.pallas_call(functools.partial(kernel, tuple(places), nb, len(backs), l...  6.88 us
    pallas_call x1, Pallas kernels, forward_sums(): pl.pallas_call(functools.partial(forward_kernel, nb, group, units > group...  6.72 us
    pallas_call x1, Pallas kernels, adjacency(): pl.pallas_call(functools.partial(adjacency_kernel, nb, group, units > gro...  4.24 us
    convert_element_type x1, other arithmetic, on_device(): direct = (mine.astype(F32) + recv.astype(F32)).astype(BF16)  1.59 us
  transfers between devices with their start and end apart: 30, of which 10 were waited for; matrix products, arithmetic and copies ran while one was open for 3% of the time, Pallas kernels for 14%

profile of v4, /device:TPU:0, one launch (start us, length us, event | category | flops | bytes accessed | tf_op | source)
XLA Modules:
  0.0 67.1 jit_solution(2352121016502997945)
XLA Ops:
  0.6 6.7 %forward_sums.1 = (bf16[4,128,512]{2,1,0:T(8,128)(2,1)}, bf16[4,128,512]{2,1,0:T(8,128)(2,1)}, f32[8,128,512]{2,1,0:T(8,128)}) custom-call(s32[128]{0:T(128)} %bitcast.54, s32[128]{0:T(128)} %src_ref.3, s32[128]{0:T(128)} %dst_ref.3, bf16[512,128]{1,0:T(8,128)(2,1)} %x_ref.1, s32[128,128,128]{2,1,0:T(8,128)} %pat_hbm.3), custom_call_target="tpu_custom_call" | custom-call | tf_op jit(solution)/shard_map/forward_sums/pallas_call | solution.py:115
  8.0 1.7 %collective-permute-done.1 = bf16[4,128,512]{2,1,0:T(8,128)(2,1)S(1)} collective-permute-done((bf16[4,128,512]{2,1,0:T(8,128)(2,1)}, bf16[4,128,512]{2,1,0:T(8,128)(2,1)S(1)}, u32[]{:S(2)}, u32[]{:S(2)}) %collective-permute-start.1) | collective-permute-done | bytes 524320 | tf_op jit(solution)/shard_map/ppermute | solution.py:22
  9.6 1.6 %fusion.5 = (bf16[128,512]{1,0:T(8,128)(2,1)S(1)}, bf16[128,512]{1,0:T(8,128)(2,1)S(1)}, bf16[128,512]{1,0:T(8,128)(2,1)S(1)}, f32[128,512]{1,0:T(8,128)S(1)}, f32[128,512]{1,0:T(8,128)S(1)}) fusion(f32[8,128,512]{2,1,0:T(8,128)} %get-tuple-element.25.own_ref, bf16[4,128,512]{2,1,0:T(8,128)(2,1)S(1)} %collective-permute-done.1), kind=kLoop, calls=%fused_computation.18 | loop fusion | flops 589824 | bytes 2621440 | tf_op jit(solution)/shard_map/convert_element_type | solution.py:500
  11.3 3.0 %collective-permute-start.2 = (bf16[128,512]{1,0:T(8,128)(2,1)S(1)}, bf16[128,512]{1,0:T(8,128)(2,1)S(1)}, u32[]{:S(2)}, u32[]{:S(2)}) collective-permute-start(bf16[128,512]{1,0:T(8,128)(2,1)S(1)} %get-tuple-element.47), channel_id=1, source_target_pairs={{0,2},{1,3},{2,0},{3,1},{4,6},{5,7},{6,4},{7,5},{8,10},{9,11},{10,... | collective-permute-start | bytes 393224 | tf_op jit(solution)/shard_map/ppermute | solution.py:22
  14.4 2.1 %collective-permute-start.4 = (bf16[128,512]{1,0:T(8,128)(2,1)S(1)}, bf16[128,512]{1,0:T(8,128)(2,1)S(1)}, u32[]{:S(2)}, u32[]{:S(2)}) collective-permute-start(bf16[128,512]{1,0:T(8,128)(2,1)S(1)} %add_convert_fusion.2), channel_id=1, source_target_pairs={{0,2},{1,3},{2,0},{3,1},{4,6},{5,7},{6,4},{7,5},{8,10},{9,11},{10,... | collective-permute-start | bytes 393224 | tf_op jit(solution)/shard_map/ppermute | solution.py:22
  16.5 1.6 %collective-permute-start.5 = (bf16[128,512]{1,0:T(8,128)(2,1)S(1)}, bf16[128,512]{1,0:T(8,128)(2,1)S(1)}, u32[]{:S(2)}, u32[]{:S(2)}) collective-permute-start(bf16[128,512]{1,0:T(8,128)(2,1)S(1)} %get-tuple-element.46), channel_id=1, source_target_pairs={{0,4},{1,5},{2,6},{3,7},{4,0},{5,1},{6,2},{7,3},{8,12},{9,13},{10,... | collective-permute-start | bytes 393224 | tf_op jit(solution)/shard_map/ppermute | solution.py:22
  18.5 4.2 %collective-permute-start.3 = (bf16[128,512]{1,0:T(8,128)(2,1)S(1)}, bf16[128,512]{1,0:T(8,128)(2,1)S(1)}, u32[]{:S(2)}, u32[]{:S(2)}) collective-permute-start(bf16[128,512]{1,0:T(8,128)(2,1)S(1)} %fusion.1), channel_id=1, source_target_pairs={{0,12},{1,13},{2,14},{3,15},{4,8},{5,9},{6,10},{7,11},{8,4},{9,5},... | collective-permute-start | bytes 393224 | tf_op jit(solution)/shard_map/ppermute | solution.py:22
  22.7 1.4 %collective-permute-done.7 = bf16[128,512]{1,0:T(8,128)(2,1)S(1)} collective-permute-done((bf16[128,512]{1,0:T(8,128)(2,1)S(1)}, bf16[128,512]{1,0:T(8,128)(2,1)S(1)}, u32[]{:S(2)}, u32[]{:S(2)}) %collective-permute-start.7) | collective-permute-done | bytes 131104 | tf_op jit(solution)/shard_map/ppermute | solution.py:22
  24.2 2.5 %collective-permute-start.8 = (bf16[128,512]{1,0:T(8,128)(2,1)S(1)}, bf16[128,512]{1,0:T(8,128)(2,1)S(1)}, u32[]{:S(2)}, u32[]{:S(2)}) collective-permute-start(bf16[128,512]{1,0:T(8,128)(2,1)S(1)} %fusion), channel_id=1, source_target_pairs={{0,8},{1,9},{2,10},{3,11},{4,12},{5,13},{6,14},{7,15},{8,0},{9,1},... | collective-permute-start | bytes 393224 | tf_op jit(solution)/shard_map/ppermute | solution.py:22
  26.6 3.7 %collective-permute-done.3 = bf16[128,512]{1,0:T(8,128)(2,1)S(1)} collective-permute-done((bf16[128,512]{1,0:T(8,128)(2,1)S(1)}, bf16[128,512]{1,0:T(8,128)(2,1)S(1)}, u32[]{:S(2)}, u32[]{:S(2)}) %collective-permute-start.3) | collective-permute-done | bytes 131104 | tf_op jit(solution)/shard_map/ppermute | solution.py:22
  30.4 4.2 %adjacency.1 = (bf16[256,128,128]{2,1,0:T(8,128)(2,1)S(1)}, f32[8,128]{1,0:T(8,128)S(1)}) custom-call(s32[128]{0:T(128)S(1)} %bitcast.55, s32[128]{0:T(128)S(1)} %copy-done.8, s32[128]{0:T(128)S(1)} %copy-done.9, s32[128,128,128]{2,1,0:T(8,128)} %pat_hbm.3, bf16[1,128,512]{2,1,0:T(8,128)(2,1)S(1)} %bitcast.49), custom_call_target="tpu_custom_call" | custom-call | flops 20000000000 | tf_op jit(solution)/shard_map/adjacency/pallas_call | solution.py:155
  34.8 1.2 %layer.1 = (bf16[512,256]{1,0:T(8,128)(2,1)}, bf16[512,256]{1,0:T(8,128)(2,1)S(1)}, bf16[128,512]{1,0:T(8,128)(2,1)S(1)}, bf16[512,128]{1,0:T(8,128)(2,1)S(1)}) custom-call(f32[8,128]{1,0:T(8,128)S(1)} %get-tuple-element.28.made_hbm, f32[8,128,512]{2,1,0:T(8,128)S(1)} %copy-done, bf16[4,128,512]{2,1,0:T(8,128)(2,1)S(1)} %collective-permute-done.refs_0_, ...), custom_call_target="tpu_custom_call" | custom-call | tf_op jit(solution)/shard_map/layer/pallas_call | solution.py:234
  36.4 1.4 %collective-permute-start.15 = (bf16[512,128]{1,0:T(8,128)(2,1)S(1)}, bf16[512,128]{1,0:T(8,128)(2,1)S(1)}, u32[]{:S(2)}, u32[]{:S(2)}) collective-permute-start(bf16[512,128]{1,0:T(8,128)(2,1)S(1)} %get-tuple-element.40), channel_id=1, source_target_pairs={{0,12},{1,13},{2,14},{3,15},{4,8},{5,9},{6,10},{7,11},{8,4},{9,5},... | collective-permute-start | bytes 393224 | tf_op jit(solution)/shard_map/ppermute | solution.py:22
  37.8 3.1 %collective-permute-start.17 = (bf16[512,128]{1,0:T(8,128)(2,1)S(1)}, bf16[512,128]{1,0:T(8,128)(2,1)S(1)}, u32[]{:S(2)}, u32[]{:S(2)}) collective-permute-start(bf16[512,128]{1,0:T(8,128)(2,1)S(1)} %get-tuple-element.40), channel_id=1, source_target_pairs={{0,2},{1,3},{2,0},{3,1},{4,6},{5,7},{6,4},{7,5},{8,10},{9,11},{10,... | collective-permute-start | bytes 393224 | tf_op jit(solution)/shard_map/ppermute | solution.py:22
  41.4 1.5 %collective-permute-start.10 = (bf16[136,256]{1,0:T(8,128)(2,1)S(1)}, bf16[136,256]{1,0:T(8,128)(2,1)S(1)}, u32[]{:S(2)}, u32[]{:S(2)}) collective-permute-start(bf16[136,256]{1,0:T(8,128)(2,1)S(1)} %fusion.2), channel_id=1, source_target_pairs={{0,2},{1,3},{2,0},{3,1},{4,6},{5,7},{6,4},{7,5},{8,10},{9,11},{10,... | collective-permute-start | bytes 208904 | tf_op jit(solution)/shard_map/ppermute | solution.py:22
  43.3 2.6 %collective-permute-done.10 = bf16[136,256]{1,0:T(8,128)(2,1)S(1)} collective-permute-done((bf16[136,256]{1,0:T(8,128)(2,1)S(1)}, bf16[136,256]{1,0:T(8,128)(2,1)S(1)}, u32[]{:S(2)}, u32[]{:S(2)}) %collective-permute-start.10) | collective-permute-done | bytes 69664 | tf_op jit(solution)/shard_map/ppermute | solution.py:22
  45.9 1.5 %collective-permute-start.19 = (bf16[512,128]{1,0:T(8,128)(2,1)S(1)}, bf16[512,128]{1,0:T(8,128)(2,1)S(1)}, u32[]{:S(2)}, u32[]{:S(2)}) collective-permute-start(bf16[512,128]{1,0:T(8,128)(2,1)S(1)} %get-tuple-element.40), channel_id=1, source_target_pairs={{0,6},{1,7},{2,4},{3,5},{4,2},{5,3},{6,0},{7,1},{8,14},{9,15},{10,... | collective-permute-start | bytes 393224 | tf_op jit(solution)/shard_map/ppermute | solution.py:22
  48.0 1.1 %collective-permute-done.16 = bf16[512,128]{1,0:T(8,128)(2,1)S(1)} collective-permute-done((bf16[512,128]{1,0:T(8,128)(2,1)S(1)}, bf16[512,128]{1,0:T(8,128)(2,1)S(1)}, u32[]{:S(2)}, u32[]{:S(2)}) %collective-permute-start.16) | collective-permute-done | bytes 131104 | tf_op jit(solution)/shard_map/ppermute | solution.py:22
  49.5 3.7 %collective-permute-start.23 = (bf16[512,128]{1,0:T(8,128)(2,1)S(1)}, bf16[512,128]{1,0:T(8,128)(2,1)S(1)}, u32[]{:S(2)}, u32[]{:S(2)}) collective-permute-start(bf16[512,128]{1,0:T(8,128)(2,1)S(1)} %collective-permute-done.15), channel_id=1, source_target_pairs={{0,2},{1,3},{2,0},{3,1},{4,6},{5,7},{6,4},{7,5},{8,10},{9,11},{10,... | collective-permute-start | bytes 393224 | tf_op jit(solution)/shard_map/ppermute | solution.py:22
  54.3 2.2 %collective-permute-start.12 = (bf16[136,256]{1,0:T(8,128)(2,1)S(1)}, bf16[136,256]{1,0:T(8,128)(2,1)S(1)}, u32[]{:S(2)}, u32[]{:S(2)}) collective-permute-start(bf16[136,256]{1,0:T(8,128)(2,1)S(1)} %get-tuple-element.51), channel_id=1, source_target_pairs={{0,8},{1,9},{2,10},{3,11},{4,12},{5,13},{6,14},{7,15},{8,0},{9,1},... | collective-permute-start | bytes 208904 | tf_op jit(solution)/shard_map/ppermute | solution.py:22
  56.5 2.1 %collective-permute-start.13 = (bf16[136,256]{1,0:T(8,128)(2,1)S(1)}, bf16[136,256]{1,0:T(8,128)(2,1)S(1)}, u32[]{:S(2)}, u32[]{:S(2)}) collective-permute-start(bf16[136,256]{1,0:T(8,128)(2,1)S(1)} %get-tuple-element.51), channel_id=1, source_target_pairs={{0,12},{1,13},{2,14},{3,15},{4,8},{5,9},{6,10},{7,11},{8,4},{9,5},... | collective-permute-start | bytes 208904 | tf_op jit(solution)/shard_map/ppermute | solution.py:22
  58.6 3.0 %spread.5.acc_ref = f32[512,128]{1,0:T(8,128)S(1)} custom-call(f32[512,128]{1,0:T(8,128)S(1)} %spread.4.refs_0_.acc_ref, bf16[256,128,128]{2,1,0:T(8,128)(2,1)S(1)} %get-tuple-element.39.adj_hbm, f32[8,128]{1,0:T(8,128)S(1)} %gate.1.refs_0_, bf16[1,512,128]{2,1,0:T(8,128)(2,1)S(1)} %bitcast.57, bf16[1,512,128]{2,1,0:T(8,128)(2,1)S(1)} %bitcast.70, ...), custom_call_target="tpu_custom_call" | custom-call | flops 20000000000 | tf_op jit(solution)/shard_map/spread/pallas_call | solution.py:400
  63.6 1.9 %spread.6.acc_ref = f32[512,128]{1,0:T(8,128)S(1)} custom-call(f32[512,128]{1,0:T(8,128)S(1)} %spread.5.acc_ref, bf16[256,128,128]{2,1,0:T(8,128)(2,1)S(1)} %get-tuple-element.39.adj_hbm, bf16[1,512,128]{2,1,0:T(8,128)(2,1)S(1)} %bitcast.65, bf16[1,512,128]{2,1,0:T(8,128)(2,1)S(1)} %bitcast.72, bf16[1,512,128]{2,1,0:T(8,128)(2,1)S(1)} %collective-permute-done.25.refs_2_, ...), custom_call_target="tpu_custom_call" | custom-call | flops 20000000000 | tf_op jit(solution)/shard_map/spread/pallas_call | solution.py:400
  65.5 1.6 %spread.7 = (bf16[512,128]{1,0:T(8,128)(2,1)}, f32[128,256]{1,0:T(8,128)}, f32[128,256]{1,0:T(8,128)}, f32[1,256]{1,0:T(1,128)}) custom-call(s32[1]{0:T(128)} %bitcast.17.me_ref, f32[136,256]{1,0:T(8,128)S(1)} %add_add_fusion.mine_ref, f32[136,256]{1,0:T(8,128)S(1)} %collective-permute-done.14.theirs_ref, f32[512,128]{1,0:T(8,128)S(1)} %spread.6.acc_ref, ...), custom_call_target="tpu_custom_call" | custom-call | flops 20000000000 | tf_op jit(solution)/shard_map/spread/pallas_call | solution.py:400
  (76 shorter events, 6.7 us)
Async XLA Ops:
  7.9 6.5 %collective-permute-start = (bf16[4,128,512]{2,1,0:T(8,128)(2,1)}, bf16[4,128,512]{2,1,0:T(8,128)(2,1)S(1)}, u32[]{:S(2)}, u32[]{:S(2)}) collective-permute-start(bf16[4,128,512]{2,1,0:T(8,128)(2,1)} %get-tuple-element.26), channel_id=1, source_target_pairs={{0,1},{1,0},{2,3},{3,2},{4,5},{5,4},{6,7},{7,6},{8,9},{9,8},{10,11... | collective-permute-start | bytes 1572872 | tf_op jit(solution)/shard_map/ppermute | solution.py:22
  11.3 7.2 %collective-permute-start.2 = (bf16[128,512]{1,0:T(8,128)(2,1)S(1)}, bf16[128,512]{1,0:T(8,128)(2,1)S(1)}, u32[]{:S(2)}, u32[]{:S(2)}) collective-permute-start(bf16[128,512]{1,0:T(8,128)(2,1)S(1)} %get-tuple-element.47), channel_id=1, source_target_pairs={{0,2},{1,3},{2,0},{3,1},{4,6},{5,7},{6,4},{7,5},{8,10},{9,11},{10,... | collective-permute-start | bytes 393224 | tf_op jit(solution)/shard_map/ppermute | solution.py:22
  14.3 9.8 %collective-permute-start.7 = (bf16[128,512]{1,0:T(8,128)(2,1)S(1)}, bf16[128,512]{1,0:T(8,128)(2,1)S(1)}, u32[]{:S(2)}, u32[]{:S(2)}) collective-permute-start(bf16[128,512]{1,0:T(8,128)(2,1)S(1)} %add_convert_fusion.3), channel_id=1, source_target_pairs={{0,2},{1,3},{2,0},{3,1},{4,6},{5,7},{6,4},{7,5},{8,10},{9,11},{10,... | collective-permute-start | bytes 393224 | tf_op jit(solution)/shard_map/ppermute | solution.py:22
  14.4 20.3 %collective-permute-start.4 = (bf16[128,512]{1,0:T(8,128)(2,1)S(1)}, bf16[128,512]{1,0:T(8,128)(2,1)S(1)}, u32[]{:S(2)}, u32[]{:S(2)}) collective-permute-start(bf16[128,512]{1,0:T(8,128)(2,1)S(1)} %add_convert_fusion.2), channel_id=1, source_target_pairs={{0,2},{1,3},{2,0},{3,1},{4,6},{5,7},{6,4},{7,5},{8,10},{9,11},{10,... | collective-permute-start | bytes 393224 | tf_op jit(solution)/shard_map/ppermute | solution.py:22
  16.5 18.2 %collective-permute-start.5 = (bf16[128,512]{1,0:T(8,128)(2,1)S(1)}, bf16[128,512]{1,0:T(8,128)(2,1)S(1)}, u32[]{:S(2)}, u32[]{:S(2)}) collective-permute-start(bf16[128,512]{1,0:T(8,128)(2,1)S(1)} %get-tuple-element.46), channel_id=1, source_target_pairs={{0,4},{1,5},{2,6},{3,7},{4,0},{5,1},{6,2},{7,3},{8,12},{9,13},{10,... | collective-permute-start | bytes 393224 | tf_op jit(solution)/shard_map/ppermute | solution.py:22
  18.0 16.6 %collective-permute-start.6 = (bf16[128,512]{1,0:T(8,128)(2,1)S(1)}, bf16[128,512]{1,0:T(8,128)(2,1)S(1)}, u32[]{:S(2)}, u32[]{:S(2)}) collective-permute-start(bf16[128,512]{1,0:T(8,128)(2,1)S(1)} %get-tuple-element.45), channel_id=1, source_target_pairs={{0,6},{1,7},{2,4},{3,5},{4,2},{5,3},{6,0},{7,1},{8,14},{9,15},{10,... | collective-permute-start | bytes 393224 | tf_op jit(solution)/shard_map/ppermute | solution.py:22
  18.5 11.8 %collective-permute-start.3 = (bf16[128,512]{1,0:T(8,128)(2,1)S(1)}, bf16[128,512]{1,0:T(8,128)(2,1)S(1)}, u32[]{:S(2)}, u32[]{:S(2)}) collective-permute-start(bf16[128,512]{1,0:T(8,128)(2,1)S(1)} %fusion.1), channel_id=1, source_target_pairs={{0,12},{1,13},{2,14},{3,15},{4,8},{5,9},{6,10},{7,11},{8,4},{9,5},... | collective-permute-start | bytes 393224 | tf_op jit(solution)/shard_map/ppermute | solution.py:22
  24.2 10.5 %collective-permute-start.8 = (bf16[128,512]{1,0:T(8,128)(2,1)S(1)}, bf16[128,512]{1,0:T(8,128)(2,1)S(1)}, u32[]{:S(2)}, u32[]{:S(2)}) collective-permute-start(bf16[128,512]{1,0:T(8,128)(2,1)S(1)} %fusion), channel_id=1, source_target_pairs={{0,8},{1,9},{2,10},{3,11},{4,12},{5,13},{6,14},{7,15},{8,0},{9,1},... | collective-permute-start | bytes 393224 | tf_op jit(solution)/shard_map/ppermute | solution.py:22
  36.3 5.1 %collective-permute-start.9 = (f32[136,256]{1,0:T(8,128)S(1)}, f32[136,256]{1,0:T(8,128)S(1)}, u32[]{:S(2)}, u32[]{:S(2)}) collective-permute-start(f32[136,256]{1,0:T(8,128)S(1)} %slice_bitcast_fusion.2), channel_id=1, source_target_pairs={{0,1},{1,0},{2,3},{3,2},{4,5},{5,4},{6,7},{7,6},{8,9},{9,8},{10,11... | collective-permute-start | bytes 417800 | tf_op jit(solution)/shard_map/ppermute | solution.py:22
  36.4 11.0 %collective-permute-start.15 = (bf16[512,128]{1,0:T(8,128)(2,1)S(1)}, bf16[512,128]{1,0:T(8,128)(2,1)S(1)}, u32[]{:S(2)}, u32[]{:S(2)}) collective-permute-start(bf16[512,128]{1,0:T(8,128)(2,1)S(1)} %get-tuple-element.40), channel_id=1, source_target_pairs={{0,12},{1,13},{2,14},{3,15},{4,8},{5,9},{6,10},{7,11},{8,4},{9,5},... | collective-permute-start | bytes 393224 | tf_op jit(solution)/shard_map/ppermute | solution.py:22
  37.8 11.3 %collective-permute-start.16 = (bf16[512,128]{1,0:T(8,128)(2,1)S(1)}, bf16[512,128]{1,0:T(8,128)(2,1)S(1)}, u32[]{:S(2)}, u32[]{:S(2)}) collective-permute-start(bf16[512,128]{1,0:T(8,128)(2,1)S(1)} %get-tuple-element.40), channel_id=1, source_target_pairs={{0,4},{1,5},{2,6},{3,7},{4,0},{5,1},{6,2},{7,3},{8,12},{9,13},{10,... | collective-permute-start | bytes 393224 | tf_op jit(solution)/shard_map/ppermute | solution.py:22
  37.8 9.7 %collective-permute-start.17 = (bf16[512,128]{1,0:T(8,128)(2,1)S(1)}, bf16[512,128]{1,0:T(8,128)(2,1)S(1)}, u32[]{:S(2)}, u32[]{:S(2)}) collective-permute-start(bf16[512,128]{1,0:T(8,128)(2,1)S(1)} %get-tuple-element.40), channel_id=1, source_target_pairs={{0,2},{1,3},{2,0},{3,1},{4,6},{5,7},{6,4},{7,5},{8,10},{9,11},{10,... | collective-permute-start | bytes 393224 | tf_op jit(solution)/shard_map/ppermute | solution.py:22
  40.8 8.7 %collective-permute-start.18 = (bf16[512,128]{1,0:T(8,128)(2,1)S(1)}, bf16[512,128]{1,0:T(8,128)(2,1)S(1)}, u32[]{:S(2)}, u32[]{:S(2)}) collective-permute-start(bf16[512,128]{1,0:T(8,128)(2,1)S(1)} %get-tuple-element.40), channel_id=1, source_target_pairs={{0,8},{1,9},{2,10},{3,11},{4,12},{5,13},{6,14},{7,15},{8,0},{9,1},... | collective-permute-start | bytes 393224 | tf_op jit(solution)/shard_map/ppermute | solution.py:22
  41.4 4.5 %collective-permute-start.10 = (bf16[136,256]{1,0:T(8,128)(2,1)S(1)}, bf16[136,256]{1,0:T(8,128)(2,1)S(1)}, u32[]{:S(2)}, u32[]{:S(2)}) collective-permute-start(bf16[136,256]{1,0:T(8,128)(2,1)S(1)} %fusion.2), channel_id=1, source_target_pairs={{0,2},{1,3},{2,0},{3,1},{4,6},{5,7},{6,4},{7,5},{8,10},{9,11},{10,... | collective-permute-start | bytes 208904 | tf_op jit(solution)/shard_map/ppermute | solution.py:22
  45.9 8.3 %collective-permute-start.19 = (bf16[512,128]{1,0:T(8,128)(2,1)S(1)}, bf16[512,128]{1,0:T(8,128)(2,1)S(1)}, u32[]{:S(2)}, u32[]{:S(2)}) collective-permute-start(bf16[512,128]{1,0:T(8,128)(2,1)S(1)} %get-tuple-element.40), channel_id=1, source_target_pairs={{0,6},{1,7},{2,4},{3,5},{4,2},{5,3},{6,0},{7,1},{8,14},{9,15},{10,... | collective-permute-start | bytes 393224 | tf_op jit(solution)/shard_map/ppermute | solution.py:22
  47.4 6.8 %collective-permute-start.20 = (bf16[1,512,128]{2,1,0:T(8,128)(2,1)S(1)}, bf16[1,512,128]{2,1,0:T(8,128)(2,1)S(1)}, u32[]{:S(2)}, u32[]{:S(2)}) collective-permute-start(bf16[1,512,128]{2,1,0:T(8,128)(2,1)S(1)} %bitcast.67), channel_id=1, source_target_pairs={{0,1},{1,0},{2,3},{3,2},{4,5},{5,4},{6,7},{7,6},{8,9},{9,8},{10,11... | collective-permute-start | bytes 393224 | tf_op jit(solution)/shard_map/ppermute | solution.py:22
  47.5 6.8 %collective-permute-start.21 = (bf16[1,512,128]{2,1,0:T(8,128)(2,1)S(1)}, bf16[1,512,128]{2,1,0:T(8,128)(2,1)S(1)}, u32[]{:S(2)}, u32[]{:S(2)}) collective-permute-start(bf16[1,512,128]{2,1,0:T(8,128)(2,1)S(1)} %bitcast.73), channel_id=1, source_target_pairs={{0,1},{1,0},{2,3},{3,2},{4,5},{5,4},{6,7},{7,6},{8,9},{9,8},{10,11... | collective-permute-start | bytes 393224 | tf_op jit(solution)/shard_map/ppermute | solution.py:22
  49.1 7.4 %collective-permute-start.22 = (bf16[1,512,128]{2,1,0:T(8,128)(2,1)S(1)}, bf16[1,512,128]{2,1,0:T(8,128)(2,1)S(1)}, u32[]{:S(2)}, u32[]{:S(2)}) collective-permute-start(bf16[1,512,128]{2,1,0:T(8,128)(2,1)S(1)} %bitcast.68), channel_id=1, source_target_pairs={{0,1},{1,0},{2,3},{3,2},{4,5},{5,4},{6,7},{7,6},{8,9},{9,8},{10,11... | collective-permute-start | bytes 393224 | tf_op jit(solution)/shard_map/ppermute | solution.py:22
  49.5 12.1 %collective-permute-start.23 = (bf16[512,128]{1,0:T(8,128)(2,1)S(1)}, bf16[512,128]{1,0:T(8,128)(2,1)S(1)}, u32[]{:S(2)}, u32[]{:S(2)}) collective-permute-start(bf16[512,128]{1,0:T(8,128)(2,1)S(1)} %collective-permute-done.15), channel_id=1, source_target_pairs={{0,2},{1,3},{2,0},{3,1},{4,6},{5,7},{6,4},{7,5},{8,10},{9,11},{10,... | collective-permute-start | bytes 393224 | tf_op jit(solution)/shard_map/ppermute | solution.py:22
  54.2 7.5 %collective-permute-start.24 = (bf16[512,128]{1,0:T(8,128)(2,1)S(1)}, bf16[512,128]{1,0:T(8,128)(2,1)S(1)}, u32[]{:S(2)}, u32[]{:S(2)}) collective-permute-start(bf16[512,128]{1,0:T(8,128)(2,1)S(1)} %collective-permute-done.18), channel_id=1, source_target_pairs={{0,2},{1,3},{2,0},{3,1},{4,6},{5,7},{6,4},{7,5},{8,10},{9,11},{10,... | collective-permute-start | bytes 393224 | tf_op jit(solution)/shard_map/ppermute | solution.py:22
  54.2 8.0 %collective-permute-start.11 = (bf16[136,256]{1,0:T(8,128)(2,1)S(1)}, bf16[136,256]{1,0:T(8,128)(2,1)S(1)}, u32[]{:S(2)}, u32[]{:S(2)}) collective-permute-start(bf16[136,256]{1,0:T(8,128)(2,1)S(1)} %get-tuple-element.51), channel_id=1, source_target_pairs={{0,4},{1,5},{2,6},{3,7},{4,0},{5,1},{6,2},{7,3},{8,12},{9,13},{10,... | collective-permute-start | bytes 208904 | tf_op jit(solution)/shard_map/ppermute | solution.py:22
  54.3 8.0 %collective-permute-start.12 = (bf16[136,256]{1,0:T(8,128)(2,1)S(1)}, bf16[136,256]{1,0:T(8,128)(2,1)S(1)}, u32[]{:S(2)}, u32[]{:S(2)}) collective-permute-start(bf16[136,256]{1,0:T(8,128)(2,1)S(1)} %get-tuple-element.51), channel_id=1, source_target_pairs={{0,8},{1,9},{2,10},{3,11},{4,12},{5,13},{6,14},{7,15},{8,0},{9,1},... | collective-permute-start | bytes 208904 | tf_op jit(solution)/shard_map/ppermute | solution.py:22
  56.5 6.2 %collective-permute-start.13 = (bf16[136,256]{1,0:T(8,128)(2,1)S(1)}, bf16[136,256]{1,0:T(8,128)(2,1)S(1)}, u32[]{:S(2)}, u32[]{:S(2)}) collective-permute-start(bf16[136,256]{1,0:T(8,128)(2,1)S(1)} %get-tuple-element.51), channel_id=1, source_target_pairs={{0,12},{1,13},{2,14},{3,15},{4,8},{5,9},{6,10},{7,11},{8,4},{9,5},... | collective-permute-start | bytes 208904 | tf_op jit(solution)/shard_map/ppermute | solution.py:22
  62.3 3.1 %collective-permute-start.28 = (bf16[1,512,128]{2,1,0:T(8,128)(2,1)S(1)}, bf16[1,512,128]{2,1,0:T(8,128)(2,1)S(1)}, u32[]{:S(2)}, u32[]{:S(2)}) collective-permute-start(bf16[1,512,128]{2,1,0:T(8,128)(2,1)S(1)} %bitcast.64), channel_id=1, source_target_pairs={{0,1},{1,0},{2,3},{3,2},{4,5},{5,4},{6,7},{7,6},{8,9},{9,8},{10,11... | collective-permute-start | bytes 393224 | tf_op jit(solution)/shard_map/ppermute | solution.py:22
  (16 other events, 104.1 us)

commit v5 on v4

--- a/solution.py
+++ b/solution.py
@@ -11,7 +11,7 @@
 BF16 = jnp.bfloat16
 F32 = jnp.float32
 GROUP = 8
-CHUNKS = 8
+CHUNKS = 16
 MIB = 1 << 20
 PLAN = {'z': (1, 3, 2), 'y': (3, 2, 1, 0), 'parts': (), 'token': 0, 'after': 4, 'adj': 1, 'ysep': 1, 'agz': (3, 2, 1), 'groups': ((0,), (12, 4, 2, 8, 6, (1,), (3,), (5,)), (14, 10, (13,), (9,), (7,)), ((15,), (11,))), 'heavy': (1, 1, 1, 1), 'pairs': ((0,), (2,), (4,), (6,), (8,), (12,), (10,), (14,)), 'terms': None, 'gy': None, 'gz': None, 'butter': 0, 'fin': 1, 'ph': 0, 'findep': 0, 'gyb': 1, 'direct': (1,), 'yfs': 0, 'agd': (1,), 'dsep': 0, 'k1l': 55, 'adjl': 38, 'gates': ((1, (12, 4, 2, 8), 1),), 'halves': ((7, 5, 2, 3), (0, 6, 4, 1))}
 LIGHT = pl.CostEstimate(flops=0, bytes_accessed=0, transcendentals=0)
@@ -43,7 +43,7 @@
         adj[pl.ds(i * per_unit, per_unit)] = jnp.zeros((per_unit,) + adj.shape[1:], BF16)
         return carry
 
-    lax.fori_loop(0, group, clear, 0)
+    lax.fori_loop(0, group, clear, 0, unroll=2)
     for c in range(chunks):
 
         @pl.when(step == 0)
@@ -64,7 +64,7 @@
                 store()
             return carry
 
-        lax.fori_loop(0, size, add, 0)
+        lax.fori_loop(0, size, add, 0, unroll=2)
 
 
 def forward_kernel(

time: 67.3 us -> 67.1 us (level)
  no operation moved by 1% of the time
where the time goes in v5:
time: 67.1 us; the launch traced here: 66.9 us
  starting transfers between devices  32.1 us (48%)
  Pallas kernels  19.2 us (29%)
  waiting for transfers between devices  12.7 us (19%)
  other arithmetic  1.81 us (3%)
  between operations  0.99 us (1%)
    ppermute x30, starting transfers between devices, swap(): return lax.ppermute(value, 'row', [(i, i ^ bits) for i in range(devices)])  32.1 us
    ppermute x30, waiting for transfers between devices, swap(): return lax.ppermute(value, 'row', [(i, i ^ bits) for i in range(devices)])  12.7 us
    pallas_call x4, Pallas kernels, spread(): pl.pallas_call(functools.partial(kernel, tuple(places), nb, len(backs), l...  6.88 us
    pallas_call x1, Pallas kernels, forward_sums(): pl.pallas_call(functools.partial(forward_kernel, nb, group, units > group...  6.63 us
    pallas_call x1, Pallas kernels, adjacency(): pl.pallas_call(functools.partial(adjacency_kernel, nb, group, units > gro...  4.15 us
    convert_element_type x1, other arithmetic, on_device(): direct = (mine.astype(F32) + recv.astype(F32)).astype(BF16)  1.59 us
  transfers between devices with their start and end apart: 30, of which 10 were waited for; matrix products, arithmetic and copies ran while one was open for 3% of the time, Pallas kernels for 14%

profile of v5, /device:TPU:0, one launch (start us, length us, event | category | flops | bytes accessed | tf_op | source)
XLA Modules:
  0.0 66.9 jit_solution(8184761170658186339)
XLA Ops:
  0.6 6.6 %forward_sums.1 = (bf16[4,128,512]{2,1,0:T(8,128)(2,1)}, bf16[4,128,512]{2,1,0:T(8,128)(2,1)}, f32[8,128,512]{2,1,0:T(8,128)}) custom-call(s32[128]{0:T(128)} %bitcast.54, s32[128]{0:T(128)} %src_ref.3, s32[128]{0:T(128)} %dst_ref.3, bf16[512,128]{1,0:T(8,128)(2,1)} %x_ref.1, s32[128,128,128]{2,1,0:T(8,128)} %pat_hbm.3), custom_call_target="tpu_custom_call" | custom-call | tf_op jit(solution)/shard_map/forward_sums/pallas_call | solution.py:115
  7.9 1.7 %collective-permute-done.1 = bf16[4,128,512]{2,1,0:T(8,128)(2,1)S(1)} collective-permute-done((bf16[4,128,512]{2,1,0:T(8,128)(2,1)}, bf16[4,128,512]{2,1,0:T(8,128)(2,1)S(1)}, u32[]{:S(2)}, u32[]{:S(2)}) %collective-permute-start.1) | collective-permute-done | bytes 524320 | tf_op jit(solution)/shard_map/ppermute | solution.py:22
  9.5 1.6 %fusion.5 = (bf16[128,512]{1,0:T(8,128)(2,1)S(1)}, bf16[128,512]{1,0:T(8,128)(2,1)S(1)}, bf16[128,512]{1,0:T(8,128)(2,1)S(1)}, f32[128,512]{1,0:T(8,128)S(1)}, f32[128,512]{1,0:T(8,128)S(1)}) fusion(f32[8,128,512]{2,1,0:T(8,128)} %get-tuple-element.25.own_ref, bf16[4,128,512]{2,1,0:T(8,128)(2,1)S(1)} %collective-permute-done.1), kind=kLoop, calls=%fused_computation.18 | loop fusion | flops 589824 | bytes 2621440 | tf_op jit(solution)/shard_map/convert_element_type | solution.py:500
  11.2 3.0 %collective-permute-start.2 = (bf16[128,512]{1,0:T(8,128)(2,1)S(1)}, bf16[128,512]{1,0:T(8,128)(2,1)S(1)}, u32[]{:S(2)}, u32[]{:S(2)}) collective-permute-start(bf16[128,512]{1,0:T(8,128)(2,1)S(1)} %get-tuple-element.47), channel_id=1, source_target_pairs={{0,2},{1,3},{2,0},{3,1},{4,6},{5,7},{6,4},{7,5},{8,10},{9,11},{10,... | collective-permute-start | bytes 393224 | tf_op jit(solution)/shard_map/ppermute | solution.py:22
  14.3 2.1 %collective-permute-start.4 = (bf16[128,512]{1,0:T(8,128)(2,1)S(1)}, bf16[128,512]{1,0:T(8,128)(2,1)S(1)}, u32[]{:S(2)}, u32[]{:S(2)}) collective-permute-start(bf16[128,512]{1,0:T(8,128)(2,1)S(1)} %add_convert_fusion.2), channel_id=1, source_target_pairs={{0,2},{1,3},{2,0},{3,1},{4,6},{5,7},{6,4},{7,5},{8,10},{9,11},{10,... | collective-permute-start | bytes 393224 | tf_op jit(solution)/shard_map/ppermute | solution.py:22
  16.4 1.6 %collective-permute-start.5 = (bf16[128,512]{1,0:T(8,128)(2,1)S(1)}, bf16[128,512]{1,0:T(8,128)(2,1)S(1)}, u32[]{:S(2)}, u32[]{:S(2)}) collective-permute-start(bf16[128,512]{1,0:T(8,128)(2,1)S(1)} %get-tuple-element.46), channel_id=1, source_target_pairs={{0,4},{1,5},{2,6},{3,7},{4,0},{5,1},{6,2},{7,3},{8,12},{9,13},{10,... | collective-permute-start | bytes 393224 | tf_op jit(solution)/shard_map/ppermute | solution.py:22
  18.5 4.2 %collective-permute-start.3 = (bf16[128,512]{1,0:T(8,128)(2,1)S(1)}, bf16[128,512]{1,0:T(8,128)(2,1)S(1)}, u32[]{:S(2)}, u32[]{:S(2)}) collective-permute-start(bf16[128,512]{1,0:T(8,128)(2,1)S(1)} %fusion.1), channel_id=1, source_target_pairs={{0,12},{1,13},{2,14},{3,15},{4,8},{5,9},{6,10},{7,11},{8,4},{9,5},... | collective-permute-start | bytes 393224 | tf_op jit(solution)/shard_map/ppermute | solution.py:22
  22.7 1.4 %collective-permute-done.7 = bf16[128,512]{1,0:T(8,128)(2,1)S(1)} collective-permute-done((bf16[128,512]{1,0:T(8,128)(2,1)S(1)}, bf16[128,512]{1,0:T(8,128)(2,1)S(1)}, u32[]{:S(2)}, u32[]{:S(2)}) %collective-permute-start.7) | collective-permute-done | bytes 131104 | tf_op jit(solution)/shard_map/ppermute | solution.py:22
  24.1 2.4 %collective-permute-start.8 = (bf16[128,512]{1,0:T(8,128)(2,1)S(1)}, bf16[128,512]{1,0:T(8,128)(2,1)S(1)}, u32[]{:S(2)}, u32[]{:S(2)}) collective-permute-start(bf16[128,512]{1,0:T(8,128)(2,1)S(1)} %fusion), channel_id=1, source_target_pairs={{0,8},{1,9},{2,10},{3,11},{4,12},{5,13},{6,14},{7,15},{8,0},{9,1},... | collective-permute-start | bytes 393224 | tf_op jit(solution)/shard_map/ppermute | solution.py:22
  26.5 3.7 %collective-permute-done.3 = bf16[128,512]{1,0:T(8,128)(2,1)S(1)} collective-permute-done((bf16[128,512]{1,0:T(8,128)(2,1)S(1)}, bf16[128,512]{1,0:T(8,128)(2,1)S(1)}, u32[]{:S(2)}, u32[]{:S(2)}) %collective-permute-start.3) | collective-permute-done | bytes 131104 | tf_op jit(solution)/shard_map/ppermute | solution.py:22
  30.3 4.1 %adjacency.1 = (bf16[256,128,128]{2,1,0:T(8,128)(2,1)S(1)}, f32[8,128]{1,0:T(8,128)S(1)}) custom-call(s32[128]{0:T(128)S(1)} %bitcast.55, s32[128]{0:T(128)S(1)} %copy-done.8, s32[128]{0:T(128)S(1)} %copy-done.9, s32[128,128,128]{2,1,0:T(8,128)} %pat_hbm.3, bf16[1,128,512]{2,1,0:T(8,128)(2,1)S(1)} %bitcast.49), custom_call_target="tpu_custom_call" | custom-call | flops 20000000000 | tf_op jit(solution)/shard_map/adjacency/pallas_call | solution.py:155
  34.6 1.2 %layer.1 = (bf16[512,256]{1,0:T(8,128)(2,1)}, bf16[512,256]{1,0:T(8,128)(2,1)S(1)}, bf16[128,512]{1,0:T(8,128)(2,1)S(1)}, bf16[512,128]{1,0:T(8,128)(2,1)S(1)}) custom-call(f32[8,128]{1,0:T(8,128)S(1)} %get-tuple-element.28.made_hbm, f32[8,128,512]{2,1,0:T(8,128)S(1)} %copy-done, bf16[4,128,512]{2,1,0:T(8,128)(2,1)S(1)} %collective-permute-done.refs_0_, ...), custom_call_target="tpu_custom_call" | custom-call | tf_op jit(solution)/shard_map/layer/pallas_call | solution.py:234
  36.2 1.4 %collective-permute-start.15 = (bf16[512,128]{1,0:T(8,128)(2,1)S(1)}, bf16[512,128]{1,0:T(8,128)(2,1)S(1)}, u32[]{:S(2)}, u32[]{:S(2)}) collective-permute-start(bf16[512,128]{1,0:T(8,128)(2,1)S(1)} %get-tuple-element.40), channel_id=1, source_target_pairs={{0,12},{1,13},{2,14},{3,15},{4,8},{5,9},{6,10},{7,11},{8,4},{9,5},... | collective-permute-start | bytes 393224 | tf_op jit(solution)/shard_map/ppermute | solution.py:22
  37.6 3.1 %collective-permute-start.17 = (bf16[512,128]{1,0:T(8,128)(2,1)S(1)}, bf16[512,128]{1,0:T(8,128)(2,1)S(1)}, u32[]{:S(2)}, u32[]{:S(2)}) collective-permute-start(bf16[512,128]{1,0:T(8,128)(2,1)S(1)} %get-tuple-element.40), channel_id=1, source_target_pairs={{0,2},{1,3},{2,0},{3,1},{4,6},{5,7},{6,4},{7,5},{8,10},{9,11},{10,... | collective-permute-start | bytes 393224 | tf_op jit(solution)/shard_map/ppermute | solution.py:22
  41.2 1.5 %collective-permute-start.10 = (bf16[136,256]{1,0:T(8,128)(2,1)S(1)}, bf16[136,256]{1,0:T(8,128)(2,1)S(1)}, u32[]{:S(2)}, u32[]{:S(2)}) collective-permute-start(bf16[136,256]{1,0:T(8,128)(2,1)S(1)} %fusion.2), channel_id=1, source_target_pairs={{0,2},{1,3},{2,0},{3,1},{4,6},{5,7},{6,4},{7,5},{8,10},{9,11},{10,... | collective-permute-start | bytes 208904 | tf_op jit(solution)/shard_map/ppermute | solution.py:22
  43.1 2.6 %collective-permute-done.10 = bf16[136,256]{1,0:T(8,128)(2,1)S(1)} collective-permute-done((bf16[136,256]{1,0:T(8,128)(2,1)S(1)}, bf16[136,256]{1,0:T(8,128)(2,1)S(1)}, u32[]{:S(2)}, u32[]{:S(2)}) %collective-permute-start.10) | collective-permute-done | bytes 69664 | tf_op jit(solution)/shard_map/ppermute | solution.py:22
  45.7 1.5 %collective-permute-start.19 = (bf16[512,128]{1,0:T(8,128)(2,1)S(1)}, bf16[512,128]{1,0:T(8,128)(2,1)S(1)}, u32[]{:S(2)}, u32[]{:S(2)}) collective-permute-start(bf16[512,128]{1,0:T(8,128)(2,1)S(1)} %get-tuple-element.40), channel_id=1, source_target_pairs={{0,6},{1,7},{2,4},{3,5},{4,2},{5,3},{6,0},{7,1},{8,14},{9,15},{10,... | collective-permute-start | bytes 393224 | tf_op jit(solution)/shard_map/ppermute | solution.py:22
  47.8 1.1 %collective-permute-done.16 = bf16[512,128]{1,0:T(8,128)(2,1)S(1)} collective-permute-done((bf16[512,128]{1,0:T(8,128)(2,1)S(1)}, bf16[512,128]{1,0:T(8,128)(2,1)S(1)}, u32[]{:S(2)}, u32[]{:S(2)}) %collective-permute-start.16) | collective-permute-done | bytes 131104 | tf_op jit(solution)/shard_map/ppermute | solution.py:22
  49.3 3.7 %collective-permute-start.23 = (bf16[512,128]{1,0:T(8,128)(2,1)S(1)}, bf16[512,128]{1,0:T(8,128)(2,1)S(1)}, u32[]{:S(2)}, u32[]{:S(2)}) collective-permute-start(bf16[512,128]{1,0:T(8,128)(2,1)S(1)} %collective-permute-done.15), channel_id=1, source_target_pairs={{0,2},{1,3},{2,0},{3,1},{4,6},{5,7},{6,4},{7,5},{8,10},{9,11},{10,... | collective-permute-start | bytes 393224 | tf_op jit(solution)/shard_map/ppermute | solution.py:22
  54.1 2.3 %collective-permute-start.12 = (bf16[136,256]{1,0:T(8,128)(2,1)S(1)}, bf16[136,256]{1,0:T(8,128)(2,1)S(1)}, u32[]{:S(2)}, u32[]{:S(2)}) collective-permute-start(bf16[136,256]{1,0:T(8,128)(2,1)S(1)} %get-tuple-element.51), channel_id=1, source_target_pairs={{0,8},{1,9},{2,10},{3,11},{4,12},{5,13},{6,14},{7,15},{8,0},{9,1},... | collective-permute-start | bytes 208904 | tf_op jit(solution)/shard_map/ppermute | solution.py:22
  56.4 2.0 %collective-permute-start.13 = (bf16[136,256]{1,0:T(8,128)(2,1)S(1)}, bf16[136,256]{1,0:T(8,128)(2,1)S(1)}, u32[]{:S(2)}, u32[]{:S(2)}) collective-permute-start(bf16[136,256]{1,0:T(8,128)(2,1)S(1)} %get-tuple-element.51), channel_id=1, source_target_pairs={{0,12},{1,13},{2,14},{3,15},{4,8},{5,9},{6,10},{7,11},{8,4},{9,5},... | collective-permute-start | bytes 208904 | tf_op jit(solution)/shard_map/ppermute | solution.py:22
  58.4 3.0 %spread.5.acc_ref = f32[512,128]{1,0:T(8,128)S(1)} custom-call(f32[512,128]{1,0:T(8,128)S(1)} %spread.4.refs_0_.acc_ref, bf16[256,128,128]{2,1,0:T(8,128)(2,1)S(1)} %get-tuple-element.39.adj_hbm, f32[8,128]{1,0:T(8,128)S(1)} %gate.1.refs_0_, bf16[1,512,128]{2,1,0:T(8,128)(2,1)S(1)} %bitcast.57, bf16[1,512,128]{2,1,0:T(8,128)(2,1)S(1)} %bitcast.70, ...), custom_call_target="tpu_custom_call" | custom-call | flops 20000000000 | tf_op jit(solution)/shard_map/spread/pallas_call | solution.py:400
  63.4 1.9 %spread.6.acc_ref = f32[512,128]{1,0:T(8,128)S(1)} custom-call(f32[512,128]{1,0:T(8,128)S(1)} %spread.5.acc_ref, bf16[256,128,128]{2,1,0:T(8,128)(2,1)S(1)} %get-tuple-element.39.adj_hbm, bf16[1,512,128]{2,1,0:T(8,128)(2,1)S(1)} %bitcast.65, bf16[1,512,128]{2,1,0:T(8,128)(2,1)S(1)} %bitcast.72, bf16[1,512,128]{2,1,0:T(8,128)(2,1)S(1)} %collective-permute-done.25.refs_2_, ...), custom_call_target="tpu_custom_call" | custom-call | flops 20000000000 | tf_op jit(solution)/shard_map/spread/pallas_call | solution.py:400
  65.3 1.6 %spread.7 = (bf16[512,128]{1,0:T(8,128)(2,1)}, f32[128,256]{1,0:T(8,128)}, f32[128,256]{1,0:T(8,128)}, f32[1,256]{1,0:T(1,128)}) custom-call(s32[1]{0:T(128)} %bitcast.17.me_ref, f32[136,256]{1,0:T(8,128)S(1)} %add_add_fusion.mine_ref, f32[136,256]{1,0:T(8,128)S(1)} %collective-permute-done.14.theirs_ref, f32[512,128]{1,0:T(8,128)S(1)} %spread.6.acc_ref, ...), custom_call_target="tpu_custom_call" | custom-call | flops 20000000000 | tf_op jit(solution)/shard_map/spread/pallas_call | solution.py:400
  (76 shorter events, 6.7 us)
Async XLA Ops:
  7.8 6.5 %collective-permute-start = (bf16[4,128,512]{2,1,0:T(8,128)(2,1)}, bf16[4,128,512]{2,1,0:T(8,128)(2,1)S(1)}, u32[]{:S(2)}, u32[]{:S(2)}) collective-permute-start(bf16[4,128,512]{2,1,0:T(8,128)(2,1)} %get-tuple-element.26), channel_id=1, source_target_pairs={{0,1},{1,0},{2,3},{3,2},{4,5},{5,4},{6,7},{7,6},{8,9},{9,8},{10,11... | collective-permute-start | bytes 1572872 | tf_op jit(solution)/shard_map/ppermute | solution.py:22
  11.2 7.2 %collective-permute-start.2 = (bf16[128,512]{1,0:T(8,128)(2,1)S(1)}, bf16[128,512]{1,0:T(8,128)(2,1)S(1)}, u32[]{:S(2)}, u32[]{:S(2)}) collective-permute-start(bf16[128,512]{1,0:T(8,128)(2,1)S(1)} %get-tuple-element.47), channel_id=1, source_target_pairs={{0,2},{1,3},{2,0},{3,1},{4,6},{5,7},{6,4},{7,5},{8,10},{9,11},{10,... | collective-permute-start | bytes 393224 | tf_op jit(solution)/shard_map/ppermute | solution.py:22
  14.2 9.8 %collective-permute-start.7 = (bf16[128,512]{1,0:T(8,128)(2,1)S(1)}, bf16[128,512]{1,0:T(8,128)(2,1)S(1)}, u32[]{:S(2)}, u32[]{:S(2)}) collective-permute-start(bf16[128,512]{1,0:T(8,128)(2,1)S(1)} %add_convert_fusion.3), channel_id=1, source_target_pairs={{0,2},{1,3},{2,0},{3,1},{4,6},{5,7},{6,4},{7,5},{8,10},{9,11},{10,... | collective-permute-start | bytes 393224 | tf_op jit(solution)/shard_map/ppermute | solution.py:22
  14.3 20.2 %collective-permute-start.4 = (bf16[128,512]{1,0:T(8,128)(2,1)S(1)}, bf16[128,512]{1,0:T(8,128)(2,1)S(1)}, u32[]{:S(2)}, u32[]{:S(2)}) collective-permute-start(bf16[128,512]{1,0:T(8,128)(2,1)S(1)} %add_convert_fusion.2), channel_id=1, source_target_pairs={{0,2},{1,3},{2,0},{3,1},{4,6},{5,7},{6,4},{7,5},{8,10},{9,11},{10,... | collective-permute-start | bytes 393224 | tf_op jit(solution)/shard_map/ppermute | solution.py:22
  16.4 18.1 %collective-permute-start.5 = (bf16[128,512]{1,0:T(8,128)(2,1)S(1)}, bf16[128,512]{1,0:T(8,128)(2,1)S(1)}, u32[]{:S(2)}, u32[]{:S(2)}) collective-permute-start(bf16[128,512]{1,0:T(8,128)(2,1)S(1)} %get-tuple-element.46), channel_id=1, source_target_pairs={{0,4},{1,5},{2,6},{3,7},{4,0},{5,1},{6,2},{7,3},{8,12},{9,13},{10,... | collective-permute-start | bytes 393224 | tf_op jit(solution)/shard_map/ppermute | solution.py:22
  18.0 16.5 %collective-permute-start.6 = (bf16[128,512]{1,0:T(8,128)(2,1)S(1)}, bf16[128,512]{1,0:T(8,128)(2,1)S(1)}, u32[]{:S(2)}, u32[]{:S(2)}) collective-permute-start(bf16[128,512]{1,0:T(8,128)(2,1)S(1)} %get-tuple-element.45), channel_id=1, source_target_pairs={{0,6},{1,7},{2,4},{3,5},{4,2},{5,3},{6,0},{7,1},{8,14},{9,15},{10,... | collective-permute-start | bytes 393224 | tf_op jit(solution)/shard_map/ppermute | solution.py:22
  18.5 11.8 %collective-permute-start.3 = (bf16[128,512]{1,0:T(8,128)(2,1)S(1)}, bf16[128,512]{1,0:T(8,128)(2,1)S(1)}, u32[]{:S(2)}, u32[]{:S(2)}) collective-permute-start(bf16[128,512]{1,0:T(8,128)(2,1)S(1)} %fusion.1), channel_id=1, source_target_pairs={{0,12},{1,13},{2,14},{3,15},{4,8},{5,9},{6,10},{7,11},{8,4},{9,5},... | collective-permute-start | bytes 393224 | tf_op jit(solution)/shard_map/ppermute | solution.py:22
  24.1 10.4 %collective-permute-start.8 = (bf16[128,512]{1,0:T(8,128)(2,1)S(1)}, bf16[128,512]{1,0:T(8,128)(2,1)S(1)}, u32[]{:S(2)}, u32[]{:S(2)}) collective-permute-start(bf16[128,512]{1,0:T(8,128)(2,1)S(1)} %fusion), channel_id=1, source_target_pairs={{0,8},{1,9},{2,10},{3,11},{4,12},{5,13},{6,14},{7,15},{8,0},{9,1},... | collective-permute-start | bytes 393224 | tf_op jit(solution)/shard_map/ppermute | solution.py:22
  36.1 5.1 %collective-permute-start.9 = (f32[136,256]{1,0:T(8,128)S(1)}, f32[136,256]{1,0:T(8,128)S(1)}, u32[]{:S(2)}, u32[]{:S(2)}) collective-permute-start(f32[136,256]{1,0:T(8,128)S(1)} %slice_bitcast_fusion.2), channel_id=1, source_target_pairs={{0,1},{1,0},{2,3},{3,2},{4,5},{5,4},{6,7},{7,6},{8,9},{9,8},{10,11... | collective-permute-start | bytes 417800 | tf_op jit(solution)/shard_map/ppermute | solution.py:22
  36.2 11.0 %collective-permute-start.15 = (bf16[512,128]{1,0:T(8,128)(2,1)S(1)}, bf16[512,128]{1,0:T(8,128)(2,1)S(1)}, u32[]{:S(2)}, u32[]{:S(2)}) collective-permute-start(bf16[512,128]{1,0:T(8,128)(2,1)S(1)} %get-tuple-element.40), channel_id=1, source_target_pairs={{0,12},{1,13},{2,14},{3,15},{4,8},{5,9},{6,10},{7,11},{8,4},{9,5},... | collective-permute-start | bytes 393224 | tf_op jit(solution)/shard_map/ppermute | solution.py:22
  37.6 11.3 %collective-permute-start.16 = (bf16[512,128]{1,0:T(8,128)(2,1)S(1)}, bf16[512,128]{1,0:T(8,128)(2,1)S(1)}, u32[]{:S(2)}, u32[]{:S(2)}) collective-permute-start(bf16[512,128]{1,0:T(8,128)(2,1)S(1)} %get-tuple-element.40), channel_id=1, source_target_pairs={{0,4},{1,5},{2,6},{3,7},{4,0},{5,1},{6,2},{7,3},{8,12},{9,13},{10,... | collective-permute-start | bytes 393224 | tf_op jit(solution)/shard_map/ppermute | solution.py:22
  37.6 9.7 %collective-permute-start.17 = (bf16[512,128]{1,0:T(8,128)(2,1)S(1)}, bf16[512,128]{1,0:T(8,128)(2,1)S(1)}, u32[]{:S(2)}, u32[]{:S(2)}) collective-permute-start(bf16[512,128]{1,0:T(8,128)(2,1)S(1)} %get-tuple-element.40), channel_id=1, source_target_pairs={{0,2},{1,3},{2,0},{3,1},{4,6},{5,7},{6,4},{7,5},{8,10},{9,11},{10,... | collective-permute-start | bytes 393224 | tf_op jit(solution)/shard_map/ppermute | solution.py:22
  40.7 8.7 %collective-permute-start.18 = (bf16[512,128]{1,0:T(8,128)(2,1)S(1)}, bf16[512,128]{1,0:T(8,128)(2,1)S(1)}, u32[]{:S(2)}, u32[]{:S(2)}) collective-permute-start(bf16[512,128]{1,0:T(8,128)(2,1)S(1)} %get-tuple-element.40), channel_id=1, source_target_pairs={{0,8},{1,9},{2,10},{3,11},{4,12},{5,13},{6,14},{7,15},{8,0},{9,1},... | collective-permute-start | bytes 393224 | tf_op jit(solution)/shard_map/ppermute | solution.py:22
  41.2 4.5 %collective-permute-start.10 = (bf16[136,256]{1,0:T(8,128)(2,1)S(1)}, bf16[136,256]{1,0:T(8,128)(2,1)S(1)}, u32[]{:S(2)}, u32[]{:S(2)}) collective-permute-start(bf16[136,256]{1,0:T(8,128)(2,1)S(1)} %fusion.2), channel_id=1, source_target_pairs={{0,2},{1,3},{2,0},{3,1},{4,6},{5,7},{6,4},{7,5},{8,10},{9,11},{10,... | collective-permute-start | bytes 208904 | tf_op jit(solution)/shard_map/ppermute | solution.py:22
  45.7 8.3 %collective-permute-start.19 = (bf16[512,128]{1,0:T(8,128)(2,1)S(1)}, bf16[512,128]{1,0:T(8,128)(2,1)S(1)}, u32[]{:S(2)}, u32[]{:S(2)}) collective-permute-start(bf16[512,128]{1,0:T(8,128)(2,1)S(1)} %get-tuple-element.40), channel_id=1, source_target_pairs={{0,6},{1,7},{2,4},{3,5},{4,2},{5,3},{6,0},{7,1},{8,14},{9,15},{10,... | collective-permute-start | bytes 393224 | tf_op jit(solution)/shard_map/ppermute | solution.py:22
  47.2 6.8 %collective-permute-start.20 = (bf16[1,512,128]{2,1,0:T(8,128)(2,1)S(1)}, bf16[1,512,128]{2,1,0:T(8,128)(2,1)S(1)}, u32[]{:S(2)}, u32[]{:S(2)}) collective-permute-start(bf16[1,512,128]{2,1,0:T(8,128)(2,1)S(1)} %bitcast.67), channel_id=1, source_target_pairs={{0,1},{1,0},{2,3},{3,2},{4,5},{5,4},{6,7},{7,6},{8,9},{9,8},{10,11... | collective-permute-start | bytes 393224 | tf_op jit(solution)/shard_map/ppermute | solution.py:22
  47.3 6.8 %collective-permute-start.21 = (bf16[1,512,128]{2,1,0:T(8,128)(2,1)S(1)}, bf16[1,512,128]{2,1,0:T(8,128)(2,1)S(1)}, u32[]{:S(2)}, u32[]{:S(2)}) collective-permute-start(bf16[1,512,128]{2,1,0:T(8,128)(2,1)S(1)} %bitcast.73), channel_id=1, source_target_pairs={{0,1},{1,0},{2,3},{3,2},{4,5},{5,4},{6,7},{7,6},{8,9},{9,8},{10,11... | collective-permute-start | bytes 393224 | tf_op jit(solution)/shard_map/ppermute | solution.py:22
  48.9 7.5 %collective-permute-start.22 = (bf16[1,512,128]{2,1,0:T(8,128)(2,1)S(1)}, bf16[1,512,128]{2,1,0:T(8,128)(2,1)S(1)}, u32[]{:S(2)}, u32[]{:S(2)}) collective-permute-start(bf16[1,512,128]{2,1,0:T(8,128)(2,1)S(1)} %bitcast.68), channel_id=1, source_target_pairs={{0,1},{1,0},{2,3},{3,2},{4,5},{5,4},{6,7},{7,6},{8,9},{9,8},{10,11... | collective-permute-start | bytes 393224 | tf_op jit(solution)/shard_map/ppermute | solution.py:22
  49.3 12.1 %collective-permute-start.23 = (bf16[512,128]{1,0:T(8,128)(2,1)S(1)}, bf16[512,128]{1,0:T(8,128)(2,1)S(1)}, u32[]{:S(2)}, u32[]{:S(2)}) collective-permute-start(bf16[512,128]{1,0:T(8,128)(2,1)S(1)} %collective-permute-done.15), channel_id=1, source_target_pairs={{0,2},{1,3},{2,0},{3,1},{4,6},{5,7},{6,4},{7,5},{8,10},{9,11},{10,... | collective-permute-start | bytes 393224 | tf_op jit(solution)/shard_map/ppermute | solution.py:22
  54.0 7.5 %collective-permute-start.24 = (bf16[512,128]{1,0:T(8,128)(2,1)S(1)}, bf16[512,128]{1,0:T(8,128)(2,1)S(1)}, u32[]{:S(2)}, u32[]{:S(2)}) collective-permute-start(bf16[512,128]{1,0:T(8,128)(2,1)S(1)} %collective-permute-done.18), channel_id=1, source_target_pairs={{0,2},{1,3},{2,0},{3,1},{4,6},{5,7},{6,4},{7,5},{8,10},{9,11},{10,... | collective-permute-start | bytes 393224 | tf_op jit(solution)/shard_map/ppermute | solution.py:22
  54.0 8.0 %collective-permute-start.11 = (bf16[136,256]{1,0:T(8,128)(2,1)S(1)}, bf16[136,256]{1,0:T(8,128)(2,1)S(1)}, u32[]{:S(2)}, u32[]{:S(2)}) collective-permute-start(bf16[136,256]{1,0:T(8,128)(2,1)S(1)} %get-tuple-element.51), channel_id=1, source_target_pairs={{0,4},{1,5},{2,6},{3,7},{4,0},{5,1},{6,2},{7,3},{8,12},{9,13},{10,... | collective-permute-start | bytes 208904 | tf_op jit(solution)/shard_map/ppermute | solution.py:22
  54.1 8.0 %collective-permute-start.12 = (bf16[136,256]{1,0:T(8,128)(2,1)S(1)}, bf16[136,256]{1,0:T(8,128)(2,1)S(1)}, u32[]{:S(2)}, u32[]{:S(2)}) collective-permute-start(bf16[136,256]{1,0:T(8,128)(2,1)S(1)} %get-tuple-element.51), channel_id=1, source_target_pairs={{0,8},{1,9},{2,10},{3,11},{4,12},{5,13},{6,14},{7,15},{8,0},{9,1},... | collective-permute-start | bytes 208904 | tf_op jit(solution)/shard_map/ppermute | solution.py:22
  56.4 6.1 %collective-permute-start.13 = (bf16[136,256]{1,0:T(8,128)(2,1)S(1)}, bf16[136,256]{1,0:T(8,128)(2,1)S(1)}, u32[]{:S(2)}, u32[]{:S(2)}) collective-permute-start(bf16[136,256]{1,0:T(8,128)(2,1)S(1)} %get-tuple-element.51), channel_id=1, source_target_pairs={{0,12},{1,13},{2,14},{3,15},{4,8},{5,9},{6,10},{7,11},{8,4},{9,5},... | collective-permute-start | bytes 208904 | tf_op jit(solution)/shard_map/ppermute | solution.py:22
  62.1 3.1 %collective-permute-start.28 = (bf16[1,512,128]{2,1,0:T(8,128)(2,1)S(1)}, bf16[1,512,128]{2,1,0:T(8,128)(2,1)S(1)}, u32[]{:S(2)}, u32[]{:S(2)}) collective-permute-start(bf16[1,512,128]{2,1,0:T(8,128)(2,1)S(1)} %bitcast.64), channel_id=1, source_target_pairs={{0,1},{1,0},{2,3},{3,2},{4,5},{5,4},{6,7},{7,6},{8,9},{9,8},{10,11... | collective-permute-start | bytes 393224 | tf_op jit(solution)/shard_map/ppermute | solution.py:22
  (16 other events, 103.5 us)
